TPU v7x, 128 devices: a whole 4x4x4 slice. The times are simulated.
128 devices in a mesh: dp: 16 (over z_lo, y, core), tensor: 8 (over z_hi, x).
Axes of the slice: x: 4, y: 4, z: 4 (z_hi: 2, z_lo: 2; z = z_hi * 2 + z_lo), core: 2. Of those that a mesh axis runs over, the one named last changes fastest.
Arguments:
- latent: bfloat16 [8192, 1408], P('dp'), may hold values from -6 to 6
- skip_input: bfloat16 [8192, 1408], P('dp'), may hold values from -6 to 6
- text_tokens: bfloat16 [333, 1024], replicated, may hold values from -6 to 6
- condition: bfloat16 [1408], replicated, may hold values from -5 to 5
- positions: int32 [8192, 2], P('dp'), may hold values from 0 to 31, as said below
- cotangent: bfloat16 [8192, 1408], P('dp'), may hold values from -6 to 6
- skip_w: bfloat16 [2816, 1408], P('tensor'), may hold values from -0.109375 to 0.109375
- skip_gain: float32 [1408], replicated, may hold values from 0.1 to 1.9
- norm1_gain: float32 [1408], replicated, may hold values from 0.1 to 1.9
- mod_w: bfloat16 [1408, 1408], replicated, may hold values from -0.15625 to 0.15625
- qkv_w: bfloat16 [1408, 3, 1408], P(None, None, 'tensor'), may hold values from -0.15625 to 0.15625
- qnorm_gain: float32 [88], replicated, may hold values from 0.1 to 1.9
- knorm_gain: float32 [88], replicated, may hold values from 0.1 to 1.9
- attn_out_w: bfloat16 [1408, 1408], P('tensor'), may hold values from -2.5 to 2.5
- norm2_gain: float32 [1408], replicated, may hold values from 0.1 to 1.9
- cq_w: bfloat16 [1408, 1408], P(None, 'tensor'), may hold values from -0.15625 to 0.15625
- ckv_w: bfloat16 [1024, 2, 1408], P(None, None, 'tensor'), may hold values from -0.1875 to 0.1875
- cqnorm_gain: float32 [88], replicated, may hold values from 0.1 to 1.9
- cknorm_gain: float32 [88], replicated, may hold values from 0.1 to 1.9
- cross_out_w: bfloat16 [1408, 1408], P('tensor'), may hold values from -1.75 to 1.75
- norm3_gain: float32 [1408], replicated, may hold values from 0.1 to 1.9
- fc1_w: bfloat16 [1408, 6144], P(None, 'tensor'), may hold values from -0.15625 to 0.15625
- fc2_w: bfloat16 [6144, 1408], P('tensor'), may hold values from -0.078125 to 0.078125
Outputs:
- output: bfloat16 [8192, 1408], P('dp')
- latent_grad: float32 [8192, 1408], P('dp')
- skip_grad: float32 [8192, 1408], P('dp')
- text_grad: float32 [333, 1024], replicated
- skip_w_grad: float32 [2816, 1408], P('tensor')
- skip_gain_grad: float32 [1408], replicated
- norm1_gain_grad: float32 [1408], replicated
- mod_w_grad: float32 [1408, 1408], replicated
- qkv_w_grad: float32 [1408, 3, 1408], P(None, None, 'tensor')
- qnorm_gain_grad: float32 [88], replicated
- knorm_gain_grad: float32 [88], replicated
- attn_out_w_grad: float32 [1408, 1408], P('tensor')
- norm2_gain_grad: float32 [1408], replicated
- cq_w_grad: float32 [1408, 1408], P(None, 'tensor')
- ckv_w_grad: float32 [1024, 2, 1408], P(None, None, 'tensor')
- cqnorm_gain_grad: float32 [88], replicated
- cknorm_gain_grad: float32 [88], replicated
- cross_out_w_grad: float32 [1408, 1408], P('tensor')
- norm3_gain_grad: float32 [1408], replicated
- fc1_w_grad: float32 [1408, 6144], P(None, 'tensor')
- fc2_w_grad: float32 [6144, 1408], P('tensor')
Inputs may be any that keep to these rules, and one draw needn't show every extreme that they name: Within each latent of 1024 consecutive tokens, positions is a permutation of the places of a 32 by 32 grid: column 0 is the row, column 1 the column, each place once.
All inputs are finite; a program needn't handle non-finite values.
Results may differ from a plain program's by a relative error of at most 0.028.
Values may be sent and summed in bfloat16 or wider, within the bound.
No kernel may reach another device: no remote copies, remote signals or barrier semaphores. Data moves between devices by JAX's collectives and lax.ppermute only.
A program may use at most 192 MiB of HBM per device.

v0:
```python
import jax
import jax.numpy as jnp
from jax import lax
from jax.sharding import PartitionSpec as P

GRID = 32


def partner_2(block, axis, stride):
    count = lax.axis_size(axis)
    route = []
    for low in range(count):
        high = low | 1 << stride
        if high != low and high < count:
            route += [(low, high), (high, low)]
    return lax.ppermute(block, axis, route)


def layer_norm(inputs, norm_gain):
    centered = inputs - jnp.mean(inputs, -1, keepdims=True)
    variance = jnp.mean(centered * centered, -1, keepdims=True)
    return centered * lax.rsqrt(variance + 1e-06) * norm_gain


def rotary_tables(positions, head_dim):
    quarter = head_dim // 4
    frequency = 10000.0 ** (-jnp.arange(quarter).astype(jnp.float32) / quarter)
    angles = positions.astype(jnp.float32)[:, :, None] * frequency
    return (jnp.cos(angles), jnp.sin(angles))


def rotate(inputs, cosine, sine_table):
    token_count, head_count, head_dim = inputs.shape
    pieces = inputs.reshape(token_count, head_count, 2, 2, head_dim // 4)
    first_half = pieces[:, :, :, 0]
    second = pieces[:, :, :, 1]
    cos_wide = cosine[:, None]
    sin_wide = sine_table[:, None]
    turned = jnp.stack(
        [first_half * cos_wide - second * sin_wide, first_half * sin_wide + second * cos_wide], 3
    )
    return turned.reshape(token_count, head_count, head_dim)


def tanh_gelu(pre_act):
    return jax.nn.gelu(pre_act, approximate=True)


def left_product(inputs, grads):
    return lax.dot_general(
        inputs, grads, (((0,), (0,)), ((), ())), preferred_element_type=jnp.float32
    )


def right_product(grads, weight):
    return lax.dot_general(
        grads, weight, (((1,), (1,)), ((), ())), preferred_element_type=jnp.float32
    )


def forward_term(left, weight):

    def term(start, count):
        return jnp.dot(left, weight, preferred_element_type=jnp.float32)

    return term


def backward_term(grads, weight):

    def term(start, count):
        return right_product(grads, weight)

    return term


def sum_rows(term_fn, token_count):
    return lax.psum(term_fn(0, token_count), "tensor")


def upper_flag(place, bit):
    return place // (1 << bit) % 2 == 1


def place_pair(own, partner, place, bit):
    upper = upper_flag(place, bit)
    first_block = jnp.where(upper, partner, own)
    second_block = jnp.where(upper, own, partner)
    return jnp.concatenate([first_block, second_block], 0)


def attend(queries, key_rows, value_rows, scaling):
    raw_scores = (
        jnp.einsum("nhd,khd->hnk", queries, key_rows, preferred_element_type=jnp.float32) * scaling
    )
    maximum = jnp.max(raw_scores, -1, keepdims=True)
    log_total = maximum + jnp.log(jnp.sum(jnp.exp(raw_scores - maximum), -1, keepdims=True))
    shares = jnp.exp(raw_scores - log_total).astype(jnp.bfloat16)
    mixture = jnp.einsum("hnk,khd->nhd", shares, value_rows, preferred_element_type=jnp.float32)
    return (mixture, log_total)


def attend_back(queries, key_rows, value_rows, log_total, grad_out, scaling):
    raw_scores = (
        jnp.einsum("nhd,khd->hnk", queries, key_rows, preferred_element_type=jnp.float32) * scaling
    )
    shares = jnp.exp(raw_scores - log_total)
    grad_share = jnp.einsum(
        "nhd,khd->hnk", grad_out, value_rows, preferred_element_type=jnp.float32
    )
    value_grad = jnp.einsum(
        "hnk,nhd->khd", shares.astype(jnp.bfloat16), grad_out, preferred_element_type=jnp.float32
    )
    weighted = jnp.sum(shares * grad_share, -1, keepdims=True)
    score_grad = (shares * (grad_share - weighted) * scaling).astype(jnp.bfloat16)
    query_grad = jnp.einsum(
        "hnk,khd->nhd", score_grad, key_rows, preferred_element_type=jnp.float32
    )
    key_grad = jnp.einsum("hnk,nhd->khd", score_grad, queries, preferred_element_type=jnp.float32)
    return (query_grad, key_grad, value_grad)


def local(
    latent,
    skip_input,
    text_tokens,
    condition,
    positions,
    cotangent,
    skip_w,
    skip_gain,
    norm1_gain,
    mod_w,
    qkv_w,
    qnorm_gain,
    knorm_gain,
    attn_out_w,
    norm2_gain,
    cq_w,
    ckv_w,
    cqnorm_gain,
    cknorm_gain,
    cross_out_w,
    norm3_gain,
    fc1_w,
    fc2_w,
):
    token_count, model_width = latent.shape
    head_dim = qnorm_gain.shape[0]
    local_width = cq_w.shape[1]
    local_heads = local_width // head_dim
    slab_width = skip_w.shape[0]
    text_count, text_width = text_tokens.shape
    scaling = head_dim ** (-0.5)
    group_size = GRID * GRID // token_count
    bit_count = group_size.bit_length() - 1
    dp_place = lax.axis_index("dp")
    cosine, sine_table = rotary_tables(positions, head_dim)
    joined = jnp.concatenate([latent, skip_input], 1)
    joined_part = lax.dynamic_slice_in_dim(
        joined, lax.axis_index("tensor") * slab_width, slab_width, 1
    )
    merged = sum_rows(forward_term(joined_part, skip_w), token_count)
    hidden_zero, skip_norm_back = jax.vjp(layer_norm, merged, skip_gain)
    silu_cond = jax.nn.silu(condition.astype(jnp.float32)).astype(jnp.bfloat16)
    shift = jnp.dot(silu_cond[None], mod_w, preferred_element_type=jnp.float32)[0]
    normed_local, norm1_back = jax.vjp(layer_norm, hidden_zero, norm1_gain)
    normed_one = (normed_local + shift).astype(jnp.bfloat16)
    qkv_flat = qkv_w.reshape(model_width, 3 * local_width)
    projected = jnp.dot(normed_one, qkv_flat, preferred_element_type=jnp.float32).reshape(
        token_count, 3, local_heads, head_dim
    )

    def query_key(query_raw, key_raw, query_gain, key_gain):
        return (
            rotate(layer_norm(query_raw, query_gain), cosine, sine_table),
            rotate(layer_norm(key_raw, key_gain), cosine, sine_table),
        )

    (queries, key_local), query_key_back = jax.vjp(
        query_key, projected[:, 0], projected[:, 1], qnorm_gain, knorm_gain
    )
    queries = queries.astype(jnp.bfloat16)
    pair_send = jnp.stack(
        [
            key_local.astype(jnp.bfloat16).reshape(token_count, local_width),
            projected[:, 2].astype(jnp.bfloat16).reshape(token_count, local_width),
        ],
        1,
    )
    pair_group = pair_send
    bit = 0
    pair_group = place_pair(pair_group, partner_2(pair_group, "dp", bit), dp_place, bit)
    key_count = pair_group.shape[0]
    key_rows = pair_group[:, 0].reshape(key_count, local_heads, head_dim)
    value_rows = pair_group[:, 1].reshape(key_count, local_heads, head_dim)
    attended, self_total = attend(queries, key_rows, value_rows, scaling)
    mixed_one = attended.reshape(token_count, local_width).astype(jnp.bfloat16)
    hidden_one = hidden_zero + sum_rows(forward_term(mixed_one, attn_out_w), token_count)
    normed_local, norm2_back = jax.vjp(layer_norm, hidden_one, norm2_gain)
    normed_two = normed_local.astype(jnp.bfloat16)
    cross_raw = jnp.dot(normed_two, cq_w, preferred_element_type=jnp.float32).reshape(
        token_count, local_heads, head_dim
    )
    cross_query, cross_query_back = jax.vjp(layer_norm, cross_raw, cqnorm_gain)
    cross_query = cross_query.astype(jnp.bfloat16)
    ckv_flat = ckv_w.reshape(text_width, 2 * local_width)
    text_proj = jnp.dot(text_tokens, ckv_flat, preferred_element_type=jnp.float32).reshape(
        text_count, 2, local_heads, head_dim
    )
    cross_key, cross_key_back = jax.vjp(layer_norm, text_proj[:, 0], cknorm_gain)
    cross_key = cross_key.astype(jnp.bfloat16)
    cross_value = text_proj[:, 1].astype(jnp.bfloat16)
    attended, cross_total = attend(cross_query, cross_key, cross_value, scaling)
    mixed_two = attended.reshape(token_count, local_width).astype(jnp.bfloat16)
    hidden_two = hidden_one + sum_rows(forward_term(mixed_two, cross_out_w), token_count)
    normed_local, norm3_back = jax.vjp(layer_norm, hidden_two, norm3_gain)
    normed_three = normed_local.astype(jnp.bfloat16)
    pre_act = jnp.dot(normed_three, fc1_w, preferred_element_type=jnp.float32)
    active, gelu_back = jax.vjp(tanh_gelu, pre_act)
    active = active.astype(jnp.bfloat16)
    output = (hidden_two + sum_rows(forward_term(active, fc2_w), token_count)).astype(jnp.bfloat16)
    residual_full = cotangent.astype(jnp.float32)
    out_grad = residual_full.astype(jnp.bfloat16)
    fc2_grad = left_product(active, out_grad)
    (pre_grad,) = gelu_back(right_product(out_grad, fc2_w))
    pre_grad = pre_grad.astype(jnp.bfloat16)
    fc1_grad = left_product(normed_three, pre_grad)
    norm3_in, norm3_grad = norm3_back(sum_rows(backward_term(pre_grad, fc1_w), token_count))
    residual = residual_full + norm3_in
    out_grad = residual.astype(jnp.bfloat16)
    cross_out_grad = left_product(mixed_two, out_grad)
    mixed_grad = (
        right_product(out_grad, cross_out_w)
        .astype(jnp.bfloat16)
        .reshape(token_count, local_heads, head_dim)
    )
    cq_head_grad, ck_head_grad, cv_head_grad = attend_back(
        cross_query, cross_key, cross_value, cross_total, mixed_grad, scaling
    )
    text_key_grad, text_value_grad = (
        lax.psum(ck_head_grad.reshape(text_count, local_width).astype(jnp.bfloat16), "dp").astype(
            jnp.float32
        ),
        lax.psum(cv_head_grad.reshape(text_count, local_width).astype(jnp.bfloat16), "dp").astype(
            jnp.float32
        ),
    )
    key_raw_grad, cknorm_part = cross_key_back(
        text_key_grad.reshape(text_count, local_heads, head_dim)
    )
    text_proj_grad = (
        jnp.stack([key_raw_grad, text_value_grad.reshape(text_count, local_heads, head_dim)], 1)
        .astype(jnp.bfloat16)
        .reshape(text_count, 2 * local_width)
    )
    ckv_grad = left_product(text_tokens, text_proj_grad).reshape(text_width, 2, local_width)
    text_part = right_product(text_proj_grad, ckv_flat)
    cross_raw_grad, cqnorm_grad = cross_query_back(cq_head_grad)
    cross_raw_grad = cross_raw_grad.reshape(token_count, local_width).astype(jnp.bfloat16)
    cq_grad = left_product(normed_two, cross_raw_grad)
    norm2_in, norm2_grad = norm2_back(sum_rows(backward_term(cross_raw_grad, cq_w), token_count))
    residual = residual + norm2_in
    out_grad = residual.astype(jnp.bfloat16)
    attn_out_grad = left_product(mixed_one, out_grad)
    mixed_grad = (
        right_product(out_grad, attn_out_w)
        .astype(jnp.bfloat16)
        .reshape(token_count, local_heads, head_dim)
    )
    query_grad, key_grad_all, value_grad_all = attend_back(
        queries, key_rows, value_rows, self_total, mixed_grad, scaling
    )
    pair_grad = jnp.stack(
        [
            key_grad_all.reshape(key_count, local_width),
            value_grad_all.reshape(key_count, local_width),
        ],
        1,
    )
    for bit in reversed(range(bit_count)):
        half = pair_grad.shape[0] // 2
        upper = upper_flag(dp_place, bit)
        keep_rows = jnp.where(upper, pair_grad[half:], pair_grad[:half])
        send_rows = jnp.where(upper, pair_grad[:half], pair_grad[half:])
        pair_grad = keep_rows + partner_2(send_rows.astype(jnp.bfloat16), "dp", bit).astype(
            send_rows.dtype
        )
    key_grad = pair_grad[:, 0].reshape(token_count, local_heads, head_dim)
    value_grad = pair_grad[:, 1].reshape(token_count, local_heads, head_dim)
    query_raw_grad, key_raw_local, qnorm_grad, knorm_grad = query_key_back((query_grad, key_grad))
    projected_grad = (
        jnp.stack([query_raw_grad, key_raw_local, value_grad], 1)
        .astype(jnp.bfloat16)
        .reshape(token_count, 3 * local_width)
    )
    qkv_grad = left_product(normed_one, projected_grad).reshape(model_width, 3, local_width)
    normed_grad = sum_rows(backward_term(projected_grad, qkv_flat), token_count)
    mod_vector = jnp.sum(normed_grad, 0)
    norm1_in, norm1_grad = norm1_back(normed_grad)
    residual = residual + norm1_in
    merged_grad, skip_gain_grad = skip_norm_back(residual)
    merged_grad = merged_grad.astype(jnp.bfloat16)
    skip_w_grad = left_product(joined_part, merged_grad)
    joined_grad = lax.all_gather(
        right_product(merged_grad, skip_w).astype(jnp.bfloat16), "tensor", axis=1, tiled=True
    ).astype(jnp.float32)
    fc1_grad, fc2_grad, cross_out_grad, cq_grad, qkv_grad, attn_out_grad, skip_w_grad = (
        lax.psum(fc1_grad.astype(jnp.bfloat16), "dp").astype(jnp.float32),
        lax.psum(fc2_grad.astype(jnp.bfloat16), "dp").astype(jnp.float32),
        lax.psum(cross_out_grad.astype(jnp.bfloat16), "dp").astype(jnp.float32),
        lax.psum(cq_grad.astype(jnp.bfloat16), "dp").astype(jnp.float32),
        lax.psum(qkv_grad.astype(jnp.bfloat16), "dp").astype(jnp.float32),
        lax.psum(attn_out_grad.astype(jnp.bfloat16), "dp").astype(jnp.float32),
        lax.psum(skip_w_grad.astype(jnp.bfloat16), "dp").astype(jnp.float32),
    )
    qnorm_grad, knorm_grad, cqnorm_grad = lax.psum(
        (qnorm_grad, knorm_grad, cqnorm_grad), ("dp", "tensor")
    )
    skip_gain_grad, norm1_grad, norm2_grad, norm3_grad, mod_vector = lax.psum(
        (skip_gain_grad, norm1_grad, norm2_grad, norm3_grad, mod_vector), "dp"
    )
    mod_grad = silu_cond.astype(jnp.float32)[:, None] * mod_vector[None, :]
    text_grad, cknorm_grad = (
        lax.psum(text_part.astype(jnp.bfloat16), "tensor").astype(jnp.float32),
        lax.psum(cknorm_part.astype(jnp.bfloat16), "tensor").astype(jnp.float32),
    )
    return (
        output,
        joined_grad[:, :model_width],
        joined_grad[:, model_width:],
        text_grad,
        skip_w_grad,
        skip_gain_grad,
        norm1_grad,
        mod_grad,
        qkv_grad,
        qnorm_grad,
        knorm_grad,
        attn_out_grad,
        norm2_grad,
        cq_grad,
        ckv_grad,
        cqnorm_grad,
        cknorm_grad,
        cross_out_grad,
        norm3_grad,
        fc1_grad,
        fc2_grad,
    )


def solution(mesh):
    placed = (
        P("dp", None),
        P("dp", None),
        P(),
        P(),
        P("dp", None),
        P("dp", None),
        P("tensor", None),
        P(),
        P(),
        P(),
        P(None, None, "tensor"),
        P(),
        P(),
        P("tensor", None),
        P(),
        P(None, "tensor"),
        P(None, None, "tensor"),
        P(),
        P(),
        P("tensor", None),
        P(),
        P(None, "tensor"),
        P("tensor", None),
    )
    return jax.shard_map(
        local,
        mesh=mesh,
        in_specs=placed,
        out_specs=(
            P("dp", None),
            P("dp", None),
            P("dp", None),
            P(),
            P("tensor", None),
            P(),
            P(),
            P(),
            P(None, None, "tensor"),
            P(),
            P(),
            P("tensor", None),
            P(),
            P(None, "tensor"),
            P(None, None, "tensor"),
            P(),
            P(),
            P("tensor", None),
            P(),
            P(None, "tensor"),
            P("tensor", None),
        ),
        check_vma=False,
    )
```

profile of v0, /device:TPU:1, one launch (start us, length us, event | category | flops | bytes accessed | tf_op | source)
XLA Modules:
  0.0 1067.8 jit_solution(383550986374451534)
XLA Ops:
  7.3 4.1 fusion.121
  16.2 92.2 %all-reduce.17.cloned.1.call-done = f32[512,1408]{1,0:T(8,128)} async-done(((f32[512,1408]{1,0:T(8,128)}), f32[512,1408]{1,0:T(8,128)}) %all-reduce.17.cloned.1.call-update) | async-done | bytes 2883600 | tf_op jit(solution)/shard_map/psum | solution.py:78
  119.0 4.9 collective-permute-start
  135.3 88.4 %all-reduce.19.cloned.1.call-done = f32[512,1408]{1,0:T(8,128)} async-done(((f32[512,1408]{1,0:T(8,128)}), f32[512,1408]{1,0:T(8,128)}) %all-reduce.19.cloned.1.call-update) | async-done | bytes 2883600 | tf_op jit(solution)/shard_map/psum | solution.py:78
  238.0 4.6 fusion.146
  242.6 91.7 %all-reduce.21.cloned.1.call-done = f32[512,1408]{1,0:T(8,128)} async-done(((f32[512,1408]{1,0:T(8,128)}), f32[512,1408]{1,0:T(8,128)}) %all-reduce.21.cloned.1.call-update) | async-done | bytes 2883600 | tf_op jit(solution)/shard_map/psum | solution.py:78
  347.5 96.0 %all-reduce.23.cloned.1.call-done = f32[512,1408]{1,0:T(8,128)} async-done(((f32[512,1408]{1,0:T(8,128)}), f32[512,1408]{1,0:T(8,128)}) %all-reduce.23.cloned.1.call-update) | async-done | bytes 2883600 | tf_op jit(solution)/shard_map/psum | solution.py:78
  443.5 4.2 multiply_reduce_fusion.2
  460.5 96.2 %all-reduce.25.cloned.1.call-done = f32[512,1408]{1,0:T(8,128)} async-done(((f32[512,1408]{1,0:T(8,128)}), f32[512,1408]{1,0:T(8,128)}) %all-reduce.25.cloned.1.call-update) | async-done | bytes 2883600 | tf_op jit(solution)/shard_map/psum | solution.py:78
  556.8 4.2 multiply_reduce_fusion.3
  571.1 10.9 %fusion.7 = f32[2,88,1024]{2,1,0:T(8,128)S(1)} fusion(f32[2,512,1024]{2,1,0:T(8,128)} %fusion.149, f32[2,512,1024]{2,1,0:T(8,128)} %copy-done.8, f32[2,512]{1,0:T(2,128)} %copy-done.107, bf16[512,2,88]{0,1,2:T(2,128)(2,1)S(1)} %bitcast.205), kind=kOutput, calls=%fused_computation.41 | convolution fusion | flops 193988608 | bytes 9293824 | tf_op jit(solution)/shard_map/hnk,nhd->khd/dot_general | solution.py:119
  582.9 5.0 collective-permute-start.1
  587.9 5.1 fusion.120
  593.0 12.2 %fusion.48 = f32[512,2,88]{0,2,1:T(8,128)} fusion(bf16[1024,2,88]{0,2,1:T(8,128)(2,1)} %bitcast.203, f32[2,512,1024]{2,1,0:T(8,128)} %fusion.149, f32[2,512,1024]{2,1,0:T(8,128)} %copy-done.8, f32[2,512]{1,0:T(2,128)} %copy-done.107), kind=kOutput, calls=%fused_computation.83 | convolution fusion | flops 193988608 | bytes 9113600 | tf_op jit(solution)/shard_map/hnk,khd->nhd/dot_general | solution.py:116
  621.6 4.4 convolution_convert_fusion
  642.2 112.9 %all-reduce.29.cloned.1.call-done = (f32[512,1408]{1,0:T(8,128)}, f32[512,1408]{1,0:T(8,128)}) async-done(((f32[512,1408]{1,0:T(8,128)}, f32[512,1408]{1,0:T(8,128)}), (f32[512,1408]{1,0:T(8,128)}, f32[512,1408]{1,0:T(8,128)})) %all-reduce.29.cloned.1.call-update) | async-done | bytes 5767184 | tf_op jit(solution)/shard_map/psum | solution.py:78
  772.6 65.5 %all-reduce.4 = (f32[88]{0:T(128)}, f32[88]{0:T(128)}, f32[88]{0:T(128)}) all-reduce(f32[88]{0:T(128)S(1)} %reduce_sum.552, f32[88]{0:T(128)S(1)} %reduce_sum.554, f32[88]{0:T(128)S(1)} %copy-done.152), channel_id=1, replica_groups=mesh['dp'=16,'tensor'=8] {'dp','tensor'}, use_global_device_ids=true, to_apply=%region_57.58 | all-reduce | flops 264 | bytes 2112 | tf_op jit(solution)/shard_map/psum | solution.py:317
  838.1 50.8 %all-reduce.5 = (f32[1408]{0:T(1024)}, f32[1408]{0:T(1024)}, f32[1408]{0:T(1024)S(1)}, f32[1408]{0:T(1024)}, f32[1408]{0:T(1024)}) all-reduce(f32[1408]{0:T(1024)S(1)} %get-tuple-element.90, f32[1408]{0:T(1024)S(1)} %get-tuple-element.84, f32[1408]{0:T(1024)S(1)} %get-tuple-element.92, ...), channel_id=1, replica_groups=mesh['dp'=16,'tensor'=8] {'dp'}, use_global_device_ids=true, to_apply=%region_50.51 | all-reduce | flops 7040 | bytes 56320 | tf_op jit(solution)/shard_map/psum | solution.py:320
  888.9 4.1 add_convert_fusion.1
  896.9 12.3 %all-reduce.31.cloned.1.call-done = (bf16[333,1,2,88]{0,3,2,1:T(8,128)(2,1)}, bf16[333,176]{0,1:T(8,128)(2,1)}, bf16[352,1408]{1,0:T(8,128)(2,1)}, bf16[1408,3,1...) async-done(((bf16[333,1,2,88]{0,3,2,1:T(8,128)(2,1)}, ...) | async-done | bytes 8524752 | tf_op jit(solution)/shard_map/psum | solution.py:245
  912.9 61.8 %all-gather.2.cloned.1.call-done = bf16[512,2816]{0,1:T(8,128)(2,1)} async-done(((bf16[512,352]{0,1:T(8,128)(2,1)}), bf16[512,2816]{0,1:T(8,128)(2,1)}) %all-gather.2.cloned.1.call-update) | async-done | bytes 2883600 | tf_op jit(solution)/shard_map/all_gather | solution.py:305
  974.7 5.1 fusion.137
  987.0 16.4 %psum.203 = bf16[88]{0:T(256)(128)(2,1)S(1)} all-reduce(bf16[88]{0:T(256)(128)(2,1)S(1)} %reduce_sum.559), channel_id=1, replica_groups=mesh['dp'=16,'tensor'=8] {'tensor'}, use_global_device_ids=true, to_apply=%region_68.69 | all-reduce | flops 88 | bytes 352 | tf_op jit(solution)/shard_map/psum | solution.py:326
  1017.5 41.0 %all-reduce.27.cloned.1.call-done = bf16[333,1024]{1,0:T(8,128)(2,1)} async-done(((bf16[333,1024]{1,0:T(8,128)(2,1)}), bf16[333,1024]{1,0:T(8,128)(2,1)}) %all-reduce.27.cloned.1.call-update) | async-done | bytes 682000 | tf_op jit(solution)/shard_map/psum | solution.py:325
  (485 shorter events, 157.5 us)
Async XLA Ops:
  7.2 331.3 %copy-start = (bf16[1408,768]{1,0:T(8,128)(2,1)S(1)}, bf16[1408,768]{1,0:T(8,128)(2,1)}, u32[]{:S(2)}) copy-start(bf16[1408,768]{1,0:T(8,128)(2,1)} %param.44) | copy-start | bytes 6488068
  7.2 101.2 %all-reduce.17.cloned.1.call-start = ((), (), s32[]{:S(2)}) async-start(), calls=%async_computation | async-start | bytes 5767168 | tf_op jit(solution)/shard_map/psum | solution.py:78
  11.4 212.3 %all-reduce.19.cloned.1.call-start = ((), (), s32[]{:S(2)}) async-start(), calls=%async_computation.1 | async-start | bytes 5767168 | tf_op jit(solution)/shard_map/psum | solution.py:78
  12.1 105.5 %copy-start.126 = (f32[2,2,22]{2,1,0:T(2,128)}, f32[2,2,22]{2,1,0:T(2,128)S(1)}, u32[]{:S(2)}) copy-start(f32[2,2,22]{2,1,0:T(2,128)S(1)} %mul.790) | copy-start | bytes 1060
  12.2 105.6 %copy-start.124 = (f32[2,2,22]{2,1,0:T(2,128)}, f32[2,2,22]{2,1,0:T(2,128)S(1)}, u32[]{:S(2)}) copy-start(f32[2,2,22]{2,1,0:T(2,128)S(1)} %mul.775) | copy-start | bytes 1060
  13.3 104.8 %copy-start.58 = (f32[512,2,22]{0,2,1:T(8,128)}, f32[512,2,22]{0,2,1:T(8,128)S(1)}, u32[]{:S(2)}) copy-start(f32[512,2,22]{0,2,1:T(8,128)S(1)} %get-tuple-element.164) | copy-start | bytes 270340
  13.3 104.8 %copy-start.59 = (f32[512,2,22]{0,2,1:T(8,128)}, f32[512,2,22]{0,2,1:T(8,128)S(1)}, u32[]{:S(2)}) copy-start(f32[512,2,22]{0,2,1:T(8,128)S(1)} %get-tuple-element.165) | copy-start | bytes 270340
  16.2 98.3 %copy-start.139 = (f32[1408]{0:T(1024)}, f32[1408]{0:T(1024)S(1)}, u32[]{:S(2)}) copy-start(f32[1408]{0:T(1024)S(1)} %convolution_reduce_fusion) | copy-start | bytes 16900
  16.2 96.7 %copy-start.73 = (f32[1408]{0:T(1024)S(1)}, f32[1408]{0:T(1024)}, u32[]{:S(2)}) copy-start(f32[1408]{0:T(1024)} %param.30) | copy-start | bytes 16900
  113.1 110.6 %copy-start.78 = (f32[512]{0:T(512)}, f32[512]{0:T(512)S(1)}, u32[]{:S(2)}) copy-start(f32[512]{0:T(512)S(1)} %fusion.101) | copy-start | bytes 6148
  119.0 6.2 collective-permute-start
  131.9 202.4 %all-reduce.21.cloned.1.call-start = ((), (), s32[]{:S(2)}) async-start(), calls=%async_computation.2 | async-start | bytes 5767168 | tf_op jit(solution)/shard_map/psum | solution.py:78
  238.0 205.5 %all-reduce.23.cloned.1.call-start = ((), (), s32[]{:S(2)}) async-start(), calls=%async_computation.3 | async-start | bytes 5767168 | tf_op jit(solution)/shard_map/psum | solution.py:78
  347.1 100.7 %copy-start.135 = (f32[512]{0:T(512)S(1)}, f32[512]{0:T(512)}, u32[]{:S(2)}) copy-start(f32[512]{0:T(512)} %copy-done.134) | copy-start | bytes 6148
  347.1 209.7 %all-reduce.25.cloned.1.call-start = ((), (), s32[]{:S(2)}) async-start(), calls=%async_computation.4 | async-start | bytes 5767168 | tf_op jit(solution)/shard_map/psum | solution.py:78
  458.2 98.6 %copy-start.85 = (f32[1408]{0:T(1024)S(1)}, f32[1408]{0:T(1024)}, u32[]{:S(2)}) copy-start(f32[1408]{0:T(1024)} %param.37) | copy-start | bytes 16900
  458.2 98.6 %copy-start.97 = (f32[512]{0:T(512)S(1)}, f32[512]{0:T(512)}, u32[]{:S(2)}) copy-start(f32[512]{0:T(512)} %copy-done.96) | copy-start | bytes 6148
  458.2 98.6 %copy-start.115 = (f32[512]{0:T(512)S(1)}, f32[512]{0:T(512)}, u32[]{:S(2)}) copy-start(f32[512]{0:T(512)} %copy-done.114) | copy-start | bytes 6148
  460.4 100.6 %copy-start.133 = (f32[512]{0:T(512)S(1)}, f32[512]{0:T(512)}, u32[]{:S(2)}) copy-start(f32[512]{0:T(512)} %copy-done.132) | copy-start | bytes 6148
  460.5 294.6 %all-reduce.29.cloned.1.call-start = ((), (), s32[]{:S(2)}) async-start(), calls=%async_computation.7 | async-start | bytes 11534336 | tf_op jit(solution)/shard_map/psum | solution.py:78
  582.9 24.4 %collective-permute-start.1 = (bf16[512,2,176]{0,2,1:T(8,128)(2,1)}, bf16[512,2,176]{0,2,1:T(8,128)(2,1)}, u32[]{:S(2)}, u32[]{:S(2)}) collective-permute-start(bf16[512,2,176]{0,2,1:T(8,128)(2,1)} %select_convert_fusion), channel_id=1, source_target_pairs={{0,8},{8,0},{16,24},{24,16},{32,40},{40,32},{48,56},{56,48},{64,72... | collective-permute-start | bytes 1081352 | tf_op jit(solution)/shard_map/ppermute | solution.py:16
  620.3 288.9 %all-reduce.31.cloned.1.call-start = ((), (), s32[]{:S(2)}) async-start(), calls=%async_computation.8 | async-start | bytes 17121280 | tf_op jit(solution)/shard_map/psum | solution.py:245
  767.8 206.9 %all-gather.2.cloned.1.call-start = ((), (), s32[]{:S(2)}) async-start(), calls=%async_computation.5 | async-start | bytes 3244032 | tf_op jit(solution)/shard_map/all_gather | solution.py:305
  772.3 286.1 %all-reduce.27.cloned.1.call-start = ((), (), s32[]{:S(2)}) async-start(), calls=%async_computation.6 | async-start | bytes 1376256 | tf_op jit(solution)/shard_map/psum | solution.py:325
  (145 other events, 1089.1 us)
Sparse Core Ops, SparseCore 0:
  11.6 96.7 all-reduce.16
  132.0 91.7 all-reduce.18
  238.1 96.1 all-reduce.20
  347.2 96.2 all-reduce.22
  460.6 96.1 all-reduce.24
  620.4 134.6 all-reduce.28
  767.9 141.2 all-reduce.30
  912.3 62.3 all-gather.1
  978.0 80.4 all-reduce.26
where the time goes:
time: 1080 us; the launch traced here: 1070 us
  waiting for transfers between devices  694 us (64%)
  blocking collectives  133 us (12%)
  matrix products  102 us (9%)
  other arithmetic  75.7 us (7%)
  local copies, waits for them, and re-layouts  36.5 us (3%)
  between operations  16.1 us (1%)
  starting transfers between devices  11.1 us (1%)
    psum x6, waiting for transfers between devices, sum_rows(): return lax.psum(term_fn(0, token_count), 'tensor')  577 us
    psum x1, blocking collectives, local(): lax.psum((qnorm_grad, knorm_grad, cqnorm_grad), ('dp', 'tensor'))  65.5 us
    all_gather x1, waiting for transfers between devices, local(): lax.all_gather(right_product(merged_grad, skip_w).astype(jnp.bfloat16), '...  61.8 us
    psum x1, blocking collectives, local(): lax.psum((skip_gain_grad, norm1_grad, norm2_grad, norm3_grad, mod_vector)...  50.8 us
    psum x1, waiting for transfers between devices, local(): lax.psum(text_part.astype(jnp.bfloat16), 'tensor').astype(jnp.float32)  41 us
    unnamed x318, local copies, waits for them, and re-layouts  25.6 us
  transfers between devices with their start and end apart: 11, of which 10 were waited for; matrix products, arithmetic and copies ran while one was open for 9% of the time, Pallas kernels for 0%

commit v1 on v0

v1 whole, which is shorter than its diff:
```python
import jax
import jax.numpy as jnp
from jax import lax
from jax.experimental import pallas as pl
from jax.experimental.pallas import tpu as pltpu
from jax.sharding import PartitionSpec as P

BF16 = jnp.bfloat16
F32 = jnp.float32


def layer_norm(inputs, norm_gain):
    centered = inputs - jnp.mean(inputs, -1, keepdims=True)
    variance = jnp.mean(centered * centered, -1, keepdims=True)
    return centered * lax.rsqrt(variance + 1e-06) * norm_gain


def rotary_tables(positions, head_dim):
    quarter = head_dim // 4
    frequency = 10000.0 ** (-jnp.arange(quarter).astype(F32) / quarter)
    angles = positions.astype(F32)[:, :, None] * frequency
    cosine, sine = jnp.cos(angles), jnp.sin(angles)
    cos_wide = jnp.stack([cosine, cosine], 2).reshape(positions.shape[0], head_dim)
    sin_wide = jnp.stack([-sine, sine], 2).reshape(positions.shape[0], head_dim)
    return cos_wide, sin_wide


def left_product(inputs, grads):
    return lax.dot_general(
        inputs, grads, (((0,), (0,)), ((), ())), preferred_element_type=jnp.float32
    )


def right_product(grads, weight):
    return lax.dot_general(
        grads, weight, (((1,), (1,)), ((), ())), preferred_element_type=jnp.float32
    )


def exchange(blocks, axis="tensor"):
    return lax.all_to_all(blocks, axis, 0, 0, tiled=True)


def spread(block, axis="tensor"):
    count = lax.axis_size(axis)
    return jnp.broadcast_to(block[None], (count,) + block.shape)


def after(value, *earlier):
    return lax.optimization_barrier((value,) + earlier)[0]


def pad_rows(rows, multiple):
    extra = -rows.shape[0] % multiple
    return jnp.pad(rows, ((0, extra),) + ((0, 0),) * (rows.ndim - 1))


def permute_gather(block, axis="tensor"):
    count = lax.axis_size(axis)
    place = lax.axis_index(axis)
    out = jnp.zeros((count,) + block.shape, block.dtype)
    out = lax.dynamic_update_index_in_dim(out, block, place, 0)
    for step in range(1, count):
        got = lax.ppermute(block, axis, [(i, i ^ step) for i in range(count)])
        out = lax.dynamic_update_index_in_dim(out, got, place ^ step, 0)
    return out


def dp_slice(rows, unit):
    places = lax.axis_size("dp")
    each = -(-rows.shape[0] // (places * unit)) * unit
    rows = pad_rows(rows, each * places)
    return lax.dynamic_slice_in_dim(rows, lax.axis_index("dp") * each, each, 0)


def dp_routes():
    count = lax.axis_size("dp")
    place = lax.axis_index("dp")
    stages = []
    for low, size in ((0, 2), (1, 4), (3, 2)):
        part = place // (1 << low) % size
        routes = []
        for step in range(1, size):
            route = []
            for source in range(count):
                here = source // (1 << low) % size
                there = (here + step) % size
                route.append((source, source + ((there - here) << low)))
            routes.append(route)
        stages.append((size, part, routes))
    return stages


def scatter_dp(grad):
    for size, part, routes in dp_routes():
        rows = grad.shape[0] // size
        total = lax.dynamic_slice_in_dim(grad, part * rows, rows, 0).astype(F32)
        for step, route in enumerate(routes, 1):
            send = lax.dynamic_slice_in_dim(grad, (part + step) % size * rows, rows, 0)
            total = total + lax.ppermute(send.astype(BF16), "dp", route).astype(F32)
        grad = total
    return grad


def spread_dp(part_rows):
    rows_all = part_rows.astype(BF16)
    for size, part, routes in reversed(dp_routes()):
        rows = rows_all.shape[0]
        out = jnp.zeros((size * rows,) + rows_all.shape[1:], rows_all.dtype)
        out = lax.dynamic_update_slice_in_dim(out, rows_all, part * rows, 0)
        for step, route in enumerate(routes, 1):
            got = lax.ppermute(rows_all, "dp", route)
            out = lax.dynamic_update_slice_in_dim(out, got, (part - step) % size * rows, 0)
        rows_all = out
    return rows_all


def sum_dp(grad):
    return spread_dp(scatter_dp(grad))


def core_swap(block):
    count = lax.axis_size("dp")
    return lax.ppermute(block, "dp", [(i, i ^ 1) for i in range(count)])


def params(limit_mb, grid=0):
    return pltpu.CompilerParams(
        vmem_limit_bytes=limit_mb * 1024 * 1024,
        dimension_semantics=("arbitrary",) * grid if grid else None,
    )


def dot(left, right):
    return lax.dot_general(left, right, (((1,), (0,)), ((), ())), preferred_element_type=F32)


def dot_t(left, right):
    return lax.dot_general(left, right, (((1,), (1,)), ((), ())), preferred_element_type=F32)


def t_dot(left, right):
    return lax.dot_general(left, right, (((0,), (0,)), ((), ())), preferred_element_type=F32)


def norm_parts(rows):
    centered = rows - jnp.mean(rows, -1, keepdims=True)
    scale = lax.rsqrt(jnp.mean(centered * centered, -1, keepdims=True) + 1e-06)
    return centered * scale, scale


def norm_back(unit, scale, gain, grad):
    weighted = grad * gain
    rows = scale * (
        weighted
        - jnp.mean(weighted, -1, keepdims=True)
        - unit * jnp.mean(weighted * unit, -1, keepdims=True)
    )
    return rows, jnp.sum(grad * unit, 0, keepdims=True)


def add_blocks(blocks):
    total = blocks[0].astype(F32)
    for i in range(1, blocks.shape[0]):
        total = total + blocks[i].astype(F32)
    return total


def whole(shape):
    return pl.BlockSpec(shape, lambda *place: (0,) * len(shape))


def struct(shape, kind):
    return jax.ShapeDtypeStruct(shape, kind)


def swap(rows):
    quarter = rows.shape[1] // 4
    cut = [rows[:, i * quarter : (i + 1) * quarter] for i in range(4)]
    return jnp.concatenate([cut[1], cut[0], cut[3], cut[2]], 1)


def first_norms(got, skip_gain, norm1_gain, shift):
    count, rows, width = got.shape

    def kernel(got_ref, skip_ref, gain_ref, shift_ref, merged_ref, hidden_ref, out_ref):
        merged = add_blocks(got_ref)
        merged_ref[...] = merged
        hidden = norm_parts(merged)[0] * skip_ref[...]
        hidden_ref[...] = hidden
        normed = (norm_parts(hidden)[0] * gain_ref[...] + shift_ref[...]).astype(BF16)
        for i in range(count):
            out_ref[i] = normed

    return pl.pallas_call(
        kernel,
        out_shape=(
            struct((rows, width), F32),
            struct((rows, width), F32),
            struct((count, rows, width), BF16),
        ),
        compiler_params=params(32),
        name="first_norms",
    )(got, skip_gain[None], norm1_gain[None], shift[None])


def project(normed, weight, cos_wide, sin_wide, qgain, kgain):
    tokens, width = normed.shape
    each = weight.shape[1] // 3
    head = qgain.shape[0]
    heads = each // head
    block = 256

    def kernel(x_ref, w_ref, cos_ref, sin_ref, qg_ref, kg_ref, raw_ref, q_ref, kv_ref):
        out = dot(x_ref[...], w_ref[...])
        raw_ref[...] = out[:, : 2 * each]
        kv_ref[:, each : 2 * each] = out[:, 2 * each :].astype(BF16)
        cos, sin = cos_ref[...], sin_ref[...]
        for h in range(heads):
            for part, gain_ref, to_ref in ((0, qg_ref, q_ref), (1, kg_ref, kv_ref)):
                start = part * each + h * head
                rows = norm_parts(out[:, start : start + head])[0] * gain_ref[...]
                turned = rows * cos + swap(rows) * sin
                to_ref[:, h * head : (h + 1) * head] = turned.astype(BF16)

    row = lambda size: pl.BlockSpec((block, size), lambda i: (i, 0))
    return pl.pallas_call(
        kernel,
        grid=(tokens // block,),
        in_specs=[
            row(width),
            whole(weight.shape),
            row(head),
            row(head),
            whole((1, head)),
            whole((1, head)),
        ],
        out_specs=(row(2 * each), row(each), row(2 * each)),
        out_shape=(
            struct((tokens, 2 * each), F32),
            struct((tokens, each), BF16),
            struct((tokens, 2 * each), BF16),
        ),
        compiler_params=params(40, 1),
        name="project",
    )(normed, weight, cos_wide, sin_wide, qgain[None], kgain[None])


def self_attention(queries, own, other, out_w, head):
    tokens, each = queries.shape
    heads = each // head
    width = out_w.shape[1]
    keys = 2 * tokens
    scaling = head ** (-0.5)
    block = 256

    def kernel(q_ref, own_ref, other_ref, w_ref, mixed_ref, total_ref, out_ref, kv_ref):
        @pl.when(pl.program_id(0) == 0)
        def _():
            kv_ref[:tokens] = own_ref[...]
            kv_ref[tokens:] = other_ref[...]

        for h in range(heads):
            cut = slice(h * head, (h + 1) * head)
            scores = dot_t(q_ref[:, cut], kv_ref[:, cut]) * scaling
            most = jnp.max(scores, -1, keepdims=True)
            total = most + jnp.log(jnp.sum(jnp.exp(scores - most), -1, keepdims=True))
            total_ref[:, h : h + 1] = total
            shares = jnp.exp(scores - total).astype(BF16)
            mixture = dot(shares, kv_ref[:, each + h * head : each + (h + 1) * head])
            mixed_ref[:, cut] = mixture.astype(BF16)
        out_ref[...] = dot(mixed_ref[...], w_ref[...]).astype(BF16)

    row = lambda size: pl.BlockSpec((block, size), lambda i: (i, 0))
    return pl.pallas_call(
        kernel,
        grid=(tokens // block,),
        in_specs=[row(each), whole(own.shape), whole(other.shape), whole(out_w.shape)],
        out_specs=(row(each), row(heads), row(width)),
        out_shape=(
            struct((tokens, each), BF16),
            struct((tokens, heads), F32),
            struct((tokens, width), BF16),
        ),
        scratch_shapes=[pltpu.VMEM((keys, 2 * each), BF16)],
        compiler_params=params(48, 1),
        name="self_attention",
    )(queries, own, other, out_w)


def self_attention_back(queries, own, other, totals, grad, out_w, head):
    tokens, each = queries.shape
    heads = each // head
    width = out_w.shape[1]
    keys = 2 * tokens
    scaling = head ** (-0.5)
    block = 256
    steps = tokens // block

    def kernel(q_ref, own_ref, other_ref, total_ref, grad_ref, w_ref, dq_ref, down_ref, dother_ref, kv_ref, dkv_ref, dm_ref):
        step = pl.program_id(0)

        @pl.when(step == 0)
        def _():
            kv_ref[:tokens] = own_ref[...]
            kv_ref[tokens:] = other_ref[...]
            dkv_ref[...] = jnp.zeros_like(dkv_ref)

        dm_ref[...] = dot_t(grad_ref[...], w_ref[...]).astype(BF16)
        for h in range(heads):
            cut = slice(h * head, (h + 1) * head)
            vcut = slice(each + h * head, each + (h + 1) * head)
            rows, grads = q_ref[:, cut], dm_ref[:, cut]
            keys_h, values_h = kv_ref[:, cut], kv_ref[:, vcut]
            shares = jnp.exp(dot_t(rows, keys_h) * scaling - total_ref[:, h : h + 1])
            dshares = dot_t(grads, values_h)
            dkv_ref[:, vcut] += t_dot(shares.astype(BF16), grads)
            weighted = jnp.sum(shares * dshares, -1, keepdims=True)
            dscores = (shares * (dshares - weighted) * scaling).astype(BF16)
            dq_ref[:, cut] = dot(dscores, keys_h)
            dkv_ref[:, cut] += t_dot(dscores, rows)

        @pl.when(step == steps - 1)
        def _():
            down_ref[...] = dkv_ref[:tokens]
            dother_ref[...] = dkv_ref[tokens:].astype(BF16)

    row = lambda size: pl.BlockSpec((block, size), lambda i: (i, 0))
    return pl.pallas_call(
        kernel,
        grid=(steps,),
        in_specs=[
            row(each),
            whole(own.shape),
            whole(other.shape),
            row(heads),
            row(width),
            whole(out_w.shape),
        ],
        out_specs=(row(each), whole(own.shape), whole(own.shape)),
        out_shape=(
            struct((tokens, each), F32),
            struct(own.shape, F32),
            struct(own.shape, BF16),
        ),
        scratch_shapes=[
            pltpu.VMEM((keys, 2 * each), BF16),
            pltpu.VMEM((keys, 2 * each), F32),
            pltpu.VMEM((block, each), BF16),
        ],
        compiler_params=params(48, 1),
        name="self_attention_back",
    )(queries, own, other, totals, grad, out_w)


def project_back(raw, cos_wide, sin_wide, qgain, kgain, dq, down, arrived, weight):
    tokens = raw.shape[0]
    each = raw.shape[1] // 2
    head = qgain.shape[0]
    heads = each // head
    width = weight.shape[0]
    block = 256

    def kernel(raw_ref, cos_ref, sin_ref, qg_ref, kg_ref, dq_ref, down_ref, arr_ref, w_ref, dp_ref, out_ref, dqg_ref, dkg_ref):
        @pl.when(pl.program_id(0) == 0)
        def _():
            dqg_ref[...] = jnp.zeros_like(dqg_ref)
            dkg_ref[...] = jnp.zeros_like(dkg_ref)

        cos, sin = cos_ref[...], sin_ref[...]
        dkv = down_ref[...] + arr_ref[...].astype(F32)
        dp_ref[:, 2 * each :] = dkv[:, each:].astype(BF16)
        for h in range(heads):
            cut = slice(h * head, (h + 1) * head)
            for part, gain_ref, dgain_ref in ((0, qg_ref, dqg_ref), (1, kg_ref, dkg_ref)):
                turned = dq_ref[:, cut] if part == 0 else dkv[:, cut]
                grad = turned * cos - swap(turned) * sin
                start = part * each + h * head
                unit, scale = norm_parts(raw_ref[:, start : start + head])
                rows, dgain = norm_back(unit, scale, gain_ref[...], grad)
                dgain_ref[...] += dgain
                dp_ref[:, start : start + head] = rows.astype(BF16)
        out_ref[...] = dot_t(dp_ref[...], w_ref[...]).astype(BF16)

    row = lambda size: pl.BlockSpec((block, size), lambda i: (i, 0))
    return pl.pallas_call(
        kernel,
        grid=(tokens // block,),
        in_specs=[
            row(2 * each),
            row(head),
            row(head),
            whole((1, head)),
            whole((1, head)),
            row(each),
            row(2 * each),
            row(2 * each),
            whole(weight.shape),
        ],
        out_specs=(row(3 * each), row(width), whole((1, head)), whole((1, head))),
        out_shape=(
            struct((tokens, 3 * each), BF16),
            struct((tokens, width), BF16),
            struct((1, head), F32),
            struct((1, head), F32),
        ),
        compiler_params=params(40, 1),
        name="project_back",
    )(raw, cos_wide, sin_wide, qgain[None], kgain[None], dq, down, arrived, weight)


def text_scores(rows, keys_h, scaling, count):
    scores = dot_t(rows, keys_h) * scaling
    place = lax.broadcasted_iota(jnp.int32, scores.shape, 1)
    scores = jnp.where(place < count, scores, -1e30)
    most = jnp.max(scores, -1, keepdims=True)
    total = most + jnp.log(jnp.sum(jnp.exp(scores - most), -1, keepdims=True))
    return jnp.exp(scores - total)


def cross_layer(got, hidden_zero, pack, text, gains, head_gain, text_count):
    count, rows, width = got.shape
    head = head_gain.shape[0]
    each = text.shape[2] // 2
    heads = each // head
    scaling = head ** (-0.5)
    slices, _, deep, _ = pack.shape

    def kernel(got_ref, h0_ref, pack_ref, text_ref, g2_ref, g3_ref, hg_ref, h1_ref, h2_ref, n2_ref, raw_ref, mixed_ref, out_ref):
        step = pl.program_id(0)

        @pl.when(step == 0)
        def _():
            hidden = h0_ref[...] + add_blocks(got_ref)
            h1_ref[...] = hidden
            h2_ref[...] = hidden
            n2_ref[...] = (norm_parts(hidden)[0] * g2_ref[...]).astype(BF16)

        weights = pack_ref[:, 0].reshape(slices * deep, width)
        raw = dot_t(n2_ref[...], weights[each : 2 * each])
        raw_ref[0] = raw
        for h in range(heads):
            cut = slice(h * head, (h + 1) * head)
            vcut = slice(each + h * head, each + (h + 1) * head)
            queries = (norm_parts(raw[:, cut])[0] * hg_ref[...]).astype(BF16)
            shares = text_scores(queries, text_ref[0, :, cut], scaling, text_count)
            mixed_ref[0, :, cut] = dot(shares.astype(BF16), text_ref[0, :, vcut]).astype(BF16)
        h2_ref[...] += dot(mixed_ref[0], weights[:each])

        @pl.when(step == count - 1)
        def _():
            normed = (norm_parts(h2_ref[...])[0] * g3_ref[...]).astype(BF16)
            for i in range(count):
                out_ref[i] = normed

    one = lambda size: pl.BlockSpec((1, rows, size), lambda i: (i, 0, 0))
    return pl.pallas_call(
        kernel,
        grid=(count,),
        in_specs=[
            whole(got.shape),
            whole((rows, width)),
            pl.BlockSpec((slices, 1, deep, width), lambda i: (0, i, 0, 0)),
            pl.BlockSpec((1,) + text.shape[1:], lambda i: (i, 0, 0)),
            whole((1, width)),
            whole((1, width)),
            whole((1, head)),
        ],
        out_specs=(
            whole((rows, width)),
            whole((rows, width)),
            whole((rows, width)),
            one(each),
            one(each),
            whole(got.shape),
        ),
        out_shape=(
            struct((rows, width), F32),
            struct((rows, width), F32),
            struct((rows, width), BF16),
            struct((count, rows, each), F32),
            struct((count, rows, each), BF16),
            struct(got.shape, BF16),
        ),
        compiler_params=params(40, 1),
        name="cross_layer",
    )(got, hidden_zero, pack, text, gains[0][None], gains[1][None], head_gain[None])


def cross_layer_back(got, cot, hidden_one, hidden_two, pack, text, raw, mixed, gains, head_gain, text_count):
    count, rows, width = got.shape
    head = head_gain.shape[0]
    each = text.shape[2] // 2
    heads = each // head
    scaling = head ** (-0.5)
    slices, _, deep, _ = pack.shape

    def kernel(got_ref, cot_ref, h1_ref, h2_ref, pack_ref, text_ref, raw_ref, mixed_ref, g2_ref, g3_ref, hg_ref,
               res_ref, d2_ref, by_ref, out_ref, dg2_ref, dg3_ref, dhg_ref, acc_ref):
        step = pl.program_id(0)

        @pl.when(step == 0)
        def _():
            unit, scale = norm_parts(h2_ref[...])
            grad, dgain = norm_back(unit, scale, g3_ref[...], add_blocks(got_ref))
            dg3_ref[...] = dgain
            residual = cot_ref[...].astype(F32) + grad
            res_ref[...] = residual
            d2_ref[...] = residual.astype(BF16)
            acc_ref[...] = jnp.zeros_like(acc_ref)
            dhg_ref[...] = jnp.zeros_like(dhg_ref)

        weights = pack_ref[:, 0].reshape(slices * deep, width)
        by_ref[0, :, each : 2 * each] = mixed_ref[0]
        by_ref[0, :, 3 * each :] = dot_t(d2_ref[...], weights[:each]).astype(BF16)
        for h in range(heads):
            cut = slice(h * head, (h + 1) * head)
            vcut = slice(each + h * head, each + (h + 1) * head)
            unit, scale = norm_parts(raw_ref[0, :, cut])
            queries = (unit * hg_ref[...]).astype(BF16)
            by_ref[0, :, 2 * each + h * head : 2 * each + (h + 1) * head] = queries
            grads = by_ref[0, :, 3 * each + h * head : 3 * each + (h + 1) * head]
            keys_h = text_ref[0, :, cut]
            shares = text_scores(queries, keys_h, scaling, text_count)
            dshares = dot_t(grads, text_ref[0, :, vcut])
            weighted = jnp.sum(shares * dshares, -1, keepdims=True)
            dscores = (shares * (dshares - weighted) * scaling).astype(BF16)
            draw, dgain = norm_back(unit, scale, hg_ref[...], dot(dscores, keys_h))
            dhg_ref[...] += dgain
            by_ref[0, :, cut] = draw.astype(BF16)
        acc_ref[...] += dot(by_ref[0, :, :each], weights[each : 2 * each])

        @pl.when(step == count - 1)
        def _():
            unit, scale = norm_parts(h1_ref[...])
            grad, dgain = norm_back(unit, scale, g2_ref[...], acc_ref[...])
            dg2_ref[...] = dgain
            residual = res_ref[...] + grad
            res_ref[...] = residual
            rounded = residual.astype(BF16)
            for i in range(count):
                out_ref[i] = rounded

    one = lambda size: pl.BlockSpec((1, rows, size), lambda i: (i, 0, 0))
    return pl.pallas_call(
        kernel,
        grid=(count,),
        in_specs=[
            whole(got.shape),
            whole((rows, width)),
            whole((rows, width)),
            whole((rows, width)),
            pl.BlockSpec((slices, 1, deep, width), lambda i: (0, i, 0, 0)),
            pl.BlockSpec((1,) + text.shape[1:], lambda i: (i, 0, 0)),
            one(each),
            one(each),
            whole((1, width)),
            whole((1, width)),
            whole((1, head)),
        ],
        out_specs=(
            whole((rows, width)),
            whole((rows, width)),
            one(4 * each),
            whole(got.shape),
            whole((1, width)),
            whole((1, width)),
            whole((1, head)),
        ),
        out_shape=(
            struct((rows, width), F32),
            struct((rows, width), BF16),
            struct((count, rows, 4 * each), BF16),
            struct(got.shape, BF16),
            struct((1, width), F32),
            struct((1, width), F32),
            struct((1, head), F32),
        ),
        scratch_shapes=[pltpu.VMEM((rows, width), F32)],
        compiler_params=params(40, 1),
        name="cross_layer_back",
    )(got, cot, hidden_one, hidden_two, pack, text, raw, mixed, gains[0][None], gains[1][None], head_gain[None])


def text_back(by_head, text, head, text_count):
    tokens = by_head.shape[0]
    each = text.shape[1] // 2
    heads = each // head
    scaling = head ** (-0.5)

    def kernel(by_ref, text_ref, out_ref):
        for h in range(heads):
            cut = slice(h * head, (h + 1) * head)
            vcut = slice(each + h * head, each + (h + 1) * head)
            queries = by_ref[:, 2 * each + h * head : 2 * each + (h + 1) * head]
            grads = by_ref[:, 3 * each + h * head : 3 * each + (h + 1) * head]
            shares = text_scores(queries, text_ref[:, cut], scaling, text_count)
            dshares = dot_t(grads, text_ref[:, vcut])
            weighted = jnp.sum(shares * dshares, -1, keepdims=True)
            dscores = (shares * (dshares - weighted) * scaling).astype(BF16)
            out_ref[:, cut] = t_dot(dscores, queries).astype(BF16)
            out_ref[:, vcut] = t_dot(shares.astype(BF16), grads).astype(BF16)

    return pl.pallas_call(
        kernel,
        out_shape=struct(text.shape, BF16),
        compiler_params=params(40),
        name="text_back",
    )(by_head, text)


def last_norms(got, hidden_zero, merged, residual, gains, rows_two, rows_three, misc):
    count, rows, width = got.shape

    def kernel(got_ref, h0_ref, merged_ref, res_ref, g1_ref, gs_ref, two_ref, three_ref, misc_ref, out_ref):
        grad = add_blocks(got_ref)
        shift_grad = jnp.sum(grad, 0, keepdims=True)
        unit, scale = norm_parts(h0_ref[...])
        step, norm1_grad = norm_back(unit, scale, g1_ref[...], grad)
        residual = res_ref[...] + step
        unit, scale = norm_parts(merged_ref[...])
        step, skip_grad = norm_back(unit, scale, gs_ref[...], residual)
        small = [skip_grad, norm1_grad, two_ref[...], three_ref[...], shift_grad, misc_ref[...]]
        small = jnp.concatenate(small + [jnp.zeros((16 - len(small), width), F32)], 0).astype(BF16)
        step = step.astype(BF16)
        for i in range(count):
            out_ref[i, :rows] = step
            out_ref[i, rows:] = small

    return pl.pallas_call(
        kernel,
        out_shape=struct((count, rows + 16, width), BF16),
        compiler_params=params(32),
        name="last_norms",
    )(got, hidden_zero, merged, residual, gains[0][None], gains[1][None], rows_two, rows_three, misc)


def feed_forward(normed, cot, fc1_w, fc2_w):
    tokens, width = normed.shape
    hidden = fc1_w.shape[1]
    block = 256
    steps = hidden // block
    root = (2 / 3.141592653589793) ** 0.5

    def kernel(x_ref, cot_ref, w1_ref, w2_ref, active_ref, pre_ref, out_ref, acc_ref):
        step = pl.program_id(0)
        pre = dot(x_ref[...], w1_ref[...])
        square = pre * pre
        bent = jnp.tanh(root * pre * (1 + 0.044715 * square))
        half = 0.5 * (1 + bent)
        active_ref[...] = (pre * half).astype(BF16)
        slope = half + 0.5 * pre * (1 - bent * bent) * root * (1 + 3 * 0.044715 * square)
        pre_ref[...] = (dot_t(cot_ref[...], w2_ref[...]) * slope).astype(BF16)
        back = dot_t(pre_ref[...], w1_ref[...])

        @pl.when(step == 0)
        def _():
            acc_ref[...] = back

        @pl.when(step > 0)
        def _():
            acc_ref[...] += back

        @pl.when(step == steps - 1)
        def _():
            out_ref[...] = acc_ref[...].astype(BF16)

    return pl.pallas_call(
        kernel,
        grid=(steps,),
        in_specs=[
            whole(normed.shape),
            whole(cot.shape),
            pl.BlockSpec((width, block), lambda i: (0, i)),
            pl.BlockSpec((block, width), lambda i: (i, 0)),
        ],
        out_specs=(
            pl.BlockSpec((tokens, block), lambda i: (0, i)),
            pl.BlockSpec((tokens, block), lambda i: (0, i)),
            whole((tokens, width)),
        ),
        out_shape=(
            struct((tokens, hidden), BF16),
            struct((tokens, hidden), BF16),
            struct((tokens, width), BF16),
        ),
        scratch_shapes=[pltpu.VMEM((tokens, width), F32)],
        compiler_params=params(48, 1),
        name="feed_forward",
    )(normed, cot, fc1_w, fc2_w)


def local(
    latent,
    skip_input,
    text_tokens,
    condition,
    positions,
    cotangent,
    skip_w,
    skip_gain,
    norm1_gain,
    mod_w,
    qkv_w,
    qnorm_gain,
    knorm_gain,
    attn_out_w,
    norm2_gain,
    cq_w,
    ckv_w,
    cqnorm_gain,
    cknorm_gain,
    cross_out_w,
    norm3_gain,
    fc1_w,
    fc2_w,
):
    token_count, model_width = latent.shape
    head_dim = qnorm_gain.shape[0]
    local_width = cq_w.shape[1]
    local_heads = local_width // head_dim
    slab_width = skip_w.shape[0]
    hidden_width = fc1_w.shape[1]
    text_count, text_width = text_tokens.shape
    tensor_place = lax.axis_index("tensor")
    tensor_count = lax.axis_size("tensor")
    dp_count = lax.axis_size("dp")
    part_count = token_count // tensor_count
    blocks = (tensor_count, part_count, model_width)

    def own_rows(rows):
        return lax.dynamic_slice_in_dim(rows, tensor_place * part_count, part_count, 0)

    early_rows = 16 * dp_count * (-(-2 * local_width // (16 * dp_count))) - 2 * local_width
    cross_share = dp_slice(jnp.concatenate([cross_out_w, cq_w.T, skip_w[:early_rows]], 0), 16)
    cross_pack = lax.all_gather(permute_gather(cross_share), "dp", axis=0, tiled=False)
    skip_share = dp_slice(skip_w[early_rows:], 16)

    joined = jnp.concatenate([latent, skip_input], 1)
    joined_part = lax.dynamic_slice_in_dim(joined, tensor_place * slab_width, slab_width, 1)
    partial = jnp.dot(joined_part, skip_w, preferred_element_type=F32).astype(BF16)
    got = exchange(partial.reshape(blocks))
    silu_cond = jax.nn.silu(condition.astype(F32)).astype(BF16)
    shift = jnp.dot(silu_cond[None], mod_w, preferred_element_type=F32)[0]
    merged, hidden_zero, normed_out = first_norms(got, skip_gain, norm1_gain, shift)
    normed_one = exchange(normed_out).reshape(token_count, model_width)

    ckv_flat = ckv_w.reshape(text_width, 2 * local_width)
    text_proj = jnp.dot(text_tokens, ckv_flat, preferred_element_type=F32)
    text_proj = text_proj.reshape(text_count, 2, local_heads, head_dim)
    cross_key, cross_key_back = jax.vjp(layer_norm, text_proj[:, 0], cknorm_gain)
    text_pair = jnp.concatenate(
        [
            cross_key.astype(BF16).reshape(text_count, local_width),
            text_proj[:, 1].astype(BF16).reshape(text_count, local_width),
        ],
        1,
    )
    text_pair = pad_rows(text_pair, 16)
    text_pairs = exchange(spread(after(text_pair, normed_one)))

    qkv_flat = qkv_w.reshape(model_width, 3 * local_width)
    cos_wide, sin_wide = rotary_tables(positions, head_dim)
    raw, queries, own_pair = project(
        normed_one, qkv_flat, cos_wide, sin_wide, qnorm_gain, knorm_gain
    )
    other_pair = core_swap(own_pair)
    mixed_one, totals, partial = self_attention(
        queries, own_pair, other_pair, attn_out_w, head_dim
    )
    got = exchange(after(partial, text_pairs).reshape(blocks))
    cross_gains = (norm2_gain, norm3_gain)
    hidden_one, hidden_two, normed_two, cross_raw, mixed_two, normed_out = cross_layer(
        got, hidden_zero, cross_pack, text_pairs, cross_gains, cqnorm_gain, text_count
    )
    normed_three = exchange(normed_out).reshape(token_count, model_width)
    slow_rows = lax.all_gather(
        jnp.concatenate([after(normed_two, cross_pack), skip_share], 0), "tensor", axis=0, tiled=False
    )
    normed_two_all = slow_rows[:, :part_count].reshape(token_count, model_width)
    skip_pack = lax.all_gather(slow_rows[:, part_count:], "dp", axis=0, tiled=False)

    active, pre_grad, partial = feed_forward(normed_three, cotangent, fc1_w, fc2_w)
    got = exchange(partial.reshape(blocks))
    fc_grads = sum_dp(
        jnp.concatenate([left_product(pre_grad, normed_three), left_product(active, cotangent)], 0)
    )
    fc1_grad = fc_grads[:hidden_width].T.astype(F32)
    fc2_grad = fc_grads[hidden_width:].astype(F32)

    residual, out_grad_two, by_head, out_spread, norm2_grad, norm3_grad, cqnorm_grad = (
        cross_layer_back(
            got,
            own_rows(cotangent),
            hidden_one,
            hidden_two,
            cross_pack,
            text_pairs,
            cross_raw,
            mixed_two,
            cross_gains,
            cqnorm_gain,
            text_count,
        )
    )
    out_grad_one = exchange(out_spread).reshape(token_count, model_width)
    out_grad_two = lax.all_gather(out_grad_two, "tensor", axis=0, tiled=True)
    query_grad, own_grad, other_grad = self_attention_back(
        queries, own_pair, other_pair, totals, out_grad_one, attn_out_w, head_dim
    )
    arrived = core_swap(other_grad)
    projected_grad, partial, qnorm_grad, knorm_grad = project_back(
        raw,
        cos_wide,
        sin_wide,
        qnorm_gain,
        knorm_gain,
        query_grad,
        own_grad,
        arrived,
        qkv_flat,
    )
    got = exchange(partial.reshape(blocks))
    misc = jnp.concatenate([qnorm_grad, knorm_grad, cqnorm_grad], 1)
    misc = jnp.pad(misc, ((0, 0), (0, model_width - misc.shape[1])))
    merged_out = last_norms(
        got,
        hidden_zero,
        merged,
        residual,
        (norm1_gain, skip_gain),
        norm2_grad,
        norm3_grad,
        misc,
    )
    merged_small = exchange(merged_out)
    merged_grad = merged_small[:, :part_count].reshape(token_count, model_width)
    small = jnp.sum(merged_small[:, part_count:].astype(F32), 0)

    by_head = exchange(after(by_head, out_grad_one)).reshape(token_count, 4 * local_width)
    text_grads = text_back(by_head, text_pair, head_dim, text_count)
    late_grads = [
        left_product(projected_grad, normed_one),
        left_product(mixed_one, out_grad_one),
        left_product(by_head[:, :local_width], normed_two_all),
        left_product(by_head[:, local_width : 2 * local_width], out_grad_two),
        text_grads.reshape(-1, 8 * local_width),
    ]
    late_grads = sum_dp(pad_rows(jnp.concatenate(late_grads, 0), 16 * dp_count))
    qkv_rows = 3 * local_width
    qkv_grad = late_grads[:qkv_rows].T.astype(F32).reshape(model_width, 3, local_width)
    attn_out_grad, cq_grad, cross_out_grad = [
        late_grads[qkv_rows + i * local_width : qkv_rows + (i + 1) * local_width].astype(F32)
        for i in range(3)
    ]
    cq_grad = cq_grad.T
    text_rows = text_pair.shape[0] // 4
    text_grads = late_grads[qkv_rows + 3 * local_width :][:text_rows]
    text_grads = text_grads.reshape(-1, 2 * local_width)[:text_count].astype(F32)
    text_grads = text_grads.reshape(text_count, 2, local_heads, head_dim)

    skip_w_grad = left_product(joined_part, merged_grad)
    skip_small = sum_dp(pad_rows(jnp.concatenate([skip_w_grad, small], 0), 16 * dp_count))
    skip_w_grad = skip_small[:slab_width].astype(F32)
    small = skip_small[slab_width:].astype(F32)
    skip_gain_grad, norm1_grad, norm2_grad, norm3_grad, mod_vector = [small[i] for i in range(5)]
    qnorm_grad, knorm_grad, cqnorm_grad = [
        small[5, i * head_dim : (i + 1) * head_dim] for i in range(3)
    ]
    early_slices = early_rows // cross_share.shape[0]
    late_slices = (slab_width - early_rows) // skip_share.shape[0]
    skip_whole = jnp.concatenate(
        [
            pack.transpose(1, 0, 2, 3).reshape(tensor_count, -1, model_width)
            for pack in (cross_pack[-early_slices:], skip_pack[:late_slices])
        ],
        1,
    ).reshape(tensor_count * slab_width, model_width)
    latent_grad = right_product(merged_grad, skip_whole[:model_width])
    skip_grad = right_product(merged_grad, skip_whole[model_width:])

    key_raw_grad, cknorm_part = cross_key_back(text_grads[:, 0])
    text_proj_grad = (
        jnp.stack([key_raw_grad, text_grads[:, 1]], 1)
        .astype(BF16)
        .reshape(text_count, 2 * local_width)
    )
    ckv_grad = left_product(text_tokens, text_proj_grad).reshape(text_width, 2, local_width)
    text_part = right_product(text_proj_grad, ckv_flat)
    text_part = jnp.concatenate(
        [text_part, jnp.pad(cknorm_part, (0, text_width - head_dim))[None]], 0
    )
    text_part = pad_rows(text_part, 16 * tensor_count).astype(BF16)
    text_part = exchange(text_part.reshape(tensor_count, -1, text_width))
    text_part = jnp.sum(text_part.astype(F32), 0).astype(BF16)
    text_part = exchange(spread(text_part)).reshape(-1, text_width)
    text_grad = text_part[:text_count].astype(F32)
    cknorm_grad = text_part[text_count, :head_dim].astype(F32)

    partial = jnp.dot(active, fc2_w, preferred_element_type=F32).astype(BF16)
    got = exchange(after(partial, by_head).reshape(blocks))
    output = (hidden_two + jnp.sum(got.astype(F32), 0)).astype(BF16)
    output = lax.all_gather(output, "tensor", axis=0, tiled=True)
    mod_grad = silu_cond.astype(F32)[:, None] * mod_vector[None, :]
    return (
        output,
        latent_grad,
        skip_grad,
        text_grad,
        skip_w_grad,
        skip_gain_grad,
        norm1_grad,
        mod_grad,
        qkv_grad,
        qnorm_grad,
        knorm_grad,
        attn_out_grad,
        norm2_grad,
        cq_grad,
        ckv_grad,
        cqnorm_grad,
        cknorm_grad,
        cross_out_grad,
        norm3_grad,
        fc1_grad,
        fc2_grad,
    )


def solution(mesh):
    placed = (
        P("dp", None),
        P("dp", None),
        P(),
        P(),
        P("dp", None),
        P("dp", None),
        P("tensor", None),
        P(),
        P(),
        P(),
        P(None, None, "tensor"),
        P(),
        P(),
        P("tensor", None),
        P(),
        P(None, "tensor"),
        P(None, None, "tensor"),
        P(),
        P(),
        P("tensor", None),
        P(),
        P(None, "tensor"),
        P("tensor", None),
    )
    return jax.shard_map(
        local,
        mesh=mesh,
        in_specs=placed,
        out_specs=(
            P("dp", None),
            P("dp", None),
            P("dp", None),
            P(),
            P("tensor", None),
            P(),
            P(),
            P(),
            P(None, None, "tensor"),
            P(),
            P(),
            P("tensor", None),
            P(),
            P(None, "tensor"),
            P(None, None, "tensor"),
            P(),
            P(),
            P("tensor", None),
            P(),
            P(None, "tensor"),
            P("tensor", None),
        ),
        check_vma=False,
    )
```

time: 1080 us -> 634 us (0.59)
  waiting for transfers between devices: 694 us -> 214 us
  blocking collectives: 133 us -> 0 us
  starting transfers between devices: 11.1 us -> 122 us
  Pallas kernels: 0 us -> 77.6 us
  local copies, waits for them, and re-layouts: 36.5 us -> 114 us
  matrix products: 102 us -> 32 us
  other arithmetic: 75.7 us -> 48.5 us
    psum x8 -> x0, waiting for transfers between devices: 631 us -> none  [the longest x6 577 us: sum_rows(): return lax.psum(term_fn(0, token_count), 'tensor')]
    all_to_all x0 -> x13, waiting for transfers between devices: none -> 145 us  [exchange(): return lax.all_to_all(blocks, axis, 0, 0, tiled=True)]
    psum x3 -> x0, blocking collectives: 133 us -> none  [the longest x1 65.5 us: local(): lax.psum((qnorm_grad, knorm_grad, cqnorm_grad), ('dp', 'tensor'))]
    pallas_call x0 -> x10, Pallas kernels: none -> 77.6 us  [the longest x1 19.5 us: cross_layer_back(): pl.pallas_call(kernel, grid=(count,), in_specs=[whole(got.shape), whole((...]
    all_to_all x0 -> x13, starting transfers between devices: none -> 67.5 us  [exchange(): return lax.all_to_all(blocks, axis, 0, 0, tiled=True)]
    ppermute x2 -> x39, waiting for transfers between devices: 1.05 us -> 57.8 us  [the longest x15 33.2 us: spread_dp(): got = lax.ppermute(rows_all, 'dp', route)]
    dot_general x21 -> x4, matrix products: 63.4 us -> 7.95 us  [the longest x1 2.74 us: local(): shift = jnp.dot(silu_cond[None], mod_w, preferred_element_type=F32)[0]]
    all_gather x1 -> x5, waiting for transfers between devices: 61.8 us -> 10.1 us  [the longest x1 10 us: local(): lax.all_gather(permute_gather(cross_share), 'dp', axis=0, tiled=False)]
  transfers between devices with their start and end apart: 11 -> 57, of which waited for: 10 -> 27; matrix products, arithmetic and copies ran while one was open for 9% -> 22% of each run, Pallas kernels for 0% -> 10%
where the time goes in v1:
time: 634 us; the launch traced here: 623 us
  waiting for transfers between devices  214 us (34%)
  starting transfers between devices  122 us (19%)
  local copies, waits for them, and re-layouts  114 us (18%)
  Pallas kernels  77.6 us (12%)
  other arithmetic  48.5 us (8%)
  matrix products  32 us (5%)
  between operations  15.7 us (2%)
    all_to_all x13, waiting for transfers between devices, exchange(): return lax.all_to_all(blocks, axis, 0, 0, tiled=True)  145 us
    all_to_all x13, starting transfers between devices, exchange(): return lax.all_to_all(blocks, axis, 0, 0, tiled=True)  67.5 us
    unnamed x188, local copies, waits for them, and re-layouts  44.4 us
    ppermute x15, waiting for transfers between devices, spread_dp(): got = lax.ppermute(rows_all, 'dp', route)  33.2 us
    ppermute x15, waiting for transfers between devices, scatter_dp(): total = total + lax.ppermute(send.astype(BF16), 'dp', route).astype(F32)  22.1 us
    pallas_call x1, Pallas kernels, cross_layer_back(): pl.pallas_call(kernel, grid=(count,), in_specs=[whole(got.shape), whole((...  19.5 us
    ppermute x15, starting transfers between devices, scatter_dp(): total = total + lax.ppermute(send.astype(BF16), 'dp', route).astype(F32)  19.1 us
    pallas_call x1, Pallas kernels, cross_layer(): pl.pallas_call(kernel, grid=(count,), in_specs=[whole(got.shape), whole((...  17.2 us
  transfers between devices with their start and end apart: 57, of which 27 were waited for; matrix products, arithmetic and copies ran while one was open for 22% of the time, Pallas kernels for 10%

profile of v1, /device:TPU:1, one launch (start us, length us, event | category | flops | bytes accessed | tf_op | source)
XLA Modules:
  0.0 623.1 jit_solution(3863603205919344877)
XLA Ops:
  44.5 17.9 %all-to-all-done.got_ref = bf16[8,64,1408]{2,1,0:T(8,128)(2,1)S(1)} async-done(((bf16[8,64,1408]{2,1,0:T(8,128)(2,1)}), bf16[8,64,1408]{2,1,0:T(8,128)(2,1)S(1)}, u32[]{:S(2)}, u32[]{:S(2)}) %all-to-all-start) | async-done | bytes 1441824 | tf_op jit(solution)/shard_map/all_to_all | solution.py:41
  75.4 17.9 %all-to-all-done.1 = bf16[8,64,1408]{2,1,0:T(8,128)(2,1)S(1)} async-done(((bf16[8,64,1408]{2,1,0:T(8,128)(2,1)}), bf16[8,64,1408]{2,1,0:T(8,128)(2,1)S(1)}, u32[]{:S(2)}, u32[]{:S(2)}) %all-to-all-start.1) | async-done | bytes 1441824 | tf_op jit(solution)/shard_map/all_to_all | solution.py:41
  108.8 5.8 project.1
  136.1 22.8 %all-to-all-done.3.got_ref = bf16[8,64,1408]{2,1,0:T(8,128)(2,1)} async-done(((bf16[8,64,1408]{2,1,0:T(8,128)(2,1)}), bf16[8,64,1408]{2,1,0:T(8,128)(2,1)}, u32[]{:S(2)}, u32[]{:S(2)}) %all-to-all-start.3) | async-done | bytes 1441824 | tf_op jit(solution)/shard_map/all_to_all | solution.py:41
  158.9 10.0 %all-gather.8.cloned.1.call-done.pack_ref = bf16[16,8,32,1408]{3,2,1,0:T(8,128)(2,1)} async-done(((bf16[1,8,32,1408]{3,2,1,0:T(8,128)(2,1)}), bf16[16,8,32,1408]{3,2,1,0:T(8,128)(2,1)}) %all-gather.8.cloned.1.call-update) | async-done | bytes 11534352 | tf_op jit(solution)/shard_map/all_gather | solution.py:736
  169.9 17.2 %cross_layer.1 = (f32[64,1408]{1,0:T(8,128)S(1)}, f32[64,1408]{1,0:T(8,128)S(1)}, bf16[64,1408]{1,0:T(8,128)(2,1)S(1)}, f32[8,64,176]{2,1,0:T(8,128)S(1)}, bf16[...) custom-call(bf16[8,64,1408]{2,1,0:T(8,128)(2,1)} %all-to-all-done.3.got_ref, f32[64,1408]{1,0:T(8,128)S(1)} %copy-done.24, ...), custom_call_target="tpu_custom_call" | custom-call | tf_op jit(solution)/shard_map/cross_layer/pallas_call | solution.py:457
  191.2 6.1 all-to-all-start.4
  200.7 18.2 %all-to-all-done.4 = bf16[8,64,1408]{2,1,0:T(8,128)(2,1)} async-done(((bf16[8,64,1408]{2,1,0:T(8,128)(2,1)}), bf16[8,64,1408]{2,1,0:T(8,128)(2,1)}, u32[]{:S(2)}, u32[]{:S(2)}) %all-to-all-start.4) | async-done | bytes 1441824 | tf_op jit(solution)/shard_map/all_to_all | solution.py:41
  220.3 7.7 %feed_forward.1 = (bf16[512,768]{1,0:T(8,128)(2,1)S(1)}, bf16[512,768]{1,0:T(8,128)(2,1)S(1)}, bf16[512,1408]{1,0:T(8,128)(2,1)S(1)}) custom-call(bf16[512,1408]{1,0:T(8,128)(2,1)} %bitcast.26.x_ref, bf16[512,1408]{1,0:T(8,128)(2,1)S(1)} %copy-done.3, bf16[1408,768]{1,0:T(8,128)(2,1)} %w1_ref.1, bf16[768,1408]{1,0:T(8,128)(2,1)} %w2_ref.1), custom_call_target="tpu_custom_call" | custom-call | tf_op jit(solution)/shard_map/feed_forward/pallas_call | solution.py:668
  243.4 24.0 %all-to-all-done.5.got_ref = bf16[8,64,1408]{2,1,0:T(8,128)(2,1)} async-done(((bf16[8,64,1408]{2,1,0:T(8,128)(2,1)}), bf16[8,64,1408]{2,1,0:T(8,128)(2,1)}, u32[]{:S(2)}, u32[]{:S(2)}) %all-to-all-start.5) | async-done | bytes 1441824 | tf_op jit(solution)/shard_map/all_to_all | solution.py:41
  271.4 19.5 %cross_layer_back.1 = (f32[64,1408]{1,0:T(8,128)S(1)}, bf16[64,1408]{1,0:T(8,128)(2,1)}, bf16[8,64,704]{2,1,0:T(8,128)(2,1)S(1)}, bf16[8,64,1408]{2,1,0:T(8,128)...) custom-call(bf16[8,64,1408]{2,1,0:T(8,128)(2,1)} %all-to-all-done.5.got_ref, ...), custom_call_target="tpu_custom_call" | custom-call | tf_op jit(solution)/shard_map/cross_layer_back/pallas_call | solution.py:545
  298.6 6.6 %fusion.3 = f32[768,1408]{1,0:T(8,128)} fusion(s32[]{:T(128)S(6)} %select_n.364, f32[768,1408]{1,0:T(8,128)} %copy-done.51, f32[768,1408]{1,0:T(8,128)} %copy-done.52, bf16[768,1408]{1,0:T(8,128)(2,1)} %collective-permute-done.29), kind=kLoop, calls=%fused_computation.11 | loop fusion | flops 3244032 | bytes 15138820 | tf_op jit(solution)/shard_map/add | solution.py:100
  305.2 14.2 %all-to-all-done.6 = bf16[8,64,1408]{2,1,0:T(8,128)(2,1)S(1)} async-done(((bf16[8,64,1408]{2,1,0:T(8,128)(2,1)}), bf16[8,64,1408]{2,1,0:T(8,128)(2,1)S(1)}, u32[]{:S(2)}, u32[]{:S(2)}) %all-to-all-start.6) | async-done | bytes 1441824 | tf_op jit(solution)/shard_map/all_to_all | solution.py:41
  345.0 6.6 %self_attention_back.1 = (f32[512,176]{1,0:T(8,128)S(1)}, f32[512,352]{1,0:T(8,128)S(1)}, bf16[512,352]{1,0:T(8,128)(2,1)S(1)}) custom-call(bf16[512,176]{1,0:T(8,128)(2,1)S(1)} %copy-done.27, bf16[512,352]{1,0:T(8,128)(2,1)S(1)} %copy-done.11, bf16[512,352]{1,0:T(8,128)(2,1)S(1)} %copy-done.13, f32[512,2]{1,0:T(8,128)S(1)} %copy-done.44, ...), custom_call_target="tpu_custom_call" | custom-call | tf_op jit(solution)/shard_map/self_attention_back/pallas_call | solution.py:329
  357.0 10.3 %project_back.1 = (bf16[512,528]{1,0:T(8,128)(2,1)S(1)}, bf16[512,1408]{1,0:T(8,128)(2,1)S(1)}, f32[1,88]{1,0:T(1,128)S(1)}, f32[1,88]{1,0:T(1,128)S(1)}) custom-call(f32[512,352]{1,0:T(8,128)S(1)} %copy-done.32, f32[512,88]{1,0:T(8,128)S(1)} %copy.94.cos_ref, f32[512,88]{1,0:T(8,128)S(1)} %copy.95.sin_ref, f32[1,88]{1,0:T(1,128)S(1)} %bitcast.148, ...), custom_call_target="tpu_custom_call" | custom-call | tf_op jit(solution)/shard_map/project_back/pallas_call | solution.py:386
  369.2 6.4 %all-to-all-start.9 = ((bf16[8,64,1408]{2,1,0:T(8,128)(2,1)}), bf16[8,64,1408]{2,1,0:T(8,128)(2,1)}, u32[]{:S(2)}, u32[]{:S(2)}) async-start(bf16[8,64,1408]{2,1,0:T(8,128)(2,1)} %bitcast.142), calls=%async_computation.9 | async-start | bytes 2883584 | tf_op jit(solution)/shard_map/all_to_all | solution.py:41
  422.8 8.6 %all-to-all-start.10 = ((bf16[8,80,1408]{2,1,0:T(8,128)(2,1)}), bf16[8,80,1408]{2,1,0:T(8,128)(2,1)}, u32[]{:S(2)}, u32[]{:S(2)}) async-start(bf16[8,80,1408]{2,1,0:T(8,128)(2,1)} %last_norms.1), calls=%async_computation.10 | async-start | bytes 3604480 | tf_op jit(solution)/shard_map/all_to_all | solution.py:41
  467.1 6.3 %slice_convert_fusion = (f32[768,1408]{1,0:T(8,128)}, f32[1408,768]{0,1:T(8,128)}) fusion(bf16[1536,1408]{1,0:T(8,128)(2,1)} %constant_dynamic-update-slice_fusion), kind=kLoop, calls=%fused_computation.29 | loop fusion | flops 2162688 | bytes 12976128 | tf_op jit(solution)/shard_map/convert_element_type | solution.py:789
  479.2 15.0 %collective-permute-done.11 = bf16[160,1408]{1,0:T(8,128)(2,1)} collective-permute-done((bf16[160,1408]{1,0:T(8,128)(2,1)S(1)}, bf16[160,1408]{1,0:T(8,128)(2,1)}, u32[]{:S(2)}, u32[]{:S(2)}) %collective-permute-start.11) | collective-permute-done | bytes 450592 | tf_op jit(solution)/shard_map/ppermute | solution.py:100
  518.8 16.3 %collective-permute-done.15 = bf16[160,1408]{1,0:T(8,128)(2,1)S(1)} collective-permute-done((bf16[160,1408]{1,0:T(8,128)(2,1)S(1)}, bf16[160,1408]{1,0:T(8,128)(2,1)S(1)}, u32[]{:S(2)}, u32[]{:S(2)}) %collective-permute-start.15) | collective-permute-done | bytes 450592 | tf_op jit(solution)/shard_map/ppermute | solution.py:112
  535.2 6.3 %collective-permute-done.25 = bf16[64,1408]{1,0:T(8,128)(2,1)S(1)} collective-permute-done((bf16[64,1408]{1,0:T(8,128)(2,1)S(1)}, bf16[64,1408]{1,0:T(8,128)(2,1)S(1)}, u32[]{:S(2)}, u32[]{:S(2)}) %collective-permute-start.25) | collective-permute-done | bytes 180256 | tf_op jit(solution)/shard_map/ppermute | solution.py:112
  559.2 6.2 all-to-all-start.11
  569.0 11.0 %all-to-all-done.11 = bf16[8,48,1024]{2,1,0:T(8,128)(2,1)S(1)} async-done(((bf16[8,48,1024]{2,1,0:T(8,128)(2,1)}), bf16[8,48,1024]{2,1,0:T(8,128)(2,1)S(1)}, u32[]{:S(2)}, u32[]{:S(2)}) %all-to-all-start.11) | async-done | bytes 786464 | tf_op jit(solution)/shard_map/all_to_all | solution.py:41
  589.7 9.7 %all-to-all-done.12 = bf16[8,48,1024]{2,1,0:T(8,128)(2,1)S(1)} async-done(((bf16[8,48,1024]{2,1,0:T(8,128)(2,1)}), bf16[8,48,1024]{2,1,0:T(8,128)(2,1)S(1)}, u32[]{:S(2)}, u32[]{:S(2)}) %all-to-all-start.12) | async-done | bytes 786464 | tf_op jit(solution)/shard_map/all_to_all | solution.py:41
  (442 shorter events, 316.9 us)
Async XLA Ops:
  7.2 161.7 %all-gather.8.cloned.1.call-start = ((), (), s32[]{:S(2)}) async-start(), calls=%async_computation.13 | async-start | bytes 12255232 | tf_op jit(solution)/shard_map/all_gather | solution.py:736
  36.2 26.3 %all-to-all-start = ((bf16[8,64,1408]{2,1,0:T(8,128)(2,1)}), bf16[8,64,1408]{2,1,0:T(8,128)(2,1)S(1)}, u32[]{:S(2)}, u32[]{:S(2)}) async-start(bf16[8,64,1408]{2,1,0:T(8,128)(2,1)} %bitcast.160), calls=%async_computation | async-start | bytes 2883584 | tf_op jit(solution)/shard_map/all_to_all | solution.py:41
  65.6 27.6 %all-to-all-start.1 = ((bf16[8,64,1408]{2,1,0:T(8,128)(2,1)}), bf16[8,64,1408]{2,1,0:T(8,128)(2,1)S(1)}, u32[]{:S(2)}, u32[]{:S(2)}) async-start(bf16[8,64,1408]{2,1,0:T(8,128)(2,1)} %copy-done.17), calls=%async_computation.1 | async-start | bytes 2883584 | tf_op jit(solution)/shard_map/all_to_all | solution.py:41
  95.0 36.0 %all-to-all-start.2 = ((bf16[8,336,352]{2,1,0:T(8,128)(2,1)}), bf16[8,336,352]{2,1,0:T(8,128)(2,1)S(1)}, u32[]{:S(2)}, u32[]{:S(2)}) async-start(bf16[8,336,352]{2,1,0:T(8,128)(2,1)} %broadcast_in_dim.100), calls=%async_computation.2 | async-start | bytes 4128768 | tf_op jit(solution)/shard_map/all_to_all | solution.py:41
  131.0 27.9 %all-to-all-start.3 = ((bf16[8,64,1408]{2,1,0:T(8,128)(2,1)}), bf16[8,64,1408]{2,1,0:T(8,128)(2,1)}, u32[]{:S(2)}, u32[]{:S(2)}) async-start(bf16[8,64,1408]{2,1,0:T(8,128)(2,1)} %bitcast.144), calls=%async_computation.3 | async-start | bytes 2883584 | tf_op jit(solution)/shard_map/all_to_all | solution.py:41
  191.2 27.8 %all-to-all-start.4 = ((bf16[8,64,1408]{2,1,0:T(8,128)(2,1)}), bf16[8,64,1408]{2,1,0:T(8,128)(2,1)}, u32[]{:S(2)}, u32[]{:S(2)}) async-start(bf16[8,64,1408]{2,1,0:T(8,128)(2,1)} %copy-done.16), calls=%async_computation.4 | async-start | bytes 2883584 | tf_op jit(solution)/shard_map/all_to_all | solution.py:41
  197.2 145.0 %all-gather.14.cloned.1.call-start = ((), (), s32[]{:S(2)}) async-start(), calls=%async_computation.16 | async-start | bytes 2027520 | tf_op jit(solution)/shard_map/all_gather | solution.py:777
  236.5 62.1 %collective-permute-start.29 = (bf16[768,1408]{1,0:T(8,128)(2,1)}, bf16[768,1408]{1,0:T(8,128)(2,1)}, u32[]{:S(2)}, u32[]{:S(2)}) collective-permute-start(bf16[768,1408]{1,0:T(8,128)(2,1)} %fusion.1), channel_id=1, source_target_pairs={{0,8},{8,0},{16,24},{24,16},{32,40},{40,32},{48,56},{56,48},{64,72... | collective-permute-start | bytes 6488072 | tf_op jit(solution)/shard_map/ppermute | solution.py:100
  238.2 29.3 %all-to-all-start.5 = ((bf16[8,64,1408]{2,1,0:T(8,128)(2,1)}), bf16[8,64,1408]{2,1,0:T(8,128)(2,1)}, u32[]{:S(2)}, u32[]{:S(2)}) async-start(bf16[8,64,1408]{2,1,0:T(8,128)(2,1)} %bitcast.143), calls=%async_computation.5 | async-start | bytes 2883584 | tf_op jit(solution)/shard_map/all_to_all | solution.py:41
  297.9 92.8 %all-gather.12.cloned.1.call-start = ((), (), s32[]{:S(2)}) async-start(), calls=%async_computation.15 | async-start | bytes 1622016 | tf_op jit(solution)/shard_map/all_gather | solution.py:807
  326.7 26.3 %collective-permute-start.30 = (bf16[192,1408]{1,0:T(8,128)(2,1)}, bf16[192,1408]{1,0:T(8,128)(2,1)}, u32[]{:S(2)}, u32[]{:S(2)}) collective-permute-start(bf16[192,1408]{1,0:T(8,128)(2,1)} %get-tuple-element.221), channel_id=1, source_target_pairs={{0,16},{8,24},{16,32},{24,40},{32,48},{40,56},{48,0},{56,8},{64,80... | collective-permute-start | bytes 1622024 | tf_op jit(solution)/shard_map/ppermute | solution.py:100
  326.7 26.3 %collective-permute-start.32 = (bf16[192,1408]{1,0:T(8,128)(2,1)}, bf16[192,1408]{1,0:T(8,128)(2,1)}, u32[]{:S(2)}, u32[]{:S(2)}) collective-permute-start(bf16[192,1408]{1,0:T(8,128)(2,1)} %get-tuple-element.222), channel_id=1, source_target_pairs={{0,48},{8,56},{16,0},{24,8},{32,16},{40,24},{48,32},{56,40},{64,11... | collective-permute-start | bytes 1622024 | tf_op jit(solution)/shard_map/ppermute | solution.py:100
  337.8 31.4 %all-to-all-start.8 = ((bf16[8,64,1408]{2,1,0:T(8,128)(2,1)}), bf16[8,64,1408]{2,1,0:T(8,128)(2,1)}, u32[]{:S(2)}, u32[]{:S(2)}) async-start(bf16[8,64,1408]{2,1,0:T(8,128)(2,1)} %bitcast.173), calls=%async_computation.8 | async-start | bytes 2883584 | tf_op jit(solution)/shard_map/all_to_all | solution.py:41
  369.2 50.2 %all-to-all-start.9 = ((bf16[8,64,1408]{2,1,0:T(8,128)(2,1)}), bf16[8,64,1408]{2,1,0:T(8,128)(2,1)}, u32[]{:S(2)}, u32[]{:S(2)}) async-start(bf16[8,64,1408]{2,1,0:T(8,128)(2,1)} %bitcast.142), calls=%async_computation.9 | async-start | bytes 2883584 | tf_op jit(solution)/shard_map/all_to_all | solution.py:41
  375.7 168.0 %all-gather.10.cloned.1.call-start = ((), (), s32[]{:S(2)}) async-start(), calls=%async_computation.14 | async-start | bytes 1622016 | tf_op jit(solution)/shard_map/all_gather | solution.py:903
  378.1 223.1 %all-gather.16.cloned.1.call-start = ((), (), s32[]{:S(2)}) async-start(), calls=%async_computation.17 | async-start | bytes 6127616 | tf_op jit(solution)/shard_map/all_gather | solution.py:781
  398.3 47.7 %collective-permute-start.9 = (bf16[640,1408]{1,0:T(8,128)(2,1)}, bf16[640,1408]{1,0:T(8,128)(2,1)}, u32[]{:S(2)}, u32[]{:S(2)}) collective-permute-start(bf16[640,1408]{1,0:T(8,128)(2,1)} %fusion.6), channel_id=1, source_target_pairs={{0,8},{8,0},{16,24},{24,16},{32,40},{40,32},{48,56},{56,48},{64,72... | collective-permute-start | bytes 5406728 | tf_op jit(solution)/shard_map/ppermute | solution.py:100
  422.8 34.1 %all-to-all-start.10 = ((bf16[8,80,1408]{2,1,0:T(8,128)(2,1)}), bf16[8,80,1408]{2,1,0:T(8,128)(2,1)}, u32[]{:S(2)}, u32[]{:S(2)}) async-start(bf16[8,80,1408]{2,1,0:T(8,128)(2,1)} %last_norms.1), calls=%async_computation.10 | async-start | bytes 3604480 | tf_op jit(solution)/shard_map/all_to_all | solution.py:41
  450.8 28.4 %collective-permute-start.10 = (bf16[160,1408]{1,0:T(8,128)(2,1)}, bf16[160,1408]{1,0:T(8,128)(2,1)S(1)}, u32[]{:S(2)}, u32[]{:S(2)}) collective-permute-start(bf16[160,1408]{1,0:T(8,128)(2,1)} %get-tuple-element.227), channel_id=1, source_target_pairs={{0,16},{8,24},{16,32},{24,40},{32,48},{40,56},{48,0},{56,8},{64,80... | collective-permute-start | bytes 1351688 | tf_op jit(solution)/shard_map/ppermute | solution.py:100
  451.3 27.9 %collective-permute-start.12 = (bf16[160,1408]{1,0:T(8,128)(2,1)S(1)}, bf16[160,1408]{1,0:T(8,128)(2,1)}, u32[]{:S(2)}, u32[]{:S(2)}) collective-permute-start(bf16[160,1408]{1,0:T(8,128)(2,1)S(1)} %get-tuple-element.228), channel_id=1, source_target_pairs={{0,48},{8,56},{16,0},{24,8},{32,16},{40,24},{48,32},{56,40},{64,11... | collective-permute-start | bytes 1351688 | tf_op jit(solution)/shard_map/ppermute | solution.py:100
  453.5 40.7 %collective-permute-start.11 = (bf16[160,1408]{1,0:T(8,128)(2,1)S(1)}, bf16[160,1408]{1,0:T(8,128)(2,1)}, u32[]{:S(2)}, u32[]{:S(2)}) collective-permute-start(bf16[160,1408]{1,0:T(8,128)(2,1)S(1)} %get-tuple-element.229), channel_id=1, source_target_pairs={{0,32},{8,40},{16,48},{24,56},{32,0},{40,8},{48,16},{56,24},{64,96... | collective-permute-start | bytes 1351688 | tf_op jit(solution)/shard_map/ppermute | solution.py:100
  462.8 33.5 %collective-permute-start.19 = (bf16[256,1408]{1,0:T(8,128)(2,1)S(1)}, bf16[256,1408]{1,0:T(8,128)(2,1)S(1)}, u32[]{:S(2)}, u32[]{:S(2)}) collective-permute-start(bf16[256,1408]{1,0:T(8,128)(2,1)S(1)} %dynamic-slice_convert_fusion), channel_id=1, source_target_pairs={{0,8},{8,0},{16,24},{24,16},{32,40},{40,32},{48,56},{56,48},{64,72... | collective-permute-start | bytes 2162696 | tf_op jit(solution)/shard_map/ppermute | solution.py:100
  507.0 36.5 %collective-permute-start.17 = (bf16[160,1408]{1,0:T(8,128)(2,1)S(1)}, bf16[160,1408]{1,0:T(8,128)(2,1)S(1)}, u32[]{:S(2)}, u32[]{:S(2)}) collective-permute-start(bf16[160,1408]{1,0:T(8,128)(2,1)S(1)} %constant_dynamic-update-slice_fusion.22), channel_id=1, source_target_pairs={{0,48},{8,56},{16,0},{24,8},{32,16},{40,24},{48,32},{56,40},{64,11... | collective-permute-start | bytes 1351688 | tf_op jit(solution)/shard_map/ppermute | solution.py:112
  514.9 26.7 %collective-permute-start.27 = (bf16[64,1408]{1,0:T(8,128)(2,1)S(1)}, bf16[64,1408]{1,0:T(8,128)(2,1)S(1)}, u32[]{:S(2)}, u32[]{:S(2)}) collective-permute-start(bf16[64,1408]{1,0:T(8,128)(2,1)S(1)} %constant_dynamic-update-slice_fusion.14), channel_id=1, source_target_pairs={{0,48},{8,56},{16,0},{24,8},{32,16},{40,24},{48,32},{56,40},{64,11... | collective-permute-start | bytes 540680 | tf_op jit(solution)/shard_map/ppermute | solution.py:112
  (127 other events, 977.1 us)
Sparse Core Ops, SparseCore 0:
  34.1 134.7 all-gather.7
  200.8 61.4 all-gather.13
  301.0 70.5 all-gather.11
  378.5 53.6 all-gather.9
  433.7 66.6 all-gather.15

commit v2 on v0

v2 whole, which is shorter than its diff:
```python
import jax
import jax.numpy as jnp
from jax import lax
from jax.experimental import pallas as pl
from jax.experimental.pallas import tpu as pltpu
from jax.sharding import PartitionSpec as P

BF16 = jnp.bfloat16
F32 = jnp.float32


def layer_norm(inputs, norm_gain):
    centered = inputs - jnp.mean(inputs, -1, keepdims=True)
    variance = jnp.mean(centered * centered, -1, keepdims=True)
    return centered * lax.rsqrt(variance + 1e-06) * norm_gain


def rotary_tables(positions, head_dim):
    quarter = head_dim // 4
    frequency = 10000.0 ** (-jnp.arange(quarter).astype(F32) / quarter)
    angles = positions.astype(F32)[:, :, None] * frequency
    cosine, sine = jnp.cos(angles), jnp.sin(angles)
    cos_wide = jnp.stack([cosine, cosine], 2).reshape(positions.shape[0], head_dim)
    sin_wide = jnp.stack([-sine, sine], 2).reshape(positions.shape[0], head_dim)
    return cos_wide, sin_wide


def left_product(inputs, grads):
    return lax.dot_general(
        inputs, grads, (((0,), (0,)), ((), ())), preferred_element_type=jnp.float32
    )


def right_product(grads, weight):
    return lax.dot_general(
        grads, weight, (((1,), (1,)), ((), ())), preferred_element_type=jnp.float32
    )


def exchange(blocks, axis="tensor"):
    return lax.all_to_all(blocks, axis, 0, 0, tiled=True)


def spread(block, axis="tensor"):
    count = lax.axis_size(axis)
    return jnp.broadcast_to(block[None], (count,) + block.shape)


def after(value, *earlier):
    return lax.optimization_barrier((value,) + earlier)[0]


def after_all(values, *earlier):
    return lax.optimization_barrier((tuple(values),) + earlier)[0]


def pad_rows(rows, multiple):
    extra = -rows.shape[0] % multiple
    return jnp.pad(rows, ((0, extra),) + ((0, 0),) * (rows.ndim - 1))


def ring_route(step):
    count = lax.axis_size("tensor")
    ring = count // 2
    return [(i, i // ring * ring + (i + step) % ring) for i in range(count)]


def ring_gather(block):
    ring = lax.axis_size("tensor") // 2
    got = {k: lax.ppermute(block, "tensor", ring_route(k)) for k in (1, 3, 2)}
    return [block] + [got[k] for k in range(1, ring)]


def ring_scatter(blocks):
    got = {k: lax.ppermute(blocks[k], "tensor", ring_route(-k)) for k in (1, 3, 2)}
    return [blocks[0]] + [got[k] for k in range(1, len(blocks))]


def place_blocks(blocks, half_blocks):
    ring = len(blocks)
    place = lax.axis_index("tensor")
    ring_place, half = place % ring, place // ring
    rows = blocks[0].shape[0]
    out = jnp.zeros((2 * ring * rows,) + blocks[0].shape[1:], blocks[0].dtype)
    for k in range(ring):
        at_ring = (ring_place - k) % ring
        for which, block in ((half, blocks[k]), (1 - half, half_blocks[k])):
            out = lax.dynamic_update_slice_in_dim(out, block, (which * ring + at_ring) * rows, 0)
    return out


def half_swap(block):
    count = lax.axis_size("tensor")
    return lax.ppermute(block, "tensor", [(i, (i + count // 2) % count) for i in range(count)])


def core_swap(block):
    count = lax.axis_size("dp")
    return lax.ppermute(block, "dp", [(i, i ^ 1) for i in range(count)])


def dp_slice(rows, unit):
    places = lax.axis_size("dp")
    each = -(-rows.shape[0] // (places * unit)) * unit
    rows = pad_rows(rows, each * places)
    return lax.dynamic_slice_in_dim(rows, lax.axis_index("dp") * each, each, 0)


def dp_routes():
    count = lax.axis_size("dp")
    place = lax.axis_index("dp")
    stages = []
    for low, size in ((0, 2), (1, 4), (3, 2)):
        part = place // (1 << low) % size
        routes = []
        for step in range(1, size):
            route = []
            for source in range(count):
                here = source // (1 << low) % size
                there = (here + step) % size
                route.append((source, source + ((there - here) << low)))
            routes.append(route)
        stages.append((size, part, routes))
    return stages


def join(*values):
    return lax.optimization_barrier(values)


def far_swap(block):
    dp_count, count = lax.axis_size("dp"), lax.axis_size("tensor")
    route = [
        (d * count + t, (d ^ 1) * count + (t + count // 2) % count)
        for d in range(dp_count)
        for t in range(count)
    ]
    return lax.ppermute(block, ("dp", "tensor"), route)


def low_swap(block):
    count = lax.axis_size("dp")
    return lax.ppermute(block, "dp", [(i, i ^ 8) for i in range(count)])


def low_groups():
    return [list(range(8)), list(range(8, 16))]


def scatter_low(rows):
    return lax.psum_scatter(
        rows, "dp", scatter_dimension=0, tiled=True, axis_index_groups=low_groups()
    )


def gather_low(rows):
    return lax.all_gather(rows, "dp", axis=0, tiled=False, axis_index_groups=low_groups())


def scatter_stage(stage, grads):
    size, part, routes = dp_routes()[stage]
    rows = grads.shape[1] // size
    cut = lambda place: lax.dynamic_slice_in_dim(grads, place * rows, rows, 1)
    total = cut(part).astype(F32)
    for step, route in enumerate(routes, 1):
        send = cut((part + step) % size).astype(BF16)
        total = total + lax.ppermute(send, "dp", route).astype(F32)
    return total


def half_sum(own, other):
    return own.astype(F32) + half_swap(other.astype(BF16)).astype(F32)


VMEM_LIMIT = 60 * 1024 * 1024


def cost(micros):
    return pl.CostEstimate(flops=0, transcendentals=0, bytes_accessed=int(micros * 3.3e6))


def call(kernel, micros, outs, ins, name, grid=None, in_specs=None, out_specs=None, scratch=()):
    extra = {}
    if grid:
        extra = {"grid": grid, "in_specs": in_specs, "out_specs": out_specs}
    return pl.pallas_call(
        kernel,
        out_shape=outs,
        scratch_shapes=scratch,
        compiler_params=pltpu.CompilerParams(
            vmem_limit_bytes=VMEM_LIMIT,
            dimension_semantics=("arbitrary",) * len(grid) if grid else None,
        ),
        cost_estimate=cost(micros),
        name=name,
        **extra,
    )(*ins)


def dot(left, right):
    return lax.dot_general(left, right, (((1,), (0,)), ((), ())), preferred_element_type=F32)


def dot_t(left, right):
    return lax.dot_general(left, right, (((1,), (1,)), ((), ())), preferred_element_type=F32)


def t_dot(left, right):
    return lax.dot_general(left, right, (((0,), (0,)), ((), ())), preferred_element_type=F32)


def norm_parts(rows):
    centered = rows - jnp.mean(rows, -1, keepdims=True)
    scale = lax.rsqrt(jnp.mean(centered * centered, -1, keepdims=True) + 1e-06)
    return centered * scale, scale


def norm_back(unit, scale, gain, grad):
    weighted = grad * gain
    rows = scale * (
        weighted
        - jnp.mean(weighted, -1, keepdims=True)
        - unit * jnp.mean(weighted * unit, -1, keepdims=True)
    )
    return rows, jnp.sum(grad * unit, 0, keepdims=True)


def add_all(refs):
    total = refs[0][...].astype(F32)
    for ref in refs[1:]:
        total = total + ref[...].astype(F32)
    return total


def stack(parts):
    return jnp.concatenate(parts, 0)


HBM = pl.BlockSpec(memory_space=pltpu.HBM)


def load_blocks(refs, x_ref, sems):
    rows = x_ref.shape[0] // len(refs)
    copies = [
        pltpu.make_async_copy(
            ref.at[pl.ds(0, rows)], x_ref.at[pl.ds(i * rows, rows)], sems.at[i]
        )
        for i, ref in enumerate(refs)
    ]
    for copy in copies:
        copy.start()
    for copy in copies:
        copy.wait()


def put_blocks(refs, value):
    rows = refs[0].shape[0]
    for i, ref in enumerate(refs):
        ref[...] = value[i * rows : (i + 1) * rows].astype(BF16)


def struct(shape, kind):
    return jax.ShapeDtypeStruct(shape, kind)


def whole(shape):
    return pl.BlockSpec(shape, lambda *place: (0,) * len(shape))


def at(shape, row):
    return pl.BlockSpec(shape, lambda *place: (row,) + (0,) * (len(shape) - 1))


def swap(rows):
    quarter = rows.shape[1] // 4
    cut = [rows[:, i * quarter : (i + 1) * quarter] for i in range(4)]
    return jnp.concatenate([cut[1], cut[0], cut[3], cut[2]], 1)


def pack_spec(rows, width, place, share=16):
    return pl.BlockSpec((rows // share, share, width), lambda *step: (0, place // share, 0))


def pack_rows(pack_ref):
    return pack_ref[...].reshape(-1, pack_ref.shape[2])


def first_norms(got, skip_gain, norm1_gain, shift, along):
    count, rows, width = got.shape

    def kernel(got_ref, skip_ref, gain_ref, shift_ref, along_ref, merged_ref, hidden_ref, out_ref):
        merged = add_all([got_ref.at[i] for i in range(count)])
        merged_ref[...] = merged
        hidden = norm_parts(merged)[0] * skip_ref[...]
        hidden_ref[...] = hidden
        out_ref[:rows] = (norm_parts(hidden)[0] * gain_ref[...] + shift_ref[...]).astype(BF16)
        out_ref[rows:] = along_ref[...]

    outs = (
        struct((rows, width), F32),
        struct((rows, width), F32),
        struct((rows + along.shape[0], width), BF16),
    )
    ins = (got, skip_gain[None], norm1_gain[None], shift[None], along)
    return call(kernel, 2.5, outs, ins, "first_norms")


def mid_norm(pieces, hidden, gain):
    def kernel(*refs):
        hidden_ref, gain_ref, new_ref, out_ref = refs[len(pieces) :]
        new = hidden_ref[...] + add_all(refs[: len(pieces)])
        new_ref[...] = new
        out_ref[...] = (norm_parts(new)[0] * gain_ref[...]).astype(BF16)

    outs = (struct(hidden.shape, F32), struct(hidden.shape, BF16))
    return call(kernel, 1.5, outs, (*pieces, hidden, gain[None]), "mid_norm")


def mid_norm_back(pieces, residual, hidden, gain):
    def kernel(*refs):
        res_ref, hidden_ref, gain_ref, new_ref, out_ref, dgain_ref = refs[len(pieces) :]
        unit, scale = norm_parts(hidden_ref[...])
        grad, dgain = norm_back(unit, scale, gain_ref[...], add_all(refs[: len(pieces)]))
        dgain_ref[...] = dgain
        new = res_ref[...].astype(F32) + grad
        new_ref[...] = new
        out_ref[...] = new.astype(BF16)

    width = hidden.shape[1]
    outs = (struct(hidden.shape, F32), struct(hidden.shape, BF16), struct((1, width), F32))
    return call(kernel, 2, outs, (*pieces, residual, hidden, gain[None]), "mid_norm_back")


def last_norms(pieces, hidden_zero, merged, residual, gains, rows_two, rows_three, misc):
    rows, width = merged.shape
    many = len(pieces)

    def kernel(*refs):
        h0_ref, merged_ref, res_ref, g1_ref, gs_ref, two_ref, three_ref, misc_ref, out_ref = refs[many:]
        grad = add_all(refs[:many])
        shift_grad = jnp.sum(grad, 0, keepdims=True)
        unit, scale = norm_parts(h0_ref[...])
        step, norm1_grad = norm_back(unit, scale, g1_ref[...], grad)
        residual = res_ref[...] + step
        unit, scale = norm_parts(merged_ref[...])
        step, skip_grad = norm_back(unit, scale, gs_ref[...], residual)
        small = [skip_grad, norm1_grad, two_ref[...], three_ref[...], shift_grad, misc_ref[...]]
        small = stack(small + [jnp.zeros((16 - len(small), width), F32)]).astype(BF16)
        out_ref[:rows] = step.astype(BF16)
        out_ref[rows:] = small

    ins = (*pieces, hidden_zero, merged, residual, gains[0][None], gains[1][None])
    ins += (rows_two, rows_three, misc)
    return call(kernel, 3, struct((rows + 16, width), BF16), ins, "last_norms")


def project(parts, weight, other, cos_wide, sin_wide, qgain, kgain):
    width = parts[0].shape[1]
    tokens = cos_wide.shape[0]
    wide = weight.shape[0]
    each = wide // 3
    head = qgain.shape[0]
    heads = each // head
    many = len(parts)

    def kernel(*refs):
        w_ref, o_ref, cos_ref, sin_ref, qg_ref, kg_ref = refs[many : many + 6]
        x_ref, unit_ref, scale_ref, q_ref, kv_ref, sems = refs[many + 6 :]
        load_blocks(refs[:many], x_ref, sems)
        cos, sin = cos_ref[...], sin_ref[...]
        for s in range(2):
            out = dot_t(x_ref[...], w_ref[...] if s == 0 else pack_rows(o_ref))
            base = 2 * each * s
            kv_ref[:, base + each : base + 2 * each] = out[:, 2 * each :].astype(BF16)
            for h in range(heads):
                cut = lambda start: slice(start + h * head, start + (h + 1) * head)
                turn = lambda v: (v * cos + swap(v) * sin).astype(BF16)
                for part, gain_ref in ((0, qg_ref), (1, kg_ref)):
                    unit, scale = norm_parts(out[:, cut(part * each)])
                    n = (s * 2 + part) * heads + h
                    unit_ref[:, cut(base + part * each)] = unit
                    scale_ref[:, n : n + 1] = scale
                    if part == 0:
                        q_ref[:, cut(each * s)] = turn(unit * gain_ref[...])
                    else:
                        kv_ref[:, cut(base)] = turn(unit * gain_ref[...])

    outs = (
        struct((tokens, width), BF16),
        struct((tokens, 4 * each), F32),
        struct((tokens, 4 * heads), F32),
        struct((tokens, 2 * each), BF16),
        struct((tokens, 4 * each), BF16),
    )
    ins = (*parts, weight, other, cos_wide, sin_wide, qgain[None], kgain[None])
    specs = [HBM] * many + [whole(item.shape) for item in ins[many:]]
    specs[many + 1] = pack_spec(wide, width, 0, 48)
    return call(
        kernel, 6, outs, ins, "project", (1,), specs, tuple(whole(o.shape) for o in outs),
        (pltpu.SemaphoreType.DMA((many,)),),
    )


def key_rows(refs, shard, start, size, each):
    first = 2 * each * shard + start
    second = 2 * each * (1 - shard) + start
    return stack(
        [
            ref[:, first : first + size] if i < 2 else ref[:, second : second + size]
            for i, ref in enumerate(refs)
        ]
    )


def self_attention(queries, pairs, out_w, pack, head):
    tokens, both = queries.shape
    each = both // 2
    heads = each // head
    width = out_w.shape[1]
    scaling = head ** (-0.5)

    def kernel(q_ref, a_ref, b_ref, c_ref, d_ref, w_ref, o_ref, mixed_ref, total_ref, *out_refs):
        refs = (a_ref, b_ref, c_ref, d_ref)
        for s in range(2):
            for h in range(heads):
                n = s * heads + h
                cut = slice(n * head, (n + 1) * head)
                scores = dot_t(q_ref[:, cut], key_rows(refs, s, h * head, head, each)) * scaling
                most = jnp.max(scores, -1, keepdims=True)
                total = most + jnp.log(jnp.sum(jnp.exp(scores - most), -1, keepdims=True))
                total_ref[:, n : n + 1] = total
                shares = jnp.exp(scores - total).astype(BF16)
                mixture = dot(shares, key_rows(refs, s, each + h * head, head, each))
                mixed_ref[:, cut] = mixture.astype(BF16)
        out = dot(mixed_ref[:, :each], w_ref[...])
        out = out + dot(mixed_ref[:, each:], pack_rows(o_ref))
        put_blocks(out_refs, out)

    outs = (
        struct((tokens, both), BF16),
        struct((tokens, 2 * heads), F32),
    ) + (struct((tokens // 4, width), BF16),) * 4
    ins = (queries, *pairs, out_w, pack)
    specs = [whole(item.shape) for item in ins]
    specs[-1] = pack_spec(each, width, 48)
    return call(
        kernel, 5, outs, ins, "self_attention", (1,), specs, tuple(whole(o.shape) for o in outs)
    )


def self_attention_back(queries, pairs, totals, parts, out_w, pack, head):
    tokens, both = queries.shape
    each = both // 2
    heads = each // head
    rows, width = parts[0].shape
    scaling = head ** (-0.5)
    many = len(parts)

    def kernel(*refs):
        q_ref, a_ref, b_ref, c_ref, d_ref, total_ref, w_ref, o_ref = refs[many : many + 8]
        x_ref, dq_ref, own_ref, half_ref, core_ref, far_ref, dm_ref, sems = refs[many + 8 :]
        pair_refs = (a_ref, b_ref, c_ref, d_ref)
        load_blocks(refs[:many], x_ref, sems)
        dm_ref[:, :each] = dot_t(x_ref[...], w_ref[...]).astype(BF16)
        dm_ref[:, each:] = dot_t(x_ref[...], pack_rows(o_ref)).astype(BF16)

        def put(grads, shard, start):
            first = 2 * each * shard + start
            second = 2 * each * (1 - shard) + start
            cut = lambda i: grads[i * tokens : (i + 1) * tokens]
            own_ref[:, first : first + head] = cut(0)
            core_ref[:, first : first + head] = cut(1).astype(BF16)
            half_ref[:, second : second + head] = cut(2).astype(BF16)
            far_ref[:, second : second + head] = cut(3).astype(BF16)

        for s in range(2):
            for h in range(heads):
                n = s * heads + h
                cut = slice(n * head, (n + 1) * head)
                mine, grads = q_ref[:, cut], dm_ref[:, cut]
                keys_h = key_rows(pair_refs, s, h * head, head, each)
                values_h = key_rows(pair_refs, s, each + h * head, head, each)
                shares = jnp.exp(dot_t(mine, keys_h) * scaling - total_ref[:, n : n + 1])
                dshares = dot_t(grads, values_h)
                put(t_dot(shares.astype(BF16), grads), s, each + h * head)
                weighted = jnp.sum(shares * dshares, -1, keepdims=True)
                dscores = (shares * (dshares - weighted) * scaling).astype(BF16)
                dq_ref[:, cut] = dot(dscores, keys_h)
                put(t_dot(dscores, mine), s, h * head)

    outs = (
        struct((tokens, width), BF16),
        struct((tokens, both), F32),
        struct((tokens, 4 * each), F32),
        struct((tokens, 4 * each), BF16),
        struct((tokens, 4 * each), BF16),
        struct((tokens, 4 * each), BF16),
    )
    ins = (*parts, queries, *pairs, totals, out_w, pack)
    specs = [HBM] * many + [whole(item.shape) for item in ins[many:]]
    specs[-1] = pack_spec(each, width, 48)
    return call(
        kernel, 9, outs, ins, "self_attention_back", (1,), specs,
        tuple(whole(o.shape) for o in outs),
        (pltpu.VMEM((tokens, both), BF16), pltpu.SemaphoreType.DMA((many,))),
    )


def project_back(units, scales, cos_wide, sin_wide, qgain, kgain, dq, own, core, half, far, weight, other):
    tokens = units.shape[0]
    wide, width = weight.shape
    each = wide // 3
    head = qgain.shape[0]
    heads = each // head

    def kernel(unit_ref, scale_ref, cos_ref, sin_ref, qg_ref, kg_ref, dq_ref, own_ref, core_ref, half_ref, far_ref, w_ref, o_ref,
               mine_ref, other_ref, dqg_ref, dkg_ref, *out_refs):
        cos, sin = cos_ref[...], sin_ref[...]
        dkv = own_ref[...] + core_ref[...].astype(F32)
        dkv = dkv + half_ref[...].astype(F32) + far_ref[...].astype(F32)
        dgains = [jnp.zeros((1, head), F32), jnp.zeros((1, head), F32)]
        for s, to_ref in ((0, mine_ref), (1, other_ref)):
            base = 2 * each * s
            to_ref[:, 2 * each : 3 * each] = dkv[:, base + each : base + 2 * each].astype(BF16)
            for h in range(heads):
                cut = lambda start: slice(start + h * head, start + (h + 1) * head)
                for part, gain_ref in ((0, qg_ref), (1, kg_ref)):
                    turned = dq_ref[:, cut(each * s)] if part == 0 else dkv[:, cut(base)]
                    grad = turned * cos - swap(turned) * sin
                    n = (s * 2 + part) * heads + h
                    unit = unit_ref[:, cut(base + part * each)]
                    grad, dgain = norm_back(unit, scale_ref[:, n : n + 1], gain_ref[...], grad)
                    dgains[part] = dgains[part] + dgain
                    to_ref[:, cut(part * each)] = grad.astype(BF16)
        dqg_ref[...], dkg_ref[...] = dgains
        out = dot(mine_ref[...], w_ref[...])
        put_blocks(out_refs, out + dot(other_ref[...], pack_rows(o_ref)))

    outs = (
        struct((tokens, wide), BF16),
        struct((tokens, wide), BF16),
        struct((1, head), F32),
        struct((1, head), F32),
    ) + (struct((tokens // 4, width), BF16),) * 4
    ins = (units, scales, cos_wide, sin_wide, qgain[None], kgain[None], dq, own, core, half, far, weight, other)
    specs = [whole(item.shape) for item in ins]
    specs[-1] = pack_spec(wide, width, 0, 48)
    return call(
        kernel, 8, outs, ins, "project_back", (1,), specs, tuple(whole(o.shape) for o in outs)
    )


def text_shares(scores, scaling, count):
    place = lax.broadcasted_iota(jnp.int32, scores.shape, 1)
    scores = jnp.where(place < count, scores * scaling, -1e30)
    most = jnp.max(scores, -1, keepdims=True)
    total = most + jnp.log(jnp.sum(jnp.exp(scores - most), -1, keepdims=True))
    return jnp.exp(scores - total)


def cross_layer(parts, cq_w, out_w, pack, text, other_text, gain, text_count):
    rows, width = parts[0].shape
    tokens = rows * len(parts)
    each = cq_w.shape[0]
    head = gain.shape[0]
    heads = each // head
    scaling = head ** (-0.5)
    many = len(parts)

    def kernel(*refs):
        cq_ref, w_ref, ocq_ref, ow_ref, text_ref, otext_ref, gain_ref = refs[many : many + 7]
        x_ref, raw_ref, mixed_ref, *out_refs, sems = refs[many + 7 :]
        load_blocks(refs[:many], x_ref, sems)
        raw_ref[:, :each] = dot_t(x_ref[...], cq_ref[...])
        raw_ref[:, each:] = dot_t(x_ref[...], pack_rows(ocq_ref))
        for s, keys_ref in ((0, text_ref), (1, otext_ref)):
            for h in range(heads):
                n = s * heads + h
                cut = slice(n * head, (n + 1) * head)
                mine = (norm_parts(raw_ref[:, cut])[0] * gain_ref[...]).astype(BF16)
                scores = dot_t(mine, keys_ref[:, h * head : (h + 1) * head])
                shares = text_shares(scores, scaling, text_count).astype(BF16)
                values = keys_ref[:, each + h * head : each + (h + 1) * head]
                mixed_ref[:, cut] = dot(shares, values).astype(BF16)
        out = dot(mixed_ref[:, :each], w_ref[...])
        out = out + dot(mixed_ref[:, each:], pack_rows(ow_ref))
        put_blocks(out_refs, out)

    outs = (
        struct((tokens, width), BF16),
        struct((tokens, 2 * each), F32),
        struct((tokens, 2 * each), BF16),
    ) + (struct((rows, width), BF16),) * many
    ins = (*parts, cq_w, out_w, pack, pack, text, other_text, gain[None])
    specs = [HBM] * many + [whole(item.shape) for item in ins[many:]]
    specs[many + 2] = pack_spec(each, width, 64)
    specs[many + 3] = pack_spec(each, width, 80)
    return call(
        kernel, 7, outs, ins, "cross_layer", (1,), specs, tuple(whole(o.shape) for o in outs),
        (pltpu.SemaphoreType.DMA((many,)),),
    )


def cross_layer_back(parts, raw, cq_w, out_w, pack, text, other_text, gain, text_count):
    rows, width = parts[0].shape
    tokens = rows * len(parts)
    each = cq_w.shape[0]
    head = gain.shape[0]
    heads = each // head
    scaling = head ** (-0.5)
    many = len(parts)

    def kernel(*refs):
        raw_ref, cq_ref, w_ref, ocq_ref, ow_ref, text_ref, otext_ref, gain_ref = refs[many : many + 8]
        x_ref, draw_ref, dtext_ref, dother_ref, dgain_ref, *out_refs, dm_ref, sems = refs[many + 8 :]
        load_blocks(refs[:many], x_ref, sems)
        dm_ref[:, :each] = dot_t(x_ref[...], w_ref[...]).astype(BF16)
        dm_ref[:, each:] = dot_t(x_ref[...], pack_rows(ow_ref)).astype(BF16)
        dgain = jnp.zeros((1, head), F32)
        for s, keys_ref, to_ref in ((0, text_ref, dtext_ref), (1, otext_ref, dother_ref)):
            for h in range(heads):
                n = s * heads + h
                cut = slice(n * head, (n + 1) * head)
                kcut = slice(h * head, (h + 1) * head)
                vcut = slice(each + h * head, each + (h + 1) * head)
                unit, scale = norm_parts(raw_ref[:, cut])
                mine = (unit * gain_ref[...]).astype(BF16)
                shares = text_shares(dot_t(mine, keys_ref[:, kcut]), scaling, text_count)
                dshares = dot_t(dm_ref[:, cut], keys_ref[:, vcut])
                to_ref[:, vcut] = t_dot(shares.astype(BF16), dm_ref[:, cut]).astype(BF16)
                weighted = jnp.sum(shares * dshares, -1, keepdims=True)
                dscores = (shares * (dshares - weighted) * scaling).astype(BF16)
                to_ref[:, kcut] = t_dot(dscores, mine).astype(BF16)
                grad, step = norm_back(unit, scale, gain_ref[...], dot(dscores, keys_ref[:, kcut]))
                dgain = dgain + step
                draw_ref[:, cut] = grad.astype(BF16)
        dgain_ref[...] = dgain
        out = dot(draw_ref[:, :each], cq_ref[...])
        out = out + dot(draw_ref[:, each:], pack_rows(ocq_ref))
        put_blocks(out_refs, out)

    outs = (
        struct((tokens, width), BF16),
        struct((tokens, 2 * each), BF16),
        struct(text.shape, BF16),
        struct(text.shape, BF16),
        struct((1, head), F32),
    ) + (struct((rows, width), BF16),) * many
    ins = (*parts, raw, cq_w, out_w, pack, pack, text, other_text, gain[None])
    specs = [HBM] * many + [whole(item.shape) for item in ins[many:]]
    specs[many + 3] = pack_spec(each, width, 64)
    specs[many + 4] = pack_spec(each, width, 80)
    return call(
        kernel, 10, outs, ins, "cross_layer_back", (1,), specs,
        tuple(whole(o.shape) for o in outs),
        (pltpu.VMEM((tokens, 2 * each), BF16), pltpu.SemaphoreType.DMA((many,))),
    )


def feed_forward(parts, cot, fc1_w, fc2_w, pack):
    rows, width = parts[0].shape
    tokens = rows * len(parts)
    hidden = fc2_w.shape[0]
    block = hidden // 2
    places = pack.shape[0]
    each = hidden // places
    both = 2 * each
    root = (2 / 3.141592653589793) ** 0.5
    many = len(parts)

    def kernel(*refs):
        cot_ref, w1_ref, w2_ref, pack_ref, x_ref, acts_ref, *out_refs, acc_ref, sum_ref, sems = refs[many:]
        step = pl.program_id(0)

        @pl.when(step == 0)
        def _():
            load_blocks(refs[:many], x_ref, sems)
            acc_ref[...] = jnp.zeros_like(acc_ref)
            sum_ref[...] = jnp.zeros_like(sum_ref)

        def work(pre, w2, back):
            square = pre * pre
            bent = jnp.tanh(root * pre * (1 + 0.044715 * square))
            part = 0.5 * (1 + bent)
            slope = part + 0.5 * pre * (1 - bent * bent) * root * (1 + 3 * 0.044715 * square)
            grad = (dot_t(cot_ref[...], w2) * slope).astype(BF16)
            acts_ref[0, 0] = grad
            active = (pre * part).astype(BF16)
            acts_ref[0, 1] = active
            acc_ref[...] += back(grad)
            sum_ref[...] += dot(active, w2)

        @pl.when(step < 2)
        def _():
            weight = w1_ref[...]
            work(dot(x_ref[...], weight), w2_ref[...], lambda grad: dot_t(grad, weight))

        @pl.when(step >= 2)
        def _():
            weight = pack_ref[:, :each].reshape(block, width)
            second = pack_ref[:, each:].reshape(block, width)
            work(dot_t(x_ref[...], weight), second, lambda grad: dot(grad, weight))

        @pl.when(step == 3)
        def _():
            put_blocks(out_refs[:many], acc_ref[...])
            put_blocks(out_refs[many:], sum_ref[...])

    low = lambda i: jnp.minimum(i, 1)
    high = lambda i: jnp.maximum(i - 2, 0)
    outs = (
        struct((tokens, width), BF16),
        struct((2, 2, tokens, hidden), BF16),
    ) + (struct((rows, width), BF16),) * (2 * many)
    out_specs = (
        whole((tokens, width)),
        pl.BlockSpec((1, 2, tokens, block), lambda i: (i // 2, 0, 0, i % 2)),
    ) + (whole((rows, width)),) * (2 * many)
    in_specs = [HBM] * many + [
        whole(cot.shape),
        pl.BlockSpec((width, block), lambda i: (0, low(i))),
        pl.BlockSpec((block, width), lambda i: (low(i), 0)),
        pl.BlockSpec((places // 2, both, width), lambda i: (high(i), 0, 0)),
    ]
    return call(
        kernel, 9, outs, (*parts, cot, fc1_w, fc2_w, pack), "feed_forward", (4,), in_specs, out_specs,
        (
            pltpu.VMEM((tokens, width), F32),
            pltpu.VMEM((tokens, width), F32),
            pltpu.SemaphoreType.DMA((many,)),
        ),
    )


def feed_forward_grads(acts, rows_in, cot, places):
    _, _, tokens, hidden = acts.shape
    width = cot.shape[1]
    share = 2 * hidden // places

    def kernel(acts_ref, x_ref, cot_ref, out_ref):
        which = pl.program_id(1)

        def put(right_ref):
            grads = t_dot(acts_ref[0, 0], right_ref[...]).astype(BF16)
            out_ref[...] = grads.reshape(out_ref.shape)

        pl.when(which == 0)(lambda: put(x_ref))
        pl.when(which == 1)(lambda: put(cot_ref))

    return call(
        kernel,
        7,
        struct((places, 2, share, width), BF16),
        (acts, rows_in, cot),
        "feed_forward_grads",
        (2, 2),
        [
            pl.BlockSpec((1, 1, tokens, hidden), lambda s, w: (s, w, 0, 0)),
            whole(rows_in.shape),
            whole(cot.shape),
        ],
        pl.BlockSpec((places // 2, 1, share, width), lambda s, w: (w, s, 0, 0)),
    )


def late_grads(draw, mixed_two, rows_two, grad_two, mine, other, mixed_one, rows_one, grad_one, texts):
    each = draw.shape[1] // 2
    width = rows_two.shape[1]
    wide = mine.shape[1]
    places, _, more, _ = texts.shape
    first, second = 48, 96

    def kernel(draw_ref, mixed_ref, x_ref, d_ref, mine_ref, other_ref, one_ref, y_ref, e_ref, text_ref, out_ref, hold_ref):
        step = pl.program_id(0)
        for s, grad_ref in ((0, mine_ref), (1, other_ref)):

            @pl.when(step == s)
            def _(s=s, grad_ref=grad_ref):
                cut = slice(s * each, (s + 1) * each)
                hold_ref[:each] = t_dot(draw_ref[:, cut], x_ref[...]).astype(BF16)
                hold_ref[each : 2 * each] = t_dot(mixed_ref[:, cut], d_ref[...]).astype(BF16)
                hold_ref[2 * each : 2 * each + wide] = t_dot(grad_ref[...], y_ref[...]).astype(BF16)
                hold_ref[2 * each + wide :] = t_dot(one_ref[:, cut], e_ref[...]).astype(BF16)

        for place in range(places):
            for share, start, stop, to in (
                (first, 0, 2 * each, 0),
                (second, 2 * each, 3 * each + wide, first),
            ):
                begin = min(start + place * share, stop)
                count = min(share, stop - begin)
                out_ref[place, 0, to : to + count] = hold_ref[begin : begin + count]
                if count < share:
                    blank = jnp.zeros((share - count, width), BF16)
                    out_ref[place, 0, to + count : to + share] = blank
            out_ref[place, 0, first + second :] = text_ref[place, 0]

    ins = (draw, mixed_two, rows_two, grad_two, mine, other, mixed_one, rows_one, grad_one, texts)
    rows = first + second + more
    return call(
        kernel, 9, struct((places, 2, rows, width), BF16), ins, "late_grads", (2,),
        [whole(item.shape) for item in ins[:-1]]
        + [pl.BlockSpec((places, 1, more, width), lambda s: (0, s, 0, 0))],
        pl.BlockSpec((places, 1, rows, width), lambda s: (0, s, 0, 0)),
        (pltpu.VMEM((3 * each + wide, width), BF16),),
    )


def skip_grads(parts, joined_own, joined_other, long):
    rows, width = parts[0].shape
    small = 16
    rows -= small
    tokens, slab = joined_own.shape
    many = len(parts)

    def kernel(*refs):
        own_ref, other_ref, x_ref, out_ref, all_ref, sems = refs[many:]
        load_blocks(refs[:many], all_ref, sems)
        total = jnp.zeros((small, width), F32)
        for i in range(many):
            start = i * (rows + small)
            x_ref[i * rows : (i + 1) * rows] = all_ref[start : start + rows]
            total = total + all_ref[start + rows : start + rows + small].astype(F32)
        for s, left_ref in ((0, own_ref), (1, other_ref)):
            out_ref[s, :slab] = t_dot(left_ref[...], x_ref[...])
            out_ref[s, slab : slab + small] = total
            out_ref[s, slab + small :] = jnp.zeros((long - slab - small, width), F32)

    outs = (struct((tokens, width), BF16), struct((2, long, width), F32))
    ins = (*parts, joined_own, joined_other)
    return call(
        kernel, 4, outs, ins, "skip_grads", (1,),
        [HBM] * many + [whole(joined_own.shape), whole(joined_other.shape)],
        tuple(whole(o.shape) for o in outs),
        (pltpu.VMEM((many * (rows + small), width), BF16), pltpu.SemaphoreType.DMA((many,))),
    )


def joined_grads(rows_in, pack, slab):
    tokens, width = rows_in.shape
    _, count, deep, _ = pack.shape
    held = slab // deep
    half = count // 2

    def kernel(x_ref, pack_ref, one_ref, two_ref):
        for step, out_ref in ((0, one_ref), (1, two_ref)):

            @pl.when(pl.program_id(0) == step)
            def _(out_ref=out_ref):
                for j in range(half):
                    weight = pack_ref[:, j].reshape(slab, width)
                    out_ref[:, j * slab : (j + 1) * slab] = dot_t(x_ref[...], weight)

    outs = (struct((tokens, width), F32), struct((tokens, width), F32))
    return call(
        kernel, 9, outs, (rows_in, pack), "joined_grads", (2,),
        [
            whole(rows_in.shape),
            pl.BlockSpec((held, half, deep, width), lambda i: (0, i, 0, 0)),
        ],
        (whole((tokens, width)), whole((tokens, width))),
    )


def feed_forward_out(sums):
    places, share, width = sums.shape
    half = places // 2
    hidden = half * share

    def kernel(sum_ref, one_ref, two_ref):
        @pl.when(pl.program_id(0) == 0)
        def _():
            one_ref[...] = sum_ref[...].reshape(hidden, width).astype(F32).T

        @pl.when(pl.program_id(0) == 1)
        def _():
            two_ref[...] = sum_ref[...].reshape(hidden, width).astype(F32)

    outs = (struct((width, hidden), F32), struct((hidden, width), F32))
    return call(
        kernel, 6, outs, (sums,), "feed_forward_out", (2,),
        [pl.BlockSpec((half, share, width), lambda i: (i, 0, 0))],
        (whole((width, hidden)), whole((hidden, width))),
    )


def text_layer(tokens, ckv, gain, rows):
    count, width = tokens.shape
    packed = ckv.ndim == 3
    both = ckv.shape[2] // 4 if packed else ckv.shape[1]
    each = both // 2
    head = gain.shape[0]
    heads = each // head

    def kernel(x_ref, w_ref, gain_ref, pair_ref, unit_ref, scale_ref, *more):
        if packed:
            weight_ref = more[0]
            deep = w_ref.shape[1]
            for place in range(w_ref.shape[0]):
                for k in range(4):
                    start = (place * 4 + k) * deep
                    weight_ref[start : start + deep] = w_ref[place, :, k * both : (k + 1) * both]
        else:
            weight_ref = w_ref
        out = dot(x_ref[...], weight_ref[...])
        pair_ref[...] = jnp.zeros_like(pair_ref)
        pair_ref[:count, each:] = out[:, each:].astype(BF16)
        for h in range(heads):
            cut = slice(h * head, (h + 1) * head)
            unit, scale = norm_parts(out[:, cut])
            unit_ref[:, cut] = unit
            scale_ref[:, h : h + 1] = scale
            pair_ref[:count, cut] = (unit * gain_ref[...]).astype(BF16)

    outs = (
        struct((rows, both), BF16),
        struct((count, each), F32),
        struct((count, heads), F32),
    )
    specs = [whole(tokens.shape), whole(ckv.shape), whole((1, head))]
    if packed:
        outs += (struct((width, both), BF16),)
        deep = width // ckv.shape[0] // 4
        place = ckv.shape[1] // deep - 1
        specs[1] = pl.BlockSpec((ckv.shape[0], deep, ckv.shape[2]), lambda *step: (0, place, 0))
    return call(
        kernel, 4, outs, (tokens, ckv, gain[None]), "text_layer", (1,), specs,
        tuple(whole(o.shape) for o in outs),
    )


def text_layer_back(pairs, units, scales, tokens, ckvs, gain, places):
    count, width = tokens.shape
    both = ckvs[0].shape[1]
    each = both // 2
    head = gain.shape[0]
    heads = each // head
    wide = 4 * both
    deep = 48
    more = 48
    long = more * places

    def kernel(a_ref, b_ref, ua_ref, ub_ref, sa_ref, sb_ref, x_ref, wa_ref, wb_ref, gain_ref, out_ref, dw_ref, grad_ref, part_ref):
        dgain = jnp.zeros((1, head), F32)
        part = jnp.zeros((count, width), F32)
        for s, (pair_ref, unit_ref, scale_ref, w_ref) in enumerate(
            ((a_ref, ua_ref, sa_ref, wa_ref), (b_ref, ub_ref, sb_ref, wb_ref))
        ):
            grad_ref[:, each:] = pair_ref[:count, each:]
            for h in range(heads):
                cut = slice(h * head, (h + 1) * head)
                grad, step = norm_back(
                    unit_ref[:, cut], scale_ref[:, h : h + 1], gain_ref[...], pair_ref[:count, cut].astype(F32)
                )
                dgain = dgain + step
                grad_ref[:, cut] = grad.astype(BF16)
            dw_ref[...] = t_dot(grad_ref[...], x_ref[...]).astype(BF16)
            part = part + dot_t(grad_ref[...], w_ref[...])
            for place in range(places):
                begin = min(place * deep, both)
                held = min(deep, both - begin)
                out_ref[place, s, :deep] = jnp.zeros((deep, wide), BF16)
                out_ref[place, s, :held, :width] = dw_ref[begin : begin + held]
        part_ref[...] = jnp.zeros_like(part_ref)
        part_ref[:count, :width] = part
        part_ref[long - 1 :, :head] = dgain
        for place in range(places):
            rows = part_ref[place * more : (place + 1) * more].astype(BF16)
            for s in range(2):
                out_ref[place, s, deep : deep + more] = rows

    ins = (*pairs, *units, *scales, tokens, *ckvs, gain[None])
    scratch = (
        pltpu.VMEM((both, width), BF16),
        pltpu.VMEM((count, both), BF16),
        pltpu.VMEM((long, wide), F32),
    )
    return call(
        kernel, 9, struct((places, 2, deep + more, wide), BF16), ins, "text_layer_back", scratch=scratch
    )


def local(
    latent,
    skip_input,
    text_tokens,
    condition,
    positions,
    cotangent,
    skip_w,
    skip_gain,
    norm1_gain,
    mod_w,
    qkv_w,
    qnorm_gain,
    knorm_gain,
    attn_out_w,
    norm2_gain,
    cq_w,
    ckv_w,
    cqnorm_gain,
    cknorm_gain,
    cross_out_w,
    norm3_gain,
    fc1_w,
    fc2_w,
):
    token_count, model_width = latent.shape
    head_dim = qnorm_gain.shape[0]
    local_width = cq_w.shape[1]
    local_heads = local_width // head_dim
    slab_width = skip_w.shape[0]
    hidden_width = fc1_w.shape[1]
    text_count, text_width = text_tokens.shape
    tensor_place = lax.axis_index("tensor")
    tensor_count = lax.axis_size("tensor")
    dp_count = lax.axis_size("dp")
    low_count = len(low_groups()[0])
    part_count = token_count // tensor_count
    ring = tensor_count // 2
    ring_place, half = tensor_place % ring, tensor_place // ring
    qkv_rows = 3 * local_width

    def own_rows(rows):
        return lax.dynamic_slice_in_dim(rows, tensor_place * part_count, part_count, 0)

    def ring_rows(rows, which):
        first = which * ring
        return jnp.concatenate(
            [
                lax.dynamic_slice_in_dim(
                    rows, (first + (ring_place - k) % ring) * part_count, part_count, 0
                )
                for k in range(ring)
            ],
            0,
        )

    joined = jnp.concatenate([latent, skip_input], 1)
    joined_part = lax.dynamic_slice_in_dim(joined, tensor_place * slab_width, slab_width, 1)
    partial = jnp.dot(joined_part, skip_w, preferred_element_type=F32).astype(BF16)
    got = exchange(partial.reshape(tensor_count, part_count, model_width))

    dp_place = lax.axis_index("dp")
    qkv_flat = qkv_w.transpose(1, 2, 0).reshape(qkv_rows, model_width)
    cq_turned = cq_w.T
    shares = [dp_slice(qkv_flat, 48)]
    shares += [dp_slice(rows, 16) for rows in (attn_out_w, cq_turned, cross_out_w)]
    pack = lax.all_gather(half_swap(jnp.concatenate(shares, 0)), "dp", axis=0, tiled=False)
    ckv_flat = ckv_w.reshape(text_width, 2 * local_width)
    text_pair, text_units, text_scales = text_layer(
        text_tokens, ckv_flat, cknorm_gain, model_width // 4
    )
    share = hidden_width // dp_count
    deep = text_width // dp_count // 4
    ff_share = [
        lax.dynamic_slice_in_dim(fc1_w, dp_place * share, share, 1).T,
        lax.dynamic_slice_in_dim(fc2_w, dp_place * share, share, 0),
    ]
    ckv_share = lax.dynamic_slice_in_dim(ckv_flat, dp_place * 4 * deep, 4 * deep, 0)
    ff_share.append(jnp.concatenate(jnp.split(ckv_share, 4), 1))
    ff_share = half_swap(jnp.concatenate(ff_share, 0))
    silu_cond = jax.nn.silu(condition.astype(F32)).astype(BF16)
    shift = jnp.dot(silu_cond[None], mod_w, preferred_element_type=F32)[0]
    cos_wide, sin_wide = rotary_tables(ring_rows(positions, half), head_dim)
    cot_rows = ring_rows(cotangent, half)
    got, qkv_flat, cos_wide, sin_wide, shift, text_pair, cot_rows, ff_share = join(
        got, qkv_flat, cos_wide, sin_wide, shift, text_pair, cot_rows, ff_share
    )
    skip_share = dp_slice(skip_w, 32)
    merged, hidden_zero, normed = first_norms(got, skip_gain, norm1_gain, shift, skip_share)
    normed_parts = ring_gather(normed)
    rows_one, units, scales, queries, own_pair = project(
        normed_parts, qkv_flat, pack, cos_wide, sin_wide, qnorm_gain, knorm_gain
    )
    ff_pack = lax.all_gather(after(ff_share, rows_one), "dp", axis=0, tiled=False)
    core_pair = core_swap(own_pair)
    half_pair = half_swap(own_pair)
    pairs = (own_pair, core_pair, half_pair, core_swap(half_pair))
    mixed_one, totals, *partial = self_attention(
        queries, pairs, attn_out_w, pack, head_dim
    )
    hidden_one, normed = mid_norm(ring_scatter(partial), hidden_zero, norm2_gain)
    skip_rows = jnp.concatenate([part[part_count:] for part in normed_parts], 0)
    skip_half = half_swap(after(skip_rows, normed))
    other_text, other_units, other_scales, other_ckv = text_layer(
        text_tokens, after(ff_pack, normed), cknorm_gain, model_width // 4
    )
    *normed_parts, skip_half, other_text = join(*ring_gather(normed), skip_half, other_text)
    skip_rows = place_blocks(jnp.split(skip_rows, ring), jnp.split(skip_half, ring))
    skip_pack = lax.all_gather(
        skip_rows.reshape(tensor_count, -1, model_width), "dp", axis=0, tiled=False
    )
    rows_two, cross_raw, mixed_two, *partial = cross_layer(
        normed_parts,
        cq_turned,
        cross_out_w,
        pack,
        text_pair,
        other_text,
        cqnorm_gain,
        text_count,
    )
    hidden_two, normed = mid_norm(ring_scatter(partial), hidden_one, norm3_gain)
    rows_three, acts, *partial = feed_forward(
        ring_gather(normed), cot_rows, fc1_w, fc2_w, ff_pack
    )
    partial, last_partial = partial[:ring], partial[ring:]

    fc_grads = feed_forward_grads(acts, rows_three, cot_rows, low_count)
    *pieces, fc_grads = join(*ring_scatter(partial), fc_grads.reshape(-1, model_width))
    fc_grads = scatter_low(after(fc_grads, skip_pack))
    residual, out_grad, norm3_grad = mid_norm_back(
        pieces, own_rows(cotangent), hidden_two, norm3_gain
    )
    out_parts = ring_gather(out_grad)
    grad_rows_two, cross_raw_grad, text_own, text_other, cqnorm_grad, *partial = cross_layer_back(
        out_parts,
        cross_raw,
        cq_turned,
        cross_out_w,
        pack,
        text_pair,
        other_text,
        cqnorm_gain,
        text_count,
    )
    residual, out_grad, norm2_grad = mid_norm_back(
        ring_scatter(partial), residual, hidden_one, norm2_gain
    )
    text_sums = text_layer_back(
        (text_own, text_other),
        (text_units, other_units),
        (text_scales, other_scales),
        after(text_tokens, out_grad),
        (ckv_flat, other_ckv),
        cknorm_gain,
        low_count,
    )
    *out_parts, text_sums = join(*ring_gather(out_grad), text_sums)
    grad_rows_one, query_grad, pair_grad, half_grad, core_grad, far_grad = self_attention_back(
        queries,
        pairs,
        totals,
        out_parts,
        attn_out_w,
        pack,
        head_dim,
    )
    core_grad = core_swap(core_grad)
    half_grad = half_swap(half_grad)
    far_grad = far_swap(far_grad)
    core_grad, half_grad, far_grad = join(core_grad, half_grad, far_grad)
    fc_grads = after(fc_grads, half_grad)
    share = fc_grads.shape[0] // 2
    fc_grads = half_sum(fc_grads[:share], fc_grads[share:])
    output = hidden_two
    for piece in ring_scatter(after_all(last_partial, half_grad)):
        output = output + piece.astype(F32)
    projected_grad, projected_other, qnorm_grad, knorm_grad, *partial = project_back(
        units,
        scales,
        cos_wide,
        sin_wide,
        qnorm_gain,
        knorm_gain,
        query_grad,
        pair_grad,
        core_grad,
        half_grad,
        far_grad,
        qkv_flat,
        pack,
    )
    *partial, fc_grads, output = join(*partial, fc_grads, output)
    fc_grads = fc_grads + low_swap(fc_grads.astype(BF16)).astype(F32)
    late_sums = late_grads(
        cross_raw_grad,
        mixed_two,
        rows_two,
        grad_rows_two,
        projected_grad,
        projected_other,
        mixed_one,
        rows_one,
        grad_rows_one,
        text_sums,
    )
    late_sums = late_sums.reshape(-1, model_width)
    *pieces, late_sums, fc_grads = join(*ring_scatter(partial), late_sums, fc_grads)
    late_sums = scatter_low(late_sums)
    misc = jnp.concatenate([qnorm_grad, knorm_grad, cqnorm_grad], 1)
    misc = jnp.pad(misc, ((0, 0), (0, model_width - misc.shape[1])))
    merged_out = last_norms(
        pieces,
        hidden_zero,
        merged,
        residual,
        (norm1_gain, skip_gain),
        norm2_grad,
        norm3_grad,
        misc,
    )
    joined_rows = ring_rows(joined, half)
    joined_own = lax.dynamic_slice_in_dim(joined_rows, tensor_place * slab_width, slab_width, 1)
    joined_other = lax.dynamic_slice_in_dim(
        joined_rows, (tensor_place + ring) % tensor_count * slab_width, slab_width, 1
    )
    *merged_parts, joined_own, joined_other = join(
        *ring_gather(merged_out), joined_own, joined_other
    )

    last_rows = -(-(slab_width + 16) // (8 * dp_count)) * 8 * dp_count
    merged_rows, last_sums = skip_grads(merged_parts, joined_own, joined_other, last_rows)
    merged_half = half_swap(merged_rows)
    last_sums = scatter_stage(0, last_sums)
    output = jnp.concatenate(ring_gather(after(output.astype(BF16), merged_rows)), 0)
    last_sums, output = join(last_sums, output)
    last_sums = scatter_stage(1, last_sums)
    output_half = half_swap(output)
    last_sums, merged_half, late_sums = join(last_sums, merged_half, late_sums)
    fc_grads = gather_low(after(fc_grads.astype(BF16), late_sums))
    share = late_sums.shape[0] // 2
    own_sums = jnp.concatenate([late_sums[:share].astype(F32), last_sums[0]], 0)
    other_sums = jnp.concatenate([late_sums[share:], last_sums[1].astype(BF16)], 0)
    last_sums = half_sum(own_sums, other_sums)
    merged_grad = place_blocks(jnp.split(merged_rows, ring), jnp.split(merged_half, ring))
    latent_grad, skip_grad = joined_grads(merged_grad, skip_pack, slab_width)
    last_sums, latent_grad, skip_grad = join(last_sums, latent_grad, skip_grad)
    last_sums = last_sums + low_swap(last_sums.astype(BF16)).astype(F32)
    text_share = slice(share - 48, share)
    text_parts = ring_gather(last_sums[text_share].astype(BF16))
    text_rows = last_sums[text_share]
    for part in text_parts[1:]:
        text_rows = text_rows + part.astype(F32)
    last_sums = jnp.concatenate([last_sums[: share - 48], text_rows, last_sums[share:]], 0)
    last_sums, fc_grads = join(last_sums, fc_grads)
    last_sums = gather_low(last_sums.astype(BF16))
    fc1_grad, fc2_grad = feed_forward_out(fc_grads)
    output = place_blocks(jnp.split(output, ring), jnp.split(output_half, ring))
    last_sums, output, fc1_grad, fc2_grad = join(last_sums, output, fc1_grad, fc2_grad)
    cross_sums = last_sums[:, :48].reshape(-1, model_width)
    cq_grad = cross_sums[:local_width].T.astype(F32)
    cross_out_grad = cross_sums[local_width : 2 * local_width].astype(F32)
    self_sums = last_sums[:, 48:144].reshape(-1, model_width)
    qkv_grad = self_sums[:qkv_rows].T.astype(F32).reshape(model_width, 3, local_width)
    attn_out_grad = self_sums[qkv_rows : qkv_rows + local_width].astype(F32)
    ckv_grad = last_sums[:, 144:192].reshape(-1, model_width)[: 2 * local_width, :text_width]
    ckv_grad = ckv_grad.astype(F32).T.reshape(text_width, 2, local_width)
    text_rows = last_sums[:, text_share].reshape(-1, model_width).astype(F32)
    text_grad = text_rows[:text_count, :text_width]
    cknorm_grad = text_rows[-1, :head_dim]
    last_sums = last_sums[:, share:].reshape(4, 2, -1, model_width).transpose(1, 0, 2, 3)
    last_sums = last_sums.reshape(-1, model_width)
    skip_w_grad = last_sums[:slab_width].astype(F32)
    small = last_sums[slab_width:].astype(F32)
    skip_gain_grad, norm1_grad, norm2_grad, norm3_grad, mod_vector = [small[i] for i in range(5)]
    qnorm_grad, knorm_grad, cqnorm_grad = [
        small[5, i * head_dim : (i + 1) * head_dim] for i in range(3)
    ]
    mod_grad = silu_cond.astype(F32)[:, None] * mod_vector[None, :]
    return (
        output,
        latent_grad,
        skip_grad,
        text_grad,
        skip_w_grad,
        skip_gain_grad,
        norm1_grad,
        mod_grad,
        qkv_grad,
        qnorm_grad,
        knorm_grad,
        attn_out_grad,
        norm2_grad,
        cq_grad,
        ckv_grad,
        cqnorm_grad,
        cknorm_grad,
        cross_out_grad,
        norm3_grad,
        fc1_grad,
        fc2_grad,
    )


def solution(mesh):
    placed = (
        P("dp", None),
        P("dp", None),
        P(),
        P(),
        P("dp", None),
        P("dp", None),
        P("tensor", None),
        P(),
        P(),
        P(),
        P(None, None, "tensor"),
        P(),
        P(),
        P("tensor", None),
        P(),
        P(None, "tensor"),
        P(None, None, "tensor"),
        P(),
        P(),
        P("tensor", None),
        P(),
        P(None, "tensor"),
        P("tensor", None),
    )
    return jax.shard_map(
        local,
        mesh=mesh,
        in_specs=placed,
        out_specs=(
            P("dp", None),
            P("dp", None),
            P("dp", None),
            P(),
            P("tensor", None),
            P(),
            P(),
            P(),
            P(None, None, "tensor"),
            P(),
            P(),
            P("tensor", None),
            P(),
            P(None, "tensor"),
            P(None, None, "tensor"),
            P(),
            P(),
            P("tensor", None),
            P(),
            P(None, "tensor"),
            P("tensor", None),
        ),
        check_vma=False,
    )
```

time: 1080 us -> 550 us (0.51)
  waiting for transfers between devices: 694 us -> 207 us
  Pallas kernels: 0 us -> 144 us
  blocking collectives: 133 us -> 0 us
  matrix products: 102 us -> 4.89 us
  starting transfers between devices: 11.1 us -> 95.3 us
  other arithmetic: 75.7 us -> 22.2 us
  local copies, waits for them, and re-layouts: 36.5 us -> 52.3 us
    psum x8 -> x0, waiting for transfers between devices: 631 us -> none  [the longest x6 577 us: sum_rows(): return lax.psum(term_fn(0, token_count), 'tensor')]
    ppermute x2 -> x61, waiting for transfers between devices: 1.05 us -> 167 us  [the longest x24 46.5 us: ring_gather(): got = {k: lax.ppermute(block, 'tensor', ring_route(k)) for k in (1, 3, 2)}]
    pallas_call x0 -> x21, Pallas kernels: none -> 144 us  [call(): pl.pallas_call(kernel, out_shape=outs, scratch_shapes=scratch, compiler_p...]
    psum x3 -> x0, blocking collectives: 133 us -> none  [the longest x1 65.5 us: local(): lax.psum((qnorm_grad, knorm_grad, cqnorm_grad), ('dp', 'tensor'))]
    dot_general x37 -> x2, matrix products: 102 us -> 4.89 us  [the longest x1 2.77 us: local(): shift = jnp.dot(silu_cond[None], mod_w, preferred_element_type=F32)[0]]
    ppermute x2 -> x61, starting transfers between devices: 9.9 us -> 90.8 us  [the longest x24 32.8 us: ring_gather(): got = {k: lax.ppermute(block, 'tensor', ring_route(k)) for k in (1, 3, 2)}]
    reduce_sum x31 -> x0, other arithmetic: 42.1 us -> none  [the longest x11 17.5 us: layer_norm(): return centered * lax.rsqrt(variance + 1e-06) * norm_gain]
    all_gather x1 -> x5, waiting for transfers between devices: 61.8 us -> 22.1 us  [the longest x2 22.1 us: gather_low(): lax.all_gather(rows, 'dp', axis=0, tiled=False, axis_index_groups=low_gro...]
  transfers between devices with their start and end apart: 11 -> 69, of which waited for: 10 -> 40; matrix products, arithmetic and copies ran while one was open for 9% -> 8% of each run, Pallas kernels for 0% -> 25%
where the time goes in v2:
time: 550 us; the launch traced here: 541 us
  waiting for transfers between devices  207 us (38%)
  Pallas kernels  144 us (26%)
  starting transfers between devices  95.3 us (17%)
  local copies, waits for them, and re-layouts  52.3 us (10%)
  other arithmetic  22.2 us (4%)
  between operations  15.6 us (3%)
    pallas_call x21, Pallas kernels, call(): pl.pallas_call(kernel, out_shape=outs, scratch_shapes=scratch, compiler_p...  144 us
    ppermute x24, waiting for transfers between devices, ring_gather(): got = {k: lax.ppermute(block, 'tensor', ring_route(k)) for k in (1, 3, 2)}  46.5 us
    ppermute x18, waiting for transfers between devices, ring_scatter(): lax.ppermute(blocks[k], 'tensor', ring_route(-k))  41 us
    ppermute x9, waiting for transfers between devices, half_swap(): lax.ppermute(block, 'tensor', [(i, (i + count // 2) % count) for i in ran...  36.8 us
    ppermute x24, starting transfers between devices, ring_gather(): got = {k: lax.ppermute(block, 'tensor', ring_route(k)) for k in (1, 3, 2)}  32.8 us
    ppermute x18, starting transfers between devices, ring_scatter(): lax.ppermute(blocks[k], 'tensor', ring_route(-k))  22.2 us
    all_gather x2, waiting for transfers between devices, gather_low(): lax.all_gather(rows, 'dp', axis=0, tiled=False, axis_index_groups=low_gro...  22.1 us
    ppermute x9, starting transfers between devices, half_swap(): lax.ppermute(block, 'tensor', [(i, (i + count // 2) % count) for i in ran...  19.5 us
  transfers between devices with their start and end apart: 69, of which 40 were waited for; matrix products, arithmetic and copies ran while one was open for 8% of the time, Pallas kernels for 25%

profile of v2, /device:TPU:1, one launch (start us, length us, event | category | flops | bytes accessed | tf_op | source)
XLA Modules:
  0.0 540.7 jit_solution(11334850877378120912)
XLA Ops:
  49.3 9.0 %all-to-all-done.got_ref = bf16[8,64,1408]{2,1,0:T(8,128)(2,1)S(1)} async-done(((bf16[8,64,1408]{2,1,0:T(8,128)(2,1)}), bf16[8,64,1408]{2,1,0:T(8,128)(2,1)S(1)}, u32[]{:S(2)}, u32[]{:S(2)}) %all-to-all-start) | async-done | bytes 1441824 | tf_op jit(solution)/shard_map/all_to_all | solution.py:41
  69.2 8.3 %collective-permute-done.2.refs_2_ = bf16[96,1408]{1,0:T(8,128)(2,1)S(1)} collective-permute-done((bf16[96,1408]{1,0:T(8,128)(2,1)}, bf16[96,1408]{1,0:T(8,128)(2,1)S(1)}, u32[]{:S(2)}, u32[]{:S(2)}) %collective-permute-start.2) | collective-permute-done | bytes 270368 | tf_op jit(solution)/shard_map/ppermute | solution.py:70
  78.3 9.2 %project.1 = (bf16[256,1408]{1,0:T(8,128)(2,1)}, f32[256,704]{1,0:T(8,128)}, f32[256,8]{1,0:T(8,128)}, bf16[256,352]{1,0:T(8,128)(2,1)}, bf16[256,704]{1,0:T(8,128)(2,1)}) custom-call(bf16[96,1408]{1,0:T(8,128)(2,1)} %get-tuple-element.172.refs_0_, bf16[96,1408]{1,0:T(8,128)(2,1)} %copy-done.24, bf16[96,1408]{1,0:T(8,128)(2,1)} %copy-done.22, ...), custom_call_target="tpu_custom_call" | custom-call | bytes 19800000 | tf_op jit(solution)/shard_map/project/pallas_call | solution.py:186
  91.5 6.4 %collective-permute-done.6.c_ref.refs_7_ = bf16[256,704]{1,0:T(8,128)(2,1)S(1)} collective-permute-done((bf16[256,704]{1,0:T(8,128)(2,1)}, bf16[256,704]{1,0:T(8,128)(2,1)S(1)}, u32[]{:S(2)}, u32[]{:S(2)}) %collective-permute-start.6) | collective-permute-done | bytes 360480 | tf_op jit(solution)/shard_map/ppermute | solution.py:94
  103.6 7.4 %self_attention.1 = (bf16[256,352]{1,0:T(8,128)(2,1)}, f32[256,4]{1,0:T(8,128)}, bf16[64,1408]{1,0:T(8,128)(2,1)}, bf16[64,1408]{1,0:T(8,128)(2,1)}, bf16[64,1408]{1,0:T(8,128)(2,1)}, /*index=5*/bf16[64,1408]{1,0:T(8,128)(2,1)}) custom-call(bf16[256,352]{1,0:T(8,128)(2,1)} %get-tuple-element.178.q_ref.refs_4_, ...), custom_call_target="tpu_custom_call" | custom-call | bytes 16500000 | tf_op jit(solution)/shard_map/self_attention/pallas_call | solution.py:186
  140.2 9.9 %cross_layer.1 = (bf16[256,1408]{1,0:T(8,128)(2,1)}, f32[256,352]{1,0:T(8,128)}, bf16[256,352]{1,0:T(8,128)(2,1)}, bf16[64,1408]{1,0:T(8,128)(2,1)}, bf16[64,140...) custom-call(bf16[64,1408]{1,0:T(8,128)(2,1)} %get-tuple-element.192.refs_0_, ...), custom_call_target="tpu_custom_call" | custom-call | bytes 23100000 | tf_op jit(solution)/shard_map/cross_layer/pallas_call | solution.py:186
  170.9 8.4 %collective-permute-done.18.refs_1_ = bf16[64,1408]{1,0:T(8,128)(2,1)S(1)} collective-permute-done((bf16[64,1408]{1,0:T(8,128)(2,1)}, bf16[64,1408]{1,0:T(8,128)(2,1)S(1)}, u32[]{:S(2)}, u32[]{:S(2)}) %collective-permute-start.18) | collective-permute-done | bytes 180256 | tf_op jit(solution)/shard_map/ppermute | solution.py:70
  180.7 13.3 %feed_forward.1 = (bf16[256,1408]{1,0:T(8,128)(2,1)}, bf16[2,2,256,768]{3,2,1,0:T(8,128)(2,1)}, bf16[64,1408]{1,0:T(8,128)(2,1)}, bf16[64,1408]{1,0:T(8,128)(2,1...) custom-call(bf16[64,1408]{1,0:T(8,128)(2,1)} %get-tuple-element.203., ...), custom_call_target="tpu_custom_call" | custom-call | bytes 29700000 | tf_op jit(solution)/shard_map/feed_forward/pallas_call | solution.py:186
  197.1 7.1 %feed_forward_grads.1 = bf16[8,2,192,1408]{3,2,1,0:T(8,128)(2,1)} custom-call(bf16[2,2,256,768]{3,2,1,0:T(8,128)(2,1)} %get-tuple-element.209.acts_ref, bf16[256,1408]{1,0:T(8,128)(2,1)} %get-tuple-element.210.x_ref, bf16[256,1408]{1,0:T(8,128)(2,1)} %pad_maximum_fusion.3.refs_4_.cot_ref), custom_call_target="tpu_custom_call" | custom-call | bytes 23100000 | tf_op jit(solution)/shard_map/feed_forward_grads/pallas_call | solution.py:186
  223.4 11.3 %cross_layer_back.1 = (bf16[256,1408]{1,0:T(8,128)(2,1)}, bf16[256,352]{1,0:T(8,128)(2,1)}, bf16[352,352]{1,0:T(8,128)(2,1)}, bf16[352,352]{1,0:T(8,128)(2,1)}, ...) custom-call(bf16[64,1408]{1,0:T(8,128)(2,1)} %get-tuple-element.216., ...), custom_call_target="tpu_custom_call" | custom-call | bytes 33000000 | tf_op jit(solution)/shard_map/cross_layer_back/pallas_call | solution.py:186
  256.8 7.2 %text_layer_back.1.text_ref = bf16[8,2,96,1408]{3,2,1,0:T(8,128)(2,1)} custom-call(bf16[352,352]{1,0:T(8,128)(2,1)} %get-tuple-element.224.a_ref, bf16[352,352]{1,0:T(8,128)(2,1)} %get-tuple-element.225.b_ref, f32[333,176]{1,0:T(8,128)} %get-tuple-element.226.ua_ref, f32[333,176]{1,0:T(8,128)} %get-tuple-element.227.ub_ref, ...), custom_call_target="tpu_custom_call" | custom-call | bytes 29700000 | tf_op jit(solution)/shard_map/text_layer_back/pallas_call | solution.py:186
  265.4 10.5 %self_attention_back.1 = (bf16[256,1408]{1,0:T(8,128)(2,1)}, f32[256,352]{1,0:T(8,128)}, f32[256,704]{1,0:T(8,128)}, bf16[256,704]{1,0:T(8,128)(2,1)}, bf16[256,...) custom-call(bf16[64,1408]{1,0:T(8,128)(2,1)} %get-tuple-element.232.refs_0_, bf16[64,1408]{1,0:T(8,128)(2,1)} %copy-done.52, ...), custom_call_target="tpu_custom_call" | custom-call | bytes 29700000 | tf_op jit(solution)/shard_map/self_attention_back/pallas_call | solution.py:186
  280.6 9.2 %collective-permute-done.34.half_ref = bf16[256,704]{1,0:T(8,128)(2,1)S(1)} collective-permute-done((bf16[256,704]{1,0:T(8,128)(2,1)}, bf16[256,704]{1,0:T(8,128)(2,1)S(1)}, u32[]{:S(2)}, u32[]{:S(2)}) %collective-permute-start.34) | collective-permute-done | bytes 360480 | tf_op jit(solution)/shard_map/ppermute | solution.py:94
  289.8 8.6 %collective-permute-done.35.far_ref = bf16[256,704]{1,0:T(8,128)(2,1)S(1)} collective-permute-done((bf16[256,704]{1,0:T(8,128)(2,1)}, bf16[256,704]{1,0:T(8,128)(2,1)S(1)}, u32[]{:S(2)}, u32[]{:S(2)}) %collective-permute-start.35) | collective-permute-done | bytes 360480 | tf_op jit(solution)/shard_map/ppermute | solution.py:138
  304.9 12.3 %project_back.1 = (bf16[256,528]{1,0:T(8,128)(2,1)}, bf16[256,528]{1,0:T(8,128)(2,1)}, f32[1,88]{1,0:T(1,128)}, f32[1,88]{1,0:T(1,128)}, bf16[64,1408]{1,0:T(8,1...) custom-call(f32[256,704]{1,0:T(8,128)} %get-tuple-element.176.unit_ref, ...), custom_call_target="tpu_custom_call" | custom-call | bytes 26400000 | tf_op jit(solution)/shard_map/project_back/pallas_call | solution.py:186
  319.6 8.3 %late_grads.1 = bf16[8,2,240,1408]{3,2,1,0:T(8,128)(2,1)} custom-call(bf16[256,352]{1,0:T(8,128)(2,1)} %get-tuple-element.265.draw_ref, bf16[256,352]{1,0:T(8,128)(2,1)} %get-tuple-element.266.mixed_ref, bf16[256,1408]{1,0:T(8,128)(2,1)} %get-tuple-element.267.x_ref, bf16[256,1408]{1,0:T(8,128)(2,1)} %get-tuple-element.268.d_ref, ...), custom_call_target="tpu_custom_call" | custom-call | bytes 29700000 | tf_op jit(solution)/shard_map/late_grads/pallas_call | solution.py:186
  390.5 7.1 %collective-permute-done.51 = bf16[2,48,1408]{2,1,0:T(8,128)(2,1)S(1)} collective-permute-done((bf16[2,48,1408]{2,1,0:T(8,128)(2,1)S(1)}, bf16[2,48,1408]{2,1,0:T(8,128)(2,1)S(1)}, u32[]{:S(2)}, u32[]{:S(2)}) %collective-permute-start.51) | collective-permute-done | bytes 270368 | tf_op jit(solution)/shard_map/ppermute | solution.py:167
  397.6 8.4 %collective-permute-done.52 = bf16[2,48,1408]{2,1,0:T(8,128)(2,1)S(1)} collective-permute-done((bf16[2,48,1408]{2,1,0:T(8,128)(2,1)S(1)}, bf16[2,48,1408]{2,1,0:T(8,128)(2,1)S(1)}, u32[]{:S(2)}, u32[]{:S(2)}) %collective-permute-start.52) | collective-permute-done | bytes 270368 | tf_op jit(solution)/shard_map/ppermute | solution.py:167
  406.8 8.8 %reduce-scatter.5.cloned.1.call-done = bf16[480,1408]{1,0:T(8,128)(2,1)} async-done(((bf16[3840,1408]{1,0:T(8,128)(2,1)}), bf16[480,1408]{1,0:T(8,128)(2,1)}) %reduce-scatter.5.cloned.1.call-update) | async-done | bytes 1351696 | tf_op jit(solution)/shard_map/reduce_scatter | solution.py:151
  428.7 12.1 %joined_grads.1 = (f32[512,1408]{1,0:T(8,128)}, f32[512,1408]{1,0:T(8,128)}) custom-call(bf16[512,1408]{1,0:T(8,128)(2,1)} %copy-done.1, bf16[16,8,32,1408]{3,2,1,0:T(8,128)(2,1)} %all-gather.10.cloned.1.call-done.pack_ref), custom_call_target="tpu_custom_call" | custom-call | bytes 29700000 | tf_op jit(solution)/shard_map/joined_grads/pallas_call | solution.py:186
  443.0 17.4 %collective-permute-done.56 = bf16[288,1408]{1,0:T(8,128)(2,1)S(1)} collective-permute-done((bf16[288,1408]{1,0:T(8,128)(2,1)S(1)}, bf16[288,1408]{1,0:T(8,128)(2,1)S(1)}, u32[]{:S(2)}, u32[]{:S(2)}) %collective-permute-start.56) | collective-permute-done | bytes 811040 | tf_op jit(solution)/shard_map/ppermute | solution.py:143
  471.1 15.0 %collective-permute-done.60 = bf16[256,1408]{1,0:T(8,128)(2,1)S(1)} collective-permute-done((bf16[256,1408]{1,0:T(8,128)(2,1)S(1)}, bf16[256,1408]{1,0:T(8,128)(2,1)S(1)}, u32[]{:S(2)}, u32[]{:S(2)}) %collective-permute-start.60) | collective-permute-done | bytes 720928 | tf_op jit(solution)/shard_map/ppermute | solution.py:94
  486.4 6.6 %feed_forward_out.1 = (f32[1408,768]{1,0:T(8,128)}, f32[768,1408]{1,0:T(8,128)}) custom-call(bf16[8,192,1408]{2,1,0:T(8,128)(2,1)} %bitcast.78), custom_call_target="tpu_custom_call" | custom-call | bytes 19800000 | tf_op jit(solution)/shard_map/feed_forward_out/pallas_call | solution.py:186
  493.0 22.1 %all-gather.18.cloned.1.call-done = bf16[2304,1408]{1,0:T(8,128)(2,1)} async-done(((bf16[288,1408]{1,0:T(8,128)(2,1)}), bf16[2304,1408]{1,0:T(8,128)(2,1)}) %all-gather.18.cloned.1.call-update) | async-done | bytes 6488080 | tf_op jit(solution)/shard_map/all_gather | solution.py:157
  (406 shorter events, 281.3 us)
Async XLA Ops:
  7.2 70.4 %all-gather.12.cloned.1.call-start = ((), (), s32[]{:S(2)}) async-start(), calls=%async_computation.6 | async-start | bytes 4595712 | tf_op jit(solution)/shard_map/all_gather | solution.py:1049
  23.7 25.6 %collective-permute-start = (bf16[112,1408]{1,0:T(8,128)(2,1)S(1)}, bf16[112,1408]{1,0:T(8,128)(2,1)}, u32[]{:S(2)}, u32[]{:S(2)}) collective-permute-start(bf16[112,1408]{1,0:T(8,128)(2,1)S(1)} %pad_maximum_fusion.6), channel_id=1, source_target_pairs={{0,4},{1,5},{2,6},{3,7},{4,0},{5,1},{6,2},{7,3},{8,12},{9,13},{10,... | collective-permute-start | bytes 946184 | tf_op jit(solution)/shard_map/ppermute | solution.py:94
  31.7 26.6 %all-to-all-start = ((bf16[8,64,1408]{2,1,0:T(8,128)(2,1)}), bf16[8,64,1408]{2,1,0:T(8,128)(2,1)S(1)}, u32[]{:S(2)}, u32[]{:S(2)}) async-start(bf16[8,64,1408]{2,1,0:T(8,128)(2,1)} %bitcast), calls=%async_computation | async-start | bytes 2883584 | tf_op jit(solution)/shard_map/all_to_all | solution.py:41
  35.9 95.2 %all-gather.14.cloned.1.call-start = ((), (), s32[]{:S(2)}) async-start(), calls=%async_computation.7 | async-start | bytes 5361664 | tf_op jit(solution)/shard_map/all_gather | solution.py:1076
  63.3 14.3 %collective-permute-start.2 = (bf16[96,1408]{1,0:T(8,128)(2,1)}, bf16[96,1408]{1,0:T(8,128)(2,1)S(1)}, u32[]{:S(2)}, u32[]{:S(2)}) collective-permute-start(bf16[96,1408]{1,0:T(8,128)(2,1)} %get-tuple-element.172.refs_0_), channel_id=1, source_target_pairs={{0,2},{1,3},{2,0},{3,1},{4,6},{5,7},{6,4},{7,5},{8,10},{9,11},{10,... | collective-permute-start | bytes 811016 | tf_op jit(solution)/shard_map/ppermute | solution.py:70
  87.6 120.3 %all-gather.10.cloned.1.call-start = ((), (), s32[]{:S(2)}) async-start(), calls=%async_computation.3 | async-start | bytes 12255232 | tf_op jit(solution)/shard_map/all_gather | solution.py:1091
  89.4 13.0 %collective-permute-start.5 = (bf16[256,704]{1,0:T(8,128)(2,1)}, bf16[256,704]{1,0:T(8,128)(2,1)S(1)}, u32[]{:S(2)}, u32[]{:S(2)}) collective-permute-start(bf16[256,704]{1,0:T(8,128)(2,1)} %get-tuple-element.179.a_ref.refs_5_), channel_id=1, source_target_pairs={{0,8},{8,0},{16,24},{24,16},{32,40},{40,32},{48,56},{56,48},{64,72... | collective-permute-start | bytes 1081352 | tf_op jit(solution)/shard_map/ppermute | solution.py:99
  125.8 13.2 %collective-permute-start.14 = (bf16[128,1408]{1,0:T(8,128)(2,1)S(1)}, bf16[128,1408]{1,0:T(8,128)(2,1)S(1)}, u32[]{:S(2)}, u32[]{:S(2)}) collective-permute-start(bf16[128,1408]{1,0:T(8,128)(2,1)S(1)} %pad_maximum_fusion.5), channel_id=1, source_target_pairs={{0,4},{1,5},{2,6},{3,7},{4,0},{5,1},{6,2},{7,3},{8,12},{9,13},{10,... | collective-permute-start | bytes 1081352 | tf_op jit(solution)/shard_map/ppermute | solution.py:94
  140.1 161.3 %reduce-scatter.3.cloned.1.call-start = ((), (), s32[]{:S(2)}) async-start(), calls=%async_computation.4 | async-start | bytes 9732096 | tf_op jit(solution)/shard_map/reduce_scatter | solution.py:151
  208.5 207.0 %reduce-scatter.5.cloned.1.call-start = ((), (), s32[]{:S(2)}) async-start(), calls=%async_computation.5 | async-start | bytes 12165120 | tf_op jit(solution)/shard_map/reduce_scatter | solution.py:151
  279.5 18.9 %collective-permute-start.35 = (bf16[256,704]{1,0:T(8,128)(2,1)}, bf16[256,704]{1,0:T(8,128)(2,1)S(1)}, u32[]{:S(2)}, u32[]{:S(2)}) collective-permute-start(bf16[256,704]{1,0:T(8,128)(2,1)} %get-tuple-element.241), channel_id=1, source_target_pairs={{0,12},{1,13},{2,14},{3,15},{4,8},{5,9},{6,10},{7,11},{8,4},{9,5},... | collective-permute-start | bytes 1081352 | tf_op jit(solution)/shard_map/ppermute | solution.py:138
  298.4 18.9 %collective-permute-start.37 = (bf16[64,1408]{1,0:T(8,128)(2,1)S(1)}, bf16[64,1408]{1,0:T(8,128)(2,1)S(1)}, u32[]{:S(2)}, u32[]{:S(2)}) collective-permute-start(bf16[64,1408]{1,0:T(8,128)(2,1)S(1)} %copy-done.72), channel_id=1, source_target_pairs={{0,3},{1,0},{2,1},{3,2},{4,7},{5,4},{6,5},{7,6},{8,11},{9,8},{10,9... | collective-permute-start | bytes 540680 | tf_op jit(solution)/shard_map/ppermute | solution.py:75
  300.7 16.5 %collective-permute-start.38 = (bf16[64,1408]{1,0:T(8,128)(2,1)S(1)}, bf16[64,1408]{1,0:T(8,128)(2,1)S(1)}, u32[]{:S(2)}, u32[]{:S(2)}) collective-permute-start(bf16[64,1408]{1,0:T(8,128)(2,1)S(1)} %copy-done.71), channel_id=1, source_target_pairs={{0,2},{1,3},{2,0},{3,1},{4,6},{5,7},{6,4},{7,5},{8,10},{9,11},{10,... | collective-permute-start | bytes 540680 | tf_op jit(solution)/shard_map/ppermute | solution.py:75
  300.8 16.5 %collective-permute-start.39 = (bf16[64,1408]{1,0:T(8,128)(2,1)S(1)}, bf16[64,1408]{1,0:T(8,128)(2,1)S(1)}, u32[]{:S(2)}, u32[]{:S(2)}) collective-permute-start(bf16[64,1408]{1,0:T(8,128)(2,1)S(1)} %copy-done.70), channel_id=1, source_target_pairs={{0,1},{1,2},{2,3},{3,0},{4,5},{5,6},{6,7},{7,4},{8,9},{9,10},{10,1... | collective-permute-start | bytes 540680 | tf_op jit(solution)/shard_map/ppermute | solution.py:75
  302.5 14.9 %collective-permute-start.36 = (bf16[192,1408]{1,0:T(8,128)(2,1)S(1)}, bf16[192,1408]{1,0:T(8,128)(2,1)S(1)}, u32[]{:S(2)}, u32[]{:S(2)}) collective-permute-start(bf16[192,1408]{1,0:T(8,128)(2,1)S(1)} %slice.112), channel_id=1, source_target_pairs={{0,4},{1,5},{2,6},{3,7},{4,0},{5,1},{6,2},{7,3},{8,12},{9,13},{10,... | collective-permute-start | bytes 1622024 | tf_op jit(solution)/shard_map/ppermute | solution.py:94
  341.3 128.9 %all-gather.16.cloned.1.call-start = ((), (), s32[]{:S(2)}) async-start(), calls=%async_computation.8 | async-start | bytes 4866048 | tf_op jit(solution)/shard_map/all_gather | solution.py:157
  367.9 15.3 %collective-permute-start.47 = (bf16[2,192,1408]{2,1,0:T(8,128)(2,1)S(1)}, bf16[2,192,1408]{2,1,0:T(8,128)(2,1)S(1)}, u32[]{:S(2)}, u32[]{:S(2)}) collective-permute-start(bf16[2,192,1408]{2,1,0:T(8,128)(2,1)S(1)} %dynamic-slice_convert_fusion), channel_id=1, source_target_pairs={{0,8},{8,0},{16,24},{24,16},{32,40},{40,32},{48,56},{56,48},{64,72... | collective-permute-start | bytes 3244040 | tf_op jit(solution)/shard_map/ppermute | solution.py:167
  374.2 32.6 %collective-permute-start.54 = (bf16[256,1408]{1,0:T(8,128)(2,1)}, bf16[256,1408]{1,0:T(8,128)(2,1)}, u32[]{:S(2)}, u32[]{:S(2)}) collective-permute-start(bf16[256,1408]{1,0:T(8,128)(2,1)} %get-tuple-element.294), channel_id=1, source_target_pairs={{0,4},{1,5},{2,6},{3,7},{4,0},{5,1},{6,2},{7,3},{8,12},{9,13},{10,... | collective-permute-start | bytes 2162696 | tf_op jit(solution)/shard_map/ppermute | solution.py:94
  386.1 19.9 %collective-permute-start.52 = (bf16[2,48,1408]{2,1,0:T(8,128)(2,1)S(1)}, bf16[2,48,1408]{2,1,0:T(8,128)(2,1)S(1)}, u32[]{:S(2)}, u32[]{:S(2)}) collective-permute-start(bf16[2,48,1408]{2,1,0:T(8,128)(2,1)S(1)} %get-tuple-element.334), channel_id=1, source_target_pairs={{0,32},{8,40},{16,48},{24,56},{32,0},{40,8},{48,16},{56,24},{64,96... | collective-permute-start | bytes 811016 | tf_op jit(solution)/shard_map/ppermute | solution.py:167
  387.9 18.7 %collective-permute-start.53 = (bf16[2,48,1408]{2,1,0:T(8,128)(2,1)S(1)}, bf16[2,48,1408]{2,1,0:T(8,128)(2,1)S(1)}, u32[]{:S(2)}, u32[]{:S(2)}) collective-permute-start(bf16[2,48,1408]{2,1,0:T(8,128)(2,1)S(1)} %get-tuple-element.333), channel_id=1, source_target_pairs={{0,48},{8,56},{16,0},{24,8},{32,16},{40,24},{48,32},{56,40},{64,11... | collective-permute-start | bytes 811016 | tf_op jit(solution)/shard_map/ppermute | solution.py:167
  415.6 99.5 %all-gather.18.cloned.1.call-start = ((), (), s32[]{:S(2)}) async-start(), calls=%async_computation.9 | async-start | bytes 7299072 | tf_op jit(solution)/shard_map/all_gather | solution.py:157
  418.0 22.7 %collective-permute-start.55 = (bf16[288,1408]{1,0:T(8,128)(2,1)}, bf16[288,1408]{1,0:T(8,128)(2,1)}, u32[]{:S(2)}, u32[]{:S(2)}) collective-permute-start(bf16[288,1408]{1,0:T(8,128)(2,1)} %pad_maximum_fusion.2), channel_id=1, source_target_pairs={{0,4},{1,5},{2,6},{3,7},{4,0},{5,1},{6,2},{7,3},{8,12},{9,13},{10,... | collective-permute-start | bytes 2433032 | tf_op jit(solution)/shard_map/ppermute | solution.py:94
  442.2 18.1 %collective-permute-start.56 = (bf16[288,1408]{1,0:T(8,128)(2,1)S(1)}, bf16[288,1408]{1,0:T(8,128)(2,1)S(1)}, u32[]{:S(2)}, u32[]{:S(2)}) collective-permute-start(bf16[288,1408]{1,0:T(8,128)(2,1)S(1)} %convert_element_type.175), channel_id=1, source_target_pairs={{0,64},{8,72},{16,80},{24,88},{32,96},{40,104},{48,112},{56,120},{... | collective-permute-start | bytes 2433032 | tf_op jit(solution)/shard_map/ppermute | solution.py:143
  470.2 15.9 %collective-permute-start.60 = (bf16[256,1408]{1,0:T(8,128)(2,1)S(1)}, bf16[256,1408]{1,0:T(8,128)(2,1)S(1)}, u32[]{:S(2)}, u32[]{:S(2)}) collective-permute-start(bf16[256,1408]{1,0:T(8,128)(2,1)S(1)} %pad_maximum_fusion.4), channel_id=1, source_target_pairs={{0,4},{1,5},{2,6},{3,7},{4,0},{5,1},{6,2},{7,3},{8,12},{9,13},{10,... | collective-permute-start | bytes 2162696 | tf_op jit(solution)/shard_map/ppermute | solution.py:94
  (124 other events, 879.2 us)
Sparse Core Ops, SparseCore 0:
  20.7 55.8 all-gather.11
  87.7 39.6 all-gather.13
  140.2 67.6 all-gather.9
  210.2 53.4 reduce-scatter.2
  341.4 74.1 reduce-scatter.4
  417.8 33.2 all-gather.15
  470.4 44.6 all-gather.17

commit v3 on v2

--- a/solution.py
+++ b/solution.py
@@ -126,6 +126,13 @@
 
 def join(*values):
     return lax.optimization_barrier(values)
+
+
+def low_slice(rows, unit):
+    places = len(low_groups()[0])
+    each = -(-rows.shape[0] // (places * unit)) * unit
+    rows = pad_rows(rows, each * places)
+    return lax.dynamic_slice_in_dim(rows, lax.axis_index("dp") % places * each, each, 0)
 
 
 def far_swap(block):
@@ -593,8 +600,8 @@
     ) + (struct((rows, width), BF16),) * many
     ins = (*parts, cq_w, out_w, pack, pack, text, other_text, gain[None])
     specs = [HBM] * many + [whole(item.shape) for item in ins[many:]]
-    specs[many + 2] = pack_spec(each, width, 64)
-    specs[many + 3] = pack_spec(each, width, 80)
+    specs[many + 2] = pack_spec(each, width, 0)
+    specs[many + 3] = pack_spec(each, width, 16)
     return call(
         kernel, 7, outs, ins, "cross_layer", (1,), specs, tuple(whole(o.shape) for o in outs),
         (pltpu.SemaphoreType.DMA((many,)),),
@@ -648,8 +655,8 @@
     ) + (struct((rows, width), BF16),) * many
     ins = (*parts, raw, cq_w, out_w, pack, pack, text, other_text, gain[None])
     specs = [HBM] * many + [whole(item.shape) for item in ins[many:]]
-    specs[many + 3] = pack_spec(each, width, 64)
-    specs[many + 4] = pack_spec(each, width, 80)
+    specs[many + 3] = pack_spec(each, width, 0)
+    specs[many + 4] = pack_spec(each, width, 16)
     return call(
         kernel, 10, outs, ins, "cross_layer_back", (1,), specs,
         tuple(whole(o.shape) for o in outs),
@@ -763,47 +770,48 @@
     )
 
 
-def late_grads(draw, mixed_two, rows_two, grad_two, mine, other, mixed_one, rows_one, grad_one, texts):
+def put_shares(out_ref, shard, to, share, rows_ref):
+    stop, width = rows_ref.shape
+    for place in range(out_ref.shape[0]):
+        begin = min(place * share, stop)
+        count = min(share, stop - begin)
+        if count:
+            out_ref[place, shard, to : to + count] = rows_ref[begin : begin + count]
+        if count < share:
+            out_ref[place, shard, to + count : to + share] = jnp.zeros((share - count, width), BF16)
+
+
+def cross_grads(draw, mixed, rows_in, grad_rows, places, share):
     each = draw.shape[1] // 2
-    width = rows_two.shape[1]
+    width = rows_in.shape[1]
+
+    def kernel(draw_ref, mixed_ref, x_ref, d_ref, out_ref, hold_ref):
+        for s in range(2):
+            cut = slice(s * each, (s + 1) * each)
+            hold_ref[:each] = t_dot(draw_ref[:, cut], x_ref[...]).astype(BF16)
+            hold_ref[each:] = t_dot(mixed_ref[:, cut], d_ref[...]).astype(BF16)
+            put_shares(out_ref, s, 0, share, hold_ref)
+
+    ins = (draw, mixed, rows_in, grad_rows)
+    scratch = (pltpu.VMEM((2 * each, width), BF16),)
+    return call(kernel, 4, struct((places, 2, share, width), BF16), ins, "cross_grads", scratch=scratch)
+
+
+def self_grads(mine, other, mixed, rows_in, grad_rows, places, share):
     wide = mine.shape[1]
-    places, _, more, _ = texts.shape
-    first, second = 48, 96
-
-    def kernel(draw_ref, mixed_ref, x_ref, d_ref, mine_ref, other_ref, one_ref, y_ref, e_ref, text_ref, out_ref, hold_ref):
-        step = pl.program_id(0)
+    each = wide // 3
+    width = rows_in.shape[1]
+
+    def kernel(mine_ref, other_ref, mixed_ref, x_ref, d_ref, out_ref, hold_ref):
         for s, grad_ref in ((0, mine_ref), (1, other_ref)):
-
-            @pl.when(step == s)
-            def _(s=s, grad_ref=grad_ref):
-                cut = slice(s * each, (s + 1) * each)
-                hold_ref[:each] = t_dot(draw_ref[:, cut], x_ref[...]).astype(BF16)
-                hold_ref[each : 2 * each] = t_dot(mixed_ref[:, cut], d_ref[...]).astype(BF16)
-                hold_ref[2 * each : 2 * each + wide] = t_dot(grad_ref[...], y_ref[...]).astype(BF16)
-                hold_ref[2 * each + wide :] = t_dot(one_ref[:, cut], e_ref[...]).astype(BF16)
-
-        for place in range(places):
-            for share, start, stop, to in (
-                (first, 0, 2 * each, 0),
-                (second, 2 * each, 3 * each + wide, first),
-            ):
-                begin = min(start + place * share, stop)
-                count = min(share, stop - begin)
-                out_ref[place, 0, to : to + count] = hold_ref[begin : begin + count]
-                if count < share:
-                    blank = jnp.zeros((share - count, width), BF16)
-                    out_ref[place, 0, to + count : to + share] = blank
-            out_ref[place, 0, first + second :] = text_ref[place, 0]
-
-    ins = (draw, mixed_two, rows_two, grad_two, mine, other, mixed_one, rows_one, grad_one, texts)
-    rows = first + second + more
-    return call(
-        kernel, 9, struct((places, 2, rows, width), BF16), ins, "late_grads", (2,),
-        [whole(item.shape) for item in ins[:-1]]
-        + [pl.BlockSpec((places, 1, more, width), lambda s: (0, s, 0, 0))],
-        pl.BlockSpec((places, 1, rows, width), lambda s: (0, s, 0, 0)),
-        (pltpu.VMEM((3 * each + wide, width), BF16),),
-    )
+            cut = slice(s * each, (s + 1) * each)
+            hold_ref[:wide] = t_dot(grad_ref[...], x_ref[...]).astype(BF16)
+            hold_ref[wide:] = t_dot(mixed_ref[:, cut], d_ref[...]).astype(BF16)
+            put_shares(out_ref, s, 0, share, hold_ref)
+
+    ins = (mine, other, mixed, rows_in, grad_rows)
+    scratch = (pltpu.VMEM((wide + each, width), BF16),)
+    return call(kernel, 5, struct((places, 2, share, width), BF16), ins, "self_grads", scratch=scratch)
 
 
 def skip_grads(parts, joined_own, joined_other, long):
@@ -838,8 +846,7 @@
 
 def joined_grads(rows_in, pack, slab):
     tokens, width = rows_in.shape
-    _, count, deep, _ = pack.shape
-    held = slab // deep
+    held, count, deep, _ = pack.shape
     half = count // 2
 
     def kernel(x_ref, pack_ref, one_ref, two_ref):
@@ -848,7 +855,7 @@
             @pl.when(pl.program_id(0) == step)
             def _(out_ref=out_ref):
                 for j in range(half):
-                    weight = pack_ref[:, j].reshape(slab, width)
+                    weight = pack_ref[:, j].reshape(held * deep, width)[:slab]
                     out_ref[:, j * slab : (j + 1) * slab] = dot_t(x_ref[...], weight)
 
     outs = (struct((tokens, width), F32), struct((tokens, width), F32))
@@ -862,8 +869,8 @@
     )
 
 
-def feed_forward_out(sums):
-    places, share, width = sums.shape
+def feed_forward_out(sums, share):
+    places, _, width = sums.shape
     half = places // 2
     hidden = half * share
 
@@ -929,18 +936,18 @@
     )
 
 
-def text_layer_back(pairs, units, scales, tokens, ckvs, gain, places):
+def text_layer_back(crosses, pairs, units, scales, tokens, ckvs, gain):
     count, width = tokens.shape
     both = ckvs[0].shape[1]
     each = both // 2
     head = gain.shape[0]
     heads = each // head
-    wide = 4 * both
+    places, _, first, wide = crosses.shape
     deep = 48
     more = 48
     long = more * places
 
-    def kernel(a_ref, b_ref, ua_ref, ub_ref, sa_ref, sb_ref, x_ref, wa_ref, wb_ref, gain_ref, out_ref, dw_ref, grad_ref, part_ref):
+    def kernel(first_ref, a_ref, b_ref, ua_ref, ub_ref, sa_ref, sb_ref, x_ref, wa_ref, wb_ref, gain_ref, out_ref, dw_ref, grad_ref, part_ref):
         dgain = jnp.zeros((1, head), F32)
         part = jnp.zeros((count, width), F32)
         for s, (pair_ref, unit_ref, scale_ref, w_ref) in enumerate(
@@ -959,24 +966,25 @@
             for place in range(places):
                 begin = min(place * deep, both)
                 held = min(deep, both - begin)
-                out_ref[place, s, :deep] = jnp.zeros((deep, wide), BF16)
-                out_ref[place, s, :held, :width] = dw_ref[begin : begin + held]
+                out_ref[place, s, :first] = first_ref[place, s]
+                out_ref[place, s, first : first + deep] = jnp.zeros((deep, wide), BF16)
+                out_ref[place, s, first : first + held, :width] = dw_ref[begin : begin + held]
         part_ref[...] = jnp.zeros_like(part_ref)
         part_ref[:count, :width] = part
         part_ref[long - 1 :, :head] = dgain
         for place in range(places):
             rows = part_ref[place * more : (place + 1) * more].astype(BF16)
             for s in range(2):
-                out_ref[place, s, deep : deep + more] = rows
-
-    ins = (*pairs, *units, *scales, tokens, *ckvs, gain[None])
+                out_ref[place, s, first + deep :] = rows
+
+    ins = (crosses, *pairs, *units, *scales, tokens, *ckvs, gain[None])
     scratch = (
         pltpu.VMEM((both, width), BF16),
         pltpu.VMEM((count, both), BF16),
         pltpu.VMEM((long, wide), F32),
     )
     return call(
-        kernel, 9, struct((places, 2, deep + more, wide), BF16), ins, "text_layer_back", scratch=scratch
+        kernel, 9, struct((places, 2, first + deep + more, wide), BF16), ins, "text_layer_back", scratch=scratch
     )
 
 
@@ -1044,8 +1052,7 @@
     dp_place = lax.axis_index("dp")
     qkv_flat = qkv_w.transpose(1, 2, 0).reshape(qkv_rows, model_width)
     cq_turned = cq_w.T
-    shares = [dp_slice(qkv_flat, 48)]
-    shares += [dp_slice(rows, 16) for rows in (attn_out_w, cq_turned, cross_out_w)]
+    shares = [dp_slice(qkv_flat, 48), dp_slice(attn_out_w, 16)]
     pack = lax.all_gather(half_swap(jnp.concatenate(shares, 0)), "dp", axis=0, tiled=False)
     ckv_flat = ckv_w.reshape(text_width, 2 * local_width)
     text_pair, text_units, text_scales = text_layer(
@@ -1053,55 +1060,65 @@
     )
     share = hidden_width // dp_count
     deep = text_width // dp_count // 4
+    share = hidden_width // low_count
+    low_place = dp_place % low_count
     ff_share = [
-        lax.dynamic_slice_in_dim(fc1_w, dp_place * share, share, 1).T,
-        lax.dynamic_slice_in_dim(fc2_w, dp_place * share, share, 0),
+        lax.dynamic_slice_in_dim(fc1_w, low_place * share, share, 1).T,
+        lax.dynamic_slice_in_dim(fc2_w, low_place * share, share, 0),
     ]
+    ff_share = jnp.concatenate(ff_share, 0)
     ckv_share = lax.dynamic_slice_in_dim(ckv_flat, dp_place * 4 * deep, 4 * deep, 0)
-    ff_share.append(jnp.concatenate(jnp.split(ckv_share, 4), 1))
-    ff_share = half_swap(jnp.concatenate(ff_share, 0))
+    cross_share = [dp_slice(rows, 16) for rows in (cq_turned, cross_out_w)]
+    cross_share.append(jnp.concatenate(jnp.split(ckv_share, 4), 1))
+    cross_share = jnp.concatenate(cross_share, 0)
     silu_cond = jax.nn.silu(condition.astype(F32)).astype(BF16)
     shift = jnp.dot(silu_cond[None], mod_w, preferred_element_type=F32)[0]
     cos_wide, sin_wide = rotary_tables(ring_rows(positions, half), head_dim)
     cot_rows = ring_rows(cotangent, half)
-    got, qkv_flat, cos_wide, sin_wide, shift, text_pair, cot_rows, ff_share = join(
-        got, qkv_flat, cos_wide, sin_wide, shift, text_pair, cot_rows, ff_share
-    )
-    skip_share = dp_slice(skip_w, 32)
+    got, cos_wide, sin_wide, shift, text_pair, cot_rows, ff_share, cross_share = join(
+        got, cos_wide, sin_wide, shift, text_pair, cot_rows, ff_share, cross_share
+    )
+    skip_share = low_slice(skip_w, 16)
     merged, hidden_zero, normed = first_norms(got, skip_gain, norm1_gain, shift, skip_share)
     normed_parts = ring_gather(normed)
+    cross_share = half_swap(after(cross_share, normed))
     rows_one, units, scales, queries, own_pair = project(
         normed_parts, qkv_flat, pack, cos_wide, sin_wide, qnorm_gain, knorm_gain
     )
-    ff_pack = lax.all_gather(after(ff_share, rows_one), "dp", axis=0, tiled=False)
+    own_pair, cross_share = join(own_pair, cross_share)
+    cross_pack = lax.all_gather(cross_share, "dp", axis=0, tiled=False)
     core_pair = core_swap(own_pair)
     half_pair = half_swap(own_pair)
     pairs = (own_pair, core_pair, half_pair, core_swap(half_pair))
     mixed_one, totals, *partial = self_attention(
         queries, pairs, attn_out_w, pack, head_dim
     )
+    ff_share = half_swap(after(ff_share, half_pair))
     hidden_one, normed = mid_norm(ring_scatter(partial), hidden_zero, norm2_gain)
+    ff_pack = gather_low(after(ff_share, normed))
     skip_rows = jnp.concatenate([part[part_count:] for part in normed_parts], 0)
     skip_half = half_swap(after(skip_rows, normed))
     other_text, other_units, other_scales, other_ckv = text_layer(
-        text_tokens, after(ff_pack, normed), cknorm_gain, model_width // 4
-    )
-    *normed_parts, skip_half, other_text = join(*ring_gather(normed), skip_half, other_text)
-    skip_rows = place_blocks(jnp.split(skip_rows, ring), jnp.split(skip_half, ring))
-    skip_pack = lax.all_gather(
-        skip_rows.reshape(tensor_count, -1, model_width), "dp", axis=0, tiled=False
-    )
+        text_tokens, after(cross_pack, normed), cknorm_gain, model_width // 4
+    )
+    *normed_parts, other_text = join(*ring_gather(normed), other_text)
     rows_two, cross_raw, mixed_two, *partial = cross_layer(
         normed_parts,
         cq_turned,
         cross_out_w,
-        pack,
+        cross_pack,
         text_pair,
         other_text,
         cqnorm_gain,
         text_count,
     )
-    hidden_two, normed = mid_norm(ring_scatter(partial), hidden_one, norm3_gain)
+    *partial, skip_half = join(*partial, skip_half)
+    skip_rows = place_blocks(jnp.split(skip_rows, ring), jnp.split(skip_half, ring))
+    *pieces, skip_rows = join(*ring_scatter(partial), skip_rows)
+    hidden_two, normed = mid_norm(pieces, hidden_one, norm3_gain)
+    skip_pack = gather_low(
+        skip_rows.reshape(tensor_count, -1, model_width)
+    )
     rows_three, acts, *partial = feed_forward(
         ring_gather(normed), cot_rows, fc1_w, fc2_w, ff_pack
     )
@@ -1119,25 +1136,28 @@
         cross_raw,
         cq_turned,
         cross_out_w,
-        pack,
+        cross_pack,
         text_pair,
         other_text,
         cqnorm_gain,
         text_count,
     )
-    residual, out_grad, norm2_grad = mid_norm_back(
-        ring_scatter(partial), residual, hidden_one, norm2_gain
-    )
-    text_sums = text_layer_back(
+    crosses = cross_grads(
+        cross_raw_grad, mixed_two, rows_two, grad_rows_two, low_count, 48
+    )
+    *pieces, crosses = join(*ring_scatter(partial), crosses)
+    residual, out_grad, norm2_grad = mid_norm_back(pieces, residual, hidden_one, norm2_gain)
+    early_sums = text_layer_back(
+        crosses,
         (text_own, text_other),
         (text_units, other_units),
         (text_scales, other_scales),
         after(text_tokens, out_grad),
         (ckv_flat, other_ckv),
         cknorm_gain,
-        low_count,
-    )
-    *out_parts, text_sums = join(*ring_gather(out_grad), text_sums)
+    )
+    *out_parts, early_sums, fc_grads = join(*ring_gather(out_grad), early_sums, fc_grads)
+    early_sums = scatter_low(early_sums.reshape(-1, model_width))
     grad_rows_one, query_grad, pair_grad, half_grad, core_grad, far_grad = self_attention_back(
         queries,
         pairs,
@@ -1154,9 +1174,6 @@
     fc_grads = after(fc_grads, half_grad)
     share = fc_grads.shape[0] // 2
     fc_grads = half_sum(fc_grads[:share], fc_grads[share:])
-    output = hidden_two
-    for piece in ring_scatter(after_all(last_partial, half_grad)):
-        output = output + piece.astype(F32)
     projected_grad, projected_other, qnorm_grad, knorm_grad, *partial = project_back(
         units,
         scales,
@@ -1172,23 +1189,18 @@
         qkv_flat,
         pack,
     )
-    *partial, fc_grads, output = join(*partial, fc_grads, output)
+    *partial, fc_grads = join(*partial, fc_grads)
     fc_grads = fc_grads + low_swap(fc_grads.astype(BF16)).astype(F32)
-    late_sums = late_grads(
-        cross_raw_grad,
-        mixed_two,
-        rows_two,
-        grad_rows_two,
-        projected_grad,
-        projected_other,
-        mixed_one,
-        rows_one,
-        grad_rows_one,
-        text_sums,
-    )
-    late_sums = late_sums.reshape(-1, model_width)
-    *pieces, late_sums, fc_grads = join(*ring_scatter(partial), late_sums, fc_grads)
-    late_sums = scatter_low(late_sums)
+    late_sums = self_grads(
+        projected_grad, projected_other, mixed_one, rows_one, grad_rows_one, low_count, 96
+    )
+    early_sums = after(early_sums, qnorm_grad)
+    early_share = early_sums.shape[0] // 2
+    early_sums = half_sum(early_sums[:early_share], early_sums[early_share:])
+    *pieces, late_sums, fc_grads, early_sums = join(
+        *ring_scatter(partial), late_sums, fc_grads, early_sums
+    )
+    late_sums = scatter_low(late_sums.reshape(-1, model_width))
     misc = jnp.concatenate([qnorm_grad, knorm_grad, cqnorm_grad], 1)
     misc = jnp.pad(misc, ((0, 0), (0, model_width - misc.shape[1])))
     merged_out = last_norms(
@@ -1206,50 +1218,80 @@
     joined_other = lax.dynamic_slice_in_dim(
         joined_rows, (tensor_place + ring) % tensor_count * slab_width, slab_width, 1
     )
-    *merged_parts, joined_own, joined_other = join(
-        *ring_gather(merged_out), joined_own, joined_other
-    )
+    merged_out, early_sums = join(merged_out, early_sums)
+    early_sums = early_sums + low_swap(early_sums.astype(BF16)).astype(F32)
+    *merged_parts, joined_own, joined_other, early_sums = join(
+        *ring_gather(merged_out), joined_own, joined_other, early_sums
+    )
+
+    text_rows = early_sums[-48:]
+    for part in ring_gather(text_rows.astype(BF16))[1:]:
+        text_rows = text_rows + part.astype(F32)
 
     last_rows = -(-(slab_width + 16) // (8 * dp_count)) * 8 * dp_count
     merged_rows, last_sums = skip_grads(merged_parts, joined_own, joined_other, last_rows)
+    merged_rows, last_sums, text_rows = join(merged_rows, last_sums, text_rows)
+    early_sums = jnp.concatenate([fc_grads, early_sums[:-48], text_rows], 0).astype(BF16)
+    early_sums = gather_low(after(early_sums, late_sums))
     merged_half = half_swap(merged_rows)
     last_sums = scatter_stage(0, last_sums)
-    output = jnp.concatenate(ring_gather(after(output.astype(BF16), merged_rows)), 0)
+    last_sums, merged_half = join(last_sums, merged_half)
+    last_sums = scatter_stage(1, last_sums)
+    output = hidden_two
+    for piece in ring_scatter(after_all(last_partial, merged_half)):
+        output = output + piece.astype(F32)
     last_sums, output = join(last_sums, output)
-    last_sums = scatter_stage(1, last_sums)
-    output_half = half_swap(output)
-    last_sums, merged_half, late_sums = join(last_sums, merged_half, late_sums)
-    fc_grads = gather_low(after(fc_grads.astype(BF16), late_sums))
     share = late_sums.shape[0] // 2
     own_sums = jnp.concatenate([late_sums[:share].astype(F32), last_sums[0]], 0)
     other_sums = jnp.concatenate([late_sums[share:], last_sums[1].astype(BF16)], 0)
     last_sums = half_sum(own_sums, other_sums)
+    output = jnp.concatenate(ring_gather(output.astype(BF16)), 0)
+    last_sums, output = join(last_sums, output)
+    last_sums = last_sums + low_swap(last_sums.astype(BF16)).astype(F32)
     merged_grad = place_blocks(jnp.split(merged_rows, ring), jnp.split(merged_half, ring))
     latent_grad, skip_grad = joined_grads(merged_grad, skip_pack, slab_width)
-    last_sums, latent_grad, skip_grad = join(last_sums, latent_grad, skip_grad)
-    last_sums = last_sums + low_swap(last_sums.astype(BF16)).astype(F32)
-    text_share = slice(share - 48, share)
-    text_parts = ring_gather(last_sums[text_share].astype(BF16))
-    text_rows = last_sums[text_share]
-    for part in text_parts[1:]:
-        text_rows = text_rows + part.astype(F32)
-    last_sums = jnp.concatenate([last_sums[: share - 48], text_rows, last_sums[share:]], 0)
-    last_sums, fc_grads = join(last_sums, fc_grads)
-    last_sums = gather_low(last_sums.astype(BF16))
-    fc1_grad, fc2_grad = feed_forward_out(fc_grads)
+    last_sums = gather_low(after(last_sums, early_sums).astype(BF16))
+    output_half = half_swap(after(output, early_sums))
+    fc_share = fc_grads.shape[0]
+    fc1_grad, fc2_grad = feed_forward_out(early_sums, fc_share)
     output = place_blocks(jnp.split(output, ring), jnp.split(output_half, ring))
-    last_sums, output, fc1_grad, fc2_grad = join(last_sums, output, fc1_grad, fc2_grad)
-    cross_sums = last_sums[:, :48].reshape(-1, model_width)
+    cross_sums = early_sums[:, fc_share : fc_share + 48].reshape(-1, model_width)
     cq_grad = cross_sums[:local_width].T.astype(F32)
     cross_out_grad = cross_sums[local_width : 2 * local_width].astype(F32)
-    self_sums = last_sums[:, 48:144].reshape(-1, model_width)
+    ckv_grad = early_sums[:, fc_share + 48 : fc_share + 96].reshape(-1, model_width)
+    ckv_grad = ckv_grad[: 2 * local_width, :text_width].astype(F32)
+    ckv_grad = ckv_grad.T.reshape(text_width, 2, local_width)
+    text_rows = early_sums[:, fc_share + 96 :].reshape(-1, model_width).astype(F32)
+    text_grad = text_rows[:text_count, :text_width]
+    cknorm_grad = text_rows[-1, :head_dim]
+    (
+        last_sums,
+        latent_grad,
+        skip_grad,
+        output,
+        fc1_grad,
+        fc2_grad,
+        cq_grad,
+        cross_out_grad,
+        ckv_grad,
+        text_grad,
+        cknorm_grad,
+    ) = join(
+        last_sums,
+        latent_grad,
+        skip_grad,
+        output,
+        fc1_grad,
+        fc2_grad,
+        cq_grad,
+        cross_out_grad,
+        ckv_grad,
+        text_grad,
+        cknorm_grad,
+    )
+    self_sums = last_sums[:, :share].reshape(-1, model_width)
     qkv_grad = self_sums[:qkv_rows].T.astype(F32).reshape(model_width, 3, local_width)
     attn_out_grad = self_sums[qkv_rows : qkv_rows + local_width].astype(F32)
-    ckv_grad = last_sums[:, 144:192].reshape(-1, model_width)[: 2 * local_width, :text_width]
-    ckv_grad = ckv_grad.astype(F32).T.reshape(text_width, 2, local_width)
-    text_rows = last_sums[:, text_share].reshape(-1, model_width).astype(F32)
-    text_grad = text_rows[:text_count, :text_width]
-    cknorm_grad = text_rows[-1, :head_dim]
     last_sums = last_sums[:, share:].reshape(4, 2, -1, model_width).transpose(1, 0, 2, 3)
     last_sums = last_sums.reshape(-1, model_width)
     skip_w_grad = last_sums[:slab_width].astype(F32)

time: 550 us -> 522 us (0.949)
  waiting for transfers between devices: 207 us -> 176 us
  starting transfers between devices: 95.3 us -> 103 us
    ppermute x9 -> x11, waiting for transfers between devices: 36.8 us -> 51.3 us  [half_swap(): lax.ppermute(block, 'tensor', [(i, (i + count // 2) % count) for i in ran...]
    ppermute x2 -> x3, waiting for transfers between devices: 17.4 us -> 2.93 us  [low_swap(): return lax.ppermute(block, 'dp', [(i, i ^ 8) for i in range(count)])]
    all_to_all x1, waiting for transfers between devices: 8.99 us -> 1.04 us  [exchange(): return lax.all_to_all(blocks, axis, 0, 0, tiled=True)]
    reduce_scatter x2 -> x3, waiting for transfers between devices: 8.8 us -> 1.02 us  [scatter_low(): lax.psum_scatter(rows, 'dp', scatter_dimension=0, tiled=True, axis_index_...]
    ppermute x18, waiting for transfers between devices: 41 us -> 34.3 us  [ring_scatter(): lax.ppermute(blocks[k], 'tensor', ring_route(-k))]
    all_gather x2 -> x4, waiting for transfers between devices: 22.1 us -> 17.6 us  [gather_low(): lax.all_gather(rows, 'dp', axis=0, tiled=False, axis_index_groups=low_gro...]
    ppermute x9 -> x11, starting transfers between devices: 19.5 us -> 23.5 us  [half_swap(): lax.ppermute(block, 'tensor', [(i, (i + count // 2) % count) for i in ran...]
    pallas_call x21 -> x22, Pallas kernels: 144 us -> 146 us  [call(): pl.pallas_call(kernel, out_shape=outs, scratch_shapes=scratch, compiler_p...]
  transfers between devices with their start and end apart: 69 -> 74, of which waited for: 40 -> 38; matrix products, arithmetic and copies ran while one was open for 8% -> 9% of each run, Pallas kernels for 25% -> 28%
where the time goes in v3:
time: 522 us; the launch traced here: 512 us
  waiting for transfers between devices  176 us (34%)
  Pallas kernels  146 us (28%)
  starting transfers between devices  103 us (20%)
  local copies, waits for them, and re-layouts  50.5 us (10%)
  other arithmetic  19.2 us (4%)
  between operations  15.4 us (3%)
    pallas_call x22, Pallas kernels, call(): pl.pallas_call(kernel, out_shape=outs, scratch_shapes=scratch, compiler_p...  146 us
    ppermute x11, waiting for transfers between devices, half_swap(): lax.ppermute(block, 'tensor', [(i, (i + count // 2) % count) for i in ran...  51.3 us
    ppermute x24, waiting for transfers between devices, ring_gather(): got = {k: lax.ppermute(block, 'tensor', ring_route(k)) for k in (1, 3, 2)}  43 us
    ppermute x18, waiting for transfers between devices, ring_scatter(): lax.ppermute(blocks[k], 'tensor', ring_route(-k))  34.3 us
    ppermute x24, starting transfers between devices, ring_gather(): got = {k: lax.ppermute(block, 'tensor', ring_route(k)) for k in (1, 3, 2)}  31.6 us
    ppermute x18, starting transfers between devices, ring_scatter(): lax.ppermute(blocks[k], 'tensor', ring_route(-k))  23.9 us
    ppermute x11, starting transfers between devices, half_swap(): lax.ppermute(block, 'tensor', [(i, (i + count // 2) % count) for i in ran...  23.5 us
    all_gather x4, waiting for transfers between devices, gather_low(): lax.all_gather(rows, 'dp', axis=0, tiled=False, axis_index_groups=low_gro...  17.6 us
  transfers between devices with their start and end apart: 74, of which 38 were waited for; matrix products, arithmetic and copies ran while one was open for 9% of the time, Pallas kernels for 28%

profile of v3, /device:TPU:1, one launch (start us, length us, event | category | flops | bytes accessed | tf_op | source)
XLA Modules:
  0.0 512.1 jit_solution(582126667969965558)
XLA Ops:
  23.9 6.5 %all-to-all-start = ((bf16[8,64,1408]{2,1,0:T(8,128)(2,1)}), bf16[8,64,1408]{2,1,0:T(8,128)(2,1)S(1)}, u32[]{:S(2)}, u32[]{:S(2)}) async-start(bf16[8,64,1408]{2,1,0:T(8,128)(2,1)} %bitcast), calls=%async_computation | async-start | bytes 2883584 | tf_op jit(solution)/shard_map/all_to_all | solution.py:41
  65.4 8.9 %collective-permute-done.1.refs_2_ = bf16[112,1408]{1,0:T(8,128)(2,1)S(1)} collective-permute-done((bf16[112,1408]{1,0:T(8,128)(2,1)}, bf16[112,1408]{1,0:T(8,128)(2,1)S(1)}, u32[]{:S(2)}, u32[]{:S(2)}) %collective-permute-start.1) | collective-permute-done | bytes 315424 | tf_op jit(solution)/shard_map/ppermute | solution.py:70
  75.2 9.3 %project.1 = (bf16[256,1408]{1,0:T(8,128)(2,1)}, f32[256,704]{1,0:T(8,128)}, f32[256,8]{1,0:T(8,128)}, bf16[256,352]{1,0:T(8,128)(2,1)}, bf16[256,704]{1,0:T(8,128)(2,1)}) custom-call(bf16[112,1408]{1,0:T(8,128)(2,1)} %get-tuple-element.202.refs_0_, bf16[112,1408]{1,0:T(8,128)(2,1)} %copy-done.20, bf16[112,1408]{1,0:T(8,128)(2,1)} %copy-done.18, ...), custom_call_target="tpu_custom_call" | custom-call | bytes 19800000 | tf_op jit(solution)/shard_map/project/pallas_call | solution.py:193
  87.7 7.9 %collective-permute-done.6.c_ref.refs_7_ = bf16[256,704]{1,0:T(8,128)(2,1)S(1)} collective-permute-done((bf16[256,704]{1,0:T(8,128)(2,1)}, bf16[256,704]{1,0:T(8,128)(2,1)S(1)}, u32[]{:S(2)}, u32[]{:S(2)}) %collective-permute-start.6) | collective-permute-done | bytes 360480 | tf_op jit(solution)/shard_map/ppermute | solution.py:94
  100.7 7.3 %self_attention.1 = (bf16[256,352]{1,0:T(8,128)(2,1)}, f32[256,4]{1,0:T(8,128)}, bf16[64,1408]{1,0:T(8,128)(2,1)}, bf16[64,1408]{1,0:T(8,128)(2,1)}, bf16[64,1408]{1,0:T(8,128)(2,1)}, /*index=5*/bf16[64,1408]{1,0:T(8,128)(2,1)}) custom-call(bf16[256,352]{1,0:T(8,128)(2,1)} %get-tuple-element.207.q_ref.refs_4_, ...), custom_call_target="tpu_custom_call" | custom-call | bytes 16500000 | tf_op jit(solution)/shard_map/self_attention/pallas_call | solution.py:193
  113.9 6.5 %collective-permute-done.8.refs_1_ = bf16[64,1408]{1,0:T(8,128)(2,1)S(1)} collective-permute-done((bf16[64,1408]{1,0:T(8,128)(2,1)}, bf16[64,1408]{1,0:T(8,128)(2,1)S(1)}, u32[]{:S(2)}, u32[]{:S(2)}) %collective-permute-start.8) | collective-permute-done | bytes 180256 | tf_op jit(solution)/shard_map/ppermute | solution.py:75
  142.7 10.0 %cross_layer.1 = (bf16[256,1408]{1,0:T(8,128)(2,1)}, f32[256,352]{1,0:T(8,128)}, bf16[256,352]{1,0:T(8,128)(2,1)}, bf16[64,1408]{1,0:T(8,128)(2,1)}, bf16[64,140...) custom-call(bf16[64,1408]{1,0:T(8,128)(2,1)} %get-tuple-element.221.refs_0_, ...), custom_call_target="tpu_custom_call" | custom-call | bytes 23100000 | tf_op jit(solution)/shard_map/cross_layer/pallas_call | solution.py:193
  157.3 6.7 %collective-permute-done.15.refs_1_ = bf16[64,1408]{1,0:T(8,128)(2,1)S(1)} collective-permute-done((bf16[64,1408]{1,0:T(8,128)(2,1)}, bf16[64,1408]{1,0:T(8,128)(2,1)S(1)}, u32[]{:S(2)}, u32[]{:S(2)}) %collective-permute-start.15) | collective-permute-done | bytes 180256 | tf_op jit(solution)/shard_map/ppermute | solution.py:75
  173.5 8.5 %collective-permute-done.18.refs_1_ = bf16[64,1408]{1,0:T(8,128)(2,1)S(1)} collective-permute-done((bf16[64,1408]{1,0:T(8,128)(2,1)}, bf16[64,1408]{1,0:T(8,128)(2,1)S(1)}, u32[]{:S(2)}, u32[]{:S(2)}) %collective-permute-start.18) | collective-permute-done | bytes 180256 | tf_op jit(solution)/shard_map/ppermute | solution.py:70
  182.8 13.6 %feed_forward.1 = (bf16[256,1408]{1,0:T(8,128)(2,1)}, bf16[2,2,256,768]{3,2,1,0:T(8,128)(2,1)}, bf16[64,1408]{1,0:T(8,128)(2,1)}, bf16[64,1408]{1,0:T(8,128)(2,1...) custom-call(bf16[64,1408]{1,0:T(8,128)(2,1)} %get-tuple-element.242., ...), custom_call_target="tpu_custom_call" | custom-call | bytes 29700000 | tf_op jit(solution)/shard_map/feed_forward/pallas_call | solution.py:193
  200.1 7.1 %feed_forward_grads.1 = bf16[8,2,192,1408]{3,2,1,0:T(8,128)(2,1)} custom-call(bf16[2,2,256,768]{3,2,1,0:T(8,128)(2,1)} %get-tuple-element.251.acts_ref, bf16[256,1408]{1,0:T(8,128)(2,1)} %get-tuple-element.252.x_ref, bf16[256,1408]{1,0:T(8,128)(2,1)} %pad_maximum_fusion.2.refs_4_.cot_ref), custom_call_target="tpu_custom_call" | custom-call | bytes 23100000 | tf_op jit(solution)/shard_map/feed_forward_grads/pallas_call | solution.py:193
  210.9 6.0 %all-gather.12.cloned.1.call-done.pack_ref = bf16[8,8,48,1408]{3,2,1,0:T(8,128)(2,1)} async-done(((bf16[1,8,48,1408]{3,2,1,0:T(8,128)(2,1)}), bf16[8,8,48,1408]{3,2,1,0:T(8,128)(2,1)}) %all-gather.12.cloned.1.call-update) | async-done | bytes 8650768 | tf_op jit(solution)/shard_map/all_gather | solution.py:164
  232.4 11.4 %cross_layer_back.1 = (bf16[256,1408]{1,0:T(8,128)(2,1)}, bf16[256,352]{1,0:T(8,128)(2,1)}, bf16[352,352]{1,0:T(8,128)(2,1)}, bf16[352,352]{1,0:T(8,128)(2,1)}, ...) custom-call(bf16[64,1408]{1,0:T(8,128)(2,1)} %get-tuple-element.258., ...), custom_call_target="tpu_custom_call" | custom-call | bytes 33000000 | tf_op jit(solution)/shard_map/cross_layer_back/pallas_call | solution.py:193
  264.5 8.7 %text_layer_back.1 = bf16[8,2,144,1408]{3,2,1,0:T(8,128)(2,1)} custom-call(bf16[8,2,48,1408]{3,2,1,0:T(8,128)(2,1)} %cross_grads.1.first_ref, bf16[352,352]{1,0:T(8,128)(2,1)} %get-tuple-element.275.a_ref, bf16[352,352]{1,0:T(8,128)(2,1)} %get-tuple-element.276.b_ref, f32[333,176]{1,0:T(8,128)} %get-tuple-element.277.ua_ref, ...), custom_call_target="tpu_custom_call" | custom-call | bytes 29700000 | tf_op jit(solution)/shard_map/text_layer_back/pallas_call | solution.py:193
  274.2 10.5 %self_attention_back.1 = (bf16[256,1408]{1,0:T(8,128)(2,1)}, f32[256,352]{1,0:T(8,128)}, f32[256,704]{1,0:T(8,128)}, bf16[256,704]{1,0:T(8,128)(2,1)}, bf16[256,...) custom-call(bf16[64,1408]{1,0:T(8,128)(2,1)} %get-tuple-element.286.refs_0_, bf16[64,1408]{1,0:T(8,128)(2,1)} %copy-done.38, ...), custom_call_target="tpu_custom_call" | custom-call | bytes 29700000 | tf_op jit(solution)/shard_map/self_attention_back/pallas_call | solution.py:193
  289.4 9.2 %collective-permute-done.35.half_ref = bf16[256,704]{1,0:T(8,128)(2,1)S(1)} collective-permute-done((bf16[256,704]{1,0:T(8,128)(2,1)}, bf16[256,704]{1,0:T(8,128)(2,1)S(1)}, u32[]{:S(2)}, u32[]{:S(2)}) %collective-permute-start.35) | collective-permute-done | bytes 360480 | tf_op jit(solution)/shard_map/ppermute | solution.py:94
  298.5 8.6 %collective-permute-done.36.far_ref = bf16[256,704]{1,0:T(8,128)(2,1)S(1)} collective-permute-done((bf16[256,704]{1,0:T(8,128)(2,1)}, bf16[256,704]{1,0:T(8,128)(2,1)S(1)}, u32[]{:S(2)}, u32[]{:S(2)}) %collective-permute-start.36) | collective-permute-done | bytes 360480 | tf_op jit(solution)/shard_map/ppermute | solution.py:145
  311.0 12.4 %project_back.1 = (bf16[256,528]{1,0:T(8,128)(2,1)}, bf16[256,528]{1,0:T(8,128)(2,1)}, f32[1,88]{1,0:T(1,128)}, f32[1,88]{1,0:T(1,128)}, bf16[64,1408]{1,0:T(8,1...) custom-call(f32[256,704]{1,0:T(8,128)} %get-tuple-element.205.unit_ref, ...), custom_call_target="tpu_custom_call" | custom-call | bytes 26400000 | tf_op jit(solution)/shard_map/project_back/pallas_call | solution.py:193
  337.0 9.9 %collective-permute-done.42 = bf16[144,1408]{1,0:T(8,128)(2,1)S(1)} collective-permute-done((bf16[144,1408]{1,0:T(8,128)(2,1)S(1)}, bf16[144,1408]{1,0:T(8,128)(2,1)S(1)}, u32[]{:S(2)}, u32[]{:S(2)}) %collective-permute-start.42) | collective-permute-done | bytes 405536 | tf_op jit(solution)/shard_map/ppermute | solution.py:94
  392.8 13.6 %collective-permute-done.51 = bf16[256,1408]{1,0:T(8,128)(2,1)S(1)} collective-permute-done((bf16[256,1408]{1,0:T(8,128)(2,1)}, bf16[256,1408]{1,0:T(8,128)(2,1)S(1)}, u32[]{:S(2)}, u32[]{:S(2)}) %collective-permute-start.51) | collective-permute-done | bytes 720928 | tf_op jit(solution)/shard_map/ppermute | solution.py:94
  422.3 10.3 %collective-permute-done.52 = bf16[2,48,1408]{2,1,0:T(8,128)(2,1)S(1)} collective-permute-done((bf16[2,48,1408]{2,1,0:T(8,128)(2,1)S(1)}, bf16[2,48,1408]{2,1,0:T(8,128)(2,1)S(1)}, u32[]{:S(2)}, u32[]{:S(2)}) %collective-permute-start.52) | collective-permute-done | bytes 270368 | tf_op jit(solution)/shard_map/ppermute | solution.py:174
  447.5 12.1 %joined_grads.1 = (f32[512,1408]{1,0:T(8,128)}, f32[512,1408]{1,0:T(8,128)}) custom-call(bf16[512,1408]{1,0:T(8,128)(2,1)} %copy-done, bf16[8,8,48,1408]{3,2,1,0:T(8,128)(2,1)} %all-gather.12.cloned.1.call-done.pack_ref), custom_call_target="tpu_custom_call" | custom-call | bytes 29700000 | tf_op jit(solution)/shard_map/joined_grads/pallas_call | solution.py:193
  460.7 6.1 %feed_forward_out.1 = (f32[1408,768]{1,0:T(8,128)}, f32[768,1408]{1,0:T(8,128)}) custom-call(bf16[8,336,1408]{2,1,0:T(8,128)(2,1)} %bitcast.69), custom_call_target="tpu_custom_call" | custom-call | bytes 19800000 | tf_op jit(solution)/shard_map/feed_forward_out/pallas_call | solution.py:193
  481.7 11.6 %all-gather.22.cloned.1.call-done = bf16[1152,1408]{1,0:T(8,128)(2,1)} async-done(((bf16[144,1408]{1,0:T(8,128)(2,1)}), bf16[1152,1408]{1,0:T(8,128)(2,1)}) %all-gather.22.cloned.1.call-update) | async-done | bytes 3244048 | tf_op jit(solution)/shard_map/all_gather | solution.py:164
  (439 shorter events, 274.0 us)
Async XLA Ops:
  7.2 67.2 %all-gather.14.cloned.1.call-start = ((), (), s32[]{:S(2)}) async-start(), calls=%async_computation.8 | async-start | bytes 3063808 | tf_op jit(solution)/shard_map/all_gather | solution.py:1056
  23.9 28.1 %all-to-all-start = ((bf16[8,64,1408]{2,1,0:T(8,128)(2,1)}), bf16[8,64,1408]{2,1,0:T(8,128)(2,1)S(1)}, u32[]{:S(2)}, u32[]{:S(2)}) async-start(bf16[8,64,1408]{2,1,0:T(8,128)(2,1)} %bitcast), calls=%async_computation | async-start | bytes 2883584 | tf_op jit(solution)/shard_map/all_to_all | solution.py:41
  30.4 103.4 %all-gather.16.cloned.1.call-start = ((), (), s32[]{:S(2)}) async-start(), calls=%async_computation.9 | async-start | bytes 2297856 | tf_op jit(solution)/shard_map/all_gather | solution.py:1089
  56.1 18.3 %collective-permute-start.1 = (bf16[112,1408]{1,0:T(8,128)(2,1)}, bf16[112,1408]{1,0:T(8,128)(2,1)S(1)}, u32[]{:S(2)}, u32[]{:S(2)}) collective-permute-start(bf16[112,1408]{1,0:T(8,128)(2,1)} %get-tuple-element.202.refs_0_), channel_id=1, source_target_pairs={{0,2},{1,3},{2,0},{3,1},{4,6},{5,7},{6,4},{7,5},{8,10},{9,11},{10,... | collective-permute-start | bytes 946184 | tf_op jit(solution)/shard_map/ppermute | solution.py:70
  62.2 22.3 %collective-permute-start.4 = (bf16[48,1408]{1,0:T(8,128)(2,1)S(1)}, bf16[48,1408]{1,0:T(8,128)(2,1)S(1)}, u32[]{:S(2)}, u32[]{:S(2)}) collective-permute-start(bf16[48,1408]{1,0:T(8,128)(2,1)S(1)} %pad_maximum_fusion.8), channel_id=1, source_target_pairs={{0,4},{1,5},{2,6},{3,7},{4,0},{5,1},{6,2},{7,3},{8,12},{9,13},{10,... | collective-permute-start | bytes 405512 | tf_op jit(solution)/shard_map/ppermute | solution.py:94
  85.2 96.8 %all-gather.18.cloned.1.call-start = ((), (), s32[]{:S(2)}) async-start(), calls=%async_computation.10 | async-start | bytes 4866048 | tf_op jit(solution)/shard_map/all_gather | solution.py:164
  98.6 28.4 %collective-permute-start.21 = (bf16[192,1408]{1,0:T(8,128)(2,1)S(1)}, bf16[192,1408]{1,0:T(8,128)(2,1)S(1)}, u32[]{:S(2)}, u32[]{:S(2)}) collective-permute-start(bf16[192,1408]{1,0:T(8,128)(2,1)S(1)} %copy-done.29), channel_id=1, source_target_pairs={{0,4},{1,5},{2,6},{3,7},{4,0},{5,1},{6,2},{7,3},{8,12},{9,13},{10,... | collective-permute-start | bytes 1622024 | tf_op jit(solution)/shard_map/ppermute | solution.py:94
  127.9 89.0 %all-gather.12.cloned.1.call-start = ((), (), s32[]{:S(2)}) async-start(), calls=%async_computation.4 | async-start | bytes 9732096 | tf_op jit(solution)/shard_map/all_gather | solution.py:164
  129.0 23.7 %collective-permute-start.14 = (bf16[192,1408]{1,0:T(8,128)(2,1)S(1)}, bf16[192,1408]{1,0:T(8,128)(2,1)S(1)}, u32[]{:S(2)}, u32[]{:S(2)}) collective-permute-start(bf16[192,1408]{1,0:T(8,128)(2,1)S(1)} %pad_maximum_fusion.5), channel_id=1, source_target_pairs={{0,4},{1,5},{2,6},{3,7},{4,0},{5,1},{6,2},{7,3},{8,12},{9,13},{10,... | collective-permute-start | bytes 1622024 | tf_op jit(solution)/shard_map/ppermute | solution.py:94
  167.8 105.4 %reduce-scatter.4.cloned.1.call-start = ((), (), s32[]{:S(2)}) async-start(), calls=%async_computation.5 | async-start | bytes 9732096 | tf_op jit(solution)/shard_map/reduce_scatter | solution.py:158
  217.0 116.6 %reduce-scatter.6.cloned.1.call-start = ((), (), s32[]{:S(2)}) async-start(), calls=%async_computation.6 | async-start | bytes 7299072 | tf_op jit(solution)/shard_map/reduce_scatter | solution.py:158
  274.0 107.8 %reduce-scatter.8.cloned.1.call-start = ((), (), s32[]{:S(2)}) async-start(), calls=%async_computation.7 | async-start | bytes 4866048 | tf_op jit(solution)/shard_map/reduce_scatter | solution.py:158
  289.0 18.1 %collective-permute-start.36 = (bf16[256,704]{1,0:T(8,128)(2,1)}, bf16[256,704]{1,0:T(8,128)(2,1)S(1)}, u32[]{:S(2)}, u32[]{:S(2)}) collective-permute-start(bf16[256,704]{1,0:T(8,128)(2,1)} %get-tuple-element.295), channel_id=1, source_target_pairs={{0,12},{1,13},{2,14},{3,15},{4,8},{5,9},{6,10},{7,11},{8,4},{9,5},... | collective-permute-start | bytes 1081352 | tf_op jit(solution)/shard_map/ppermute | solution.py:145
  307.2 16.3 %collective-permute-start.37 = (bf16[192,1408]{1,0:T(8,128)(2,1)S(1)}, bf16[192,1408]{1,0:T(8,128)(2,1)S(1)}, u32[]{:S(2)}, u32[]{:S(2)}) collective-permute-start(bf16[192,1408]{1,0:T(8,128)(2,1)S(1)} %slice.115), channel_id=1, source_target_pairs={{0,4},{1,5},{2,6},{3,7},{4,0},{5,1},{6,2},{7,3},{8,12},{9,13},{10,... | collective-permute-start | bytes 1622024 | tf_op jit(solution)/shard_map/ppermute | solution.py:94
  330.4 16.7 %collective-permute-start.38 = (bf16[64,1408]{1,0:T(8,128)(2,1)}, bf16[64,1408]{1,0:T(8,128)(2,1)S(1)}, u32[]{:S(2)}, u32[]{:S(2)}) collective-permute-start(bf16[64,1408]{1,0:T(8,128)(2,1)} %get-tuple-element.306), channel_id=1, source_target_pairs={{0,3},{1,0},{2,1},{3,2},{4,7},{5,4},{6,5},{7,6},{8,11},{9,8},{10,9... | collective-permute-start | bytes 540680 | tf_op jit(solution)/shard_map/ppermute | solution.py:75
  332.5 14.6 %collective-permute-start.39 = (bf16[64,1408]{1,0:T(8,128)(2,1)}, bf16[64,1408]{1,0:T(8,128)(2,1)S(1)}, u32[]{:S(2)}, u32[]{:S(2)}) collective-permute-start(bf16[64,1408]{1,0:T(8,128)(2,1)} %get-tuple-element.307), channel_id=1, source_target_pairs={{0,2},{1,3},{2,0},{3,1},{4,6},{5,7},{6,4},{7,5},{8,10},{9,11},{10,... | collective-permute-start | bytes 540680 | tf_op jit(solution)/shard_map/ppermute | solution.py:75
  332.7 14.4 %collective-permute-start.40 = (bf16[64,1408]{1,0:T(8,128)(2,1)S(1)}, bf16[64,1408]{1,0:T(8,128)(2,1)S(1)}, u32[]{:S(2)}, u32[]{:S(2)}) collective-permute-start(bf16[64,1408]{1,0:T(8,128)(2,1)S(1)} %copy-done.84), channel_id=1, source_target_pairs={{0,1},{1,2},{2,3},{3,0},{4,5},{5,6},{6,7},{7,4},{8,9},{9,10},{10,1... | collective-permute-start | bytes 540680 | tf_op jit(solution)/shard_map/ppermute | solution.py:75
  347.9 112.6 %all-gather.20.cloned.1.call-start = ((), (), s32[]{:S(2)}) async-start(), calls=%async_computation.11 | async-start | bytes 8515584 | tf_op jit(solution)/shard_map/all_gather | solution.py:164
  381.8 111.5 %all-gather.22.cloned.1.call-start = ((), (), s32[]{:S(2)}) async-start(), calls=%async_computation.12 | async-start | bytes 3649536 | tf_op jit(solution)/shard_map/all_gather | solution.py:164
  387.2 19.2 %collective-permute-start.51 = (bf16[256,1408]{1,0:T(8,128)(2,1)}, bf16[256,1408]{1,0:T(8,128)(2,1)S(1)}, u32[]{:S(2)}, u32[]{:S(2)}) collective-permute-start(bf16[256,1408]{1,0:T(8,128)(2,1)} %get-tuple-element.342), channel_id=1, source_target_pairs={{0,4},{1,5},{2,6},{3,7},{4,0},{5,1},{6,2},{7,3},{8,12},{9,13},{10,... | collective-permute-start | bytes 2162696 | tf_op jit(solution)/shard_map/ppermute | solution.py:94
  407.1 15.2 %collective-permute-start.53 = (bf16[2,48,1408]{2,1,0:T(8,128)(2,1)S(1)}, bf16[2,48,1408]{2,1,0:T(8,128)(2,1)S(1)}, u32[]{:S(2)}, u32[]{:S(2)}) collective-permute-start(bf16[2,48,1408]{2,1,0:T(8,128)(2,1)S(1)} %get-tuple-element.393), channel_id=1, source_target_pairs={{0,32},{8,40},{16,48},{24,56},{32,0},{40,8},{48,16},{56,24},{64,96... | collective-permute-start | bytes 811016 | tf_op jit(solution)/shard_map/ppermute | solution.py:174
  414.4 18.2 %collective-permute-start.52 = (bf16[2,48,1408]{2,1,0:T(8,128)(2,1)S(1)}, bf16[2,48,1408]{2,1,0:T(8,128)(2,1)S(1)}, u32[]{:S(2)}, u32[]{:S(2)}) collective-permute-start(bf16[2,48,1408]{2,1,0:T(8,128)(2,1)S(1)} %get-tuple-element.391), channel_id=1, source_target_pairs={{0,16},{8,24},{16,32},{24,40},{32,48},{40,56},{48,0},{56,8},{64,80... | collective-permute-start | bytes 811016 | tf_op jit(solution)/shard_map/ppermute | solution.py:174
  444.7 15.0 %collective-permute-start.62 = (bf16[144,1408]{1,0:T(8,128)(2,1)S(1)}, bf16[144,1408]{1,0:T(8,128)(2,1)S(1)}, u32[]{:S(2)}, u32[]{:S(2)}) collective-permute-start(bf16[144,1408]{1,0:T(8,128)(2,1)S(1)} %convert_element_type.193), channel_id=1, source_target_pairs={{0,64},{8,72},{16,80},{24,88},{32,96},{40,104},{48,112},{56,120},{... | collective-permute-start | bytes 1216520 | tf_op jit(solution)/shard_map/ppermute | solution.py:150
  466.7 14.7 %collective-permute-start.63 = (bf16[256,1408]{1,0:T(8,128)(2,1)S(1)}, bf16[256,1408]{1,0:T(8,128)(2,1)S(1)}, u32[]{:S(2)}, u32[]{:S(2)}) collective-permute-start(bf16[256,1408]{1,0:T(8,128)(2,1)S(1)} %pad_maximum_fusion.3), channel_id=1, source_target_pairs={{0,4},{1,5},{2,6},{3,7},{4,0},{5,1},{6,2},{7,3},{8,12},{9,13},{10,... | collective-permute-start | bytes 2162696 | tf_op jit(solution)/shard_map/ppermute | solution.py:94
  (138 other events, 995.4 us)
Sparse Core Ops, SparseCore 0:
  18.7 50.5 all-gather.13
  85.3 36.1 all-gather.15
  128.0 31.7 all-gather.17
  168.0 48.9 all-gather.11
  219.2 52.8 reduce-scatter.3
  274.9 43.1 reduce-scatter.5
  347.3 34.4 reduce-scatter.7
  384.1 59.6 all-gather.19
  460.6 32.5 all-gather.21

commit v4 on v3

--- a/solution.py
+++ b/solution.py
@@ -1055,8 +1055,9 @@
     shares = [dp_slice(qkv_flat, 48), dp_slice(attn_out_w, 16)]
     pack = lax.all_gather(half_swap(jnp.concatenate(shares, 0)), "dp", axis=0, tiled=False)
     ckv_flat = ckv_w.reshape(text_width, 2 * local_width)
+    text_rows_in = pad_rows(text_tokens, model_width // 4)
     text_pair, text_units, text_scales = text_layer(
-        text_tokens, ckv_flat, cknorm_gain, model_width // 4
+        text_rows_in, ckv_flat, cknorm_gain, model_width // 4
     )
     share = hidden_width // dp_count
     deep = text_width // dp_count // 4
@@ -1099,7 +1100,7 @@
     skip_rows = jnp.concatenate([part[part_count:] for part in normed_parts], 0)
     skip_half = half_swap(after(skip_rows, normed))
     other_text, other_units, other_scales, other_ckv = text_layer(
-        text_tokens, after(cross_pack, normed), cknorm_gain, model_width // 4
+        text_rows_in, after(cross_pack, normed), cknorm_gain, model_width // 4
     )
     *normed_parts, other_text = join(*ring_gather(normed), other_text)
     rows_two, cross_raw, mixed_two, *partial = cross_layer(
@@ -1152,7 +1153,7 @@
         (text_own, text_other),
         (text_units, other_units),
         (text_scales, other_scales),
-        after(text_tokens, out_grad),
+        after(text_rows_in, out_grad),
         (ckv_flat, other_ckv),
         cknorm_gain,
     )
@@ -1235,12 +1236,11 @@
     early_sums = gather_low(after(early_sums, late_sums))
     merged_half = half_swap(merged_rows)
     last_sums = scatter_stage(0, last_sums)
-    last_sums, merged_half = join(last_sums, merged_half)
+    output = hidden_two
+    for piece in ring_scatter(after_all(last_partial, last_sums)):
+        output = output + piece.astype(F32)
     last_sums = scatter_stage(1, last_sums)
-    output = hidden_two
-    for piece in ring_scatter(after_all(last_partial, merged_half)):
-        output = output + piece.astype(F32)
-    last_sums, output = join(last_sums, output)
+    last_sums, output, merged_half = join(last_sums, output, merged_half)
     share = late_sums.shape[0] // 2
     own_sums = jnp.concatenate([late_sums[:share].astype(F32), last_sums[0]], 0)
     other_sums = jnp.concatenate([late_sums[share:], last_sums[1].astype(BF16)], 0)

time: 522 us -> 515 us (0.987)
    ppermute x11, waiting for transfers between devices: 51.3 us -> 42.4 us  [half_swap(): lax.ppermute(block, 'tensor', [(i, (i + count // 2) % count) for i in ran...]
  transfers between devices with their start and end apart: 74 -> 74, of which waited for: 38 -> 37; matrix products, arithmetic and copies ran while one was open for 9% -> 9% of each run, Pallas kernels for 28% -> 29%
where the time goes in v4:
time: 515 us; the launch traced here: 505 us
  waiting for transfers between devices  172 us (33%)
  Pallas kernels  146 us (28%)
  starting transfers between devices  98.3 us (19%)
  local copies, waits for them, and re-layouts  50.9 us (10%)
  other arithmetic  19.3 us (4%)
  between operations  15.4 us (3%)
    pallas_call x22, Pallas kernels, call(): pl.pallas_call(kernel, out_shape=outs, scratch_shapes=scratch, compiler_p...  146 us
    ppermute x11, waiting for transfers between devices, half_swap(): lax.ppermute(block, 'tensor', [(i, (i + count // 2) % count) for i in ran...  42.4 us
    ppermute x18, waiting for transfers between devices, ring_scatter(): lax.ppermute(blocks[k], 'tensor', ring_route(-k))  39 us
    ppermute x24, waiting for transfers between devices, ring_gather(): got = {k: lax.ppermute(block, 'tensor', ring_route(k)) for k in (1, 3, 2)}  38.8 us
    ppermute x24, starting transfers between devices, ring_gather(): got = {k: lax.ppermute(block, 'tensor', ring_route(k)) for k in (1, 3, 2)}  31.2 us
    ppermute x18, starting transfers between devices, ring_scatter(): lax.ppermute(blocks[k], 'tensor', ring_route(-k))  23.7 us
    ppermute x11, starting transfers between devices, half_swap(): lax.ppermute(block, 'tensor', [(i, (i + count // 2) % count) for i in ran...  21.8 us
    all_gather x4, waiting for transfers between devices, gather_low(): lax.all_gather(rows, 'dp', axis=0, tiled=False, axis_index_groups=low_gro...  19.1 us
  transfers between devices with their start and end apart: 74, of which 37 were waited for; matrix products, arithmetic and copies ran while one was open for 9% of the time, Pallas kernels for 29%

profile of v4, /device:TPU:1, one launch (start us, length us, event | category | flops | bytes accessed | tf_op | source)
XLA Modules:
  0.0 505.2 jit_solution(5925810100073581855)
XLA Ops:
  23.9 6.5 %all-to-all-start = ((bf16[8,64,1408]{2,1,0:T(8,128)(2,1)}), bf16[8,64,1408]{2,1,0:T(8,128)(2,1)S(1)}, u32[]{:S(2)}, u32[]{:S(2)}) async-start(bf16[8,64,1408]{2,1,0:T(8,128)(2,1)} %bitcast), calls=%async_computation | async-start | bytes 2883584 | tf_op jit(solution)/shard_map/all_to_all | solution.py:41
  65.4 8.9 %collective-permute-done.1.refs_2_ = bf16[112,1408]{1,0:T(8,128)(2,1)S(1)} collective-permute-done((bf16[112,1408]{1,0:T(8,128)(2,1)}, bf16[112,1408]{1,0:T(8,128)(2,1)S(1)}, u32[]{:S(2)}, u32[]{:S(2)}) %collective-permute-start.1) | collective-permute-done | bytes 315424 | tf_op jit(solution)/shard_map/ppermute | solution.py:70
  75.2 9.3 %project.1 = (bf16[256,1408]{1,0:T(8,128)(2,1)}, f32[256,704]{1,0:T(8,128)}, f32[256,8]{1,0:T(8,128)}, bf16[256,352]{1,0:T(8,128)(2,1)}, bf16[256,704]{1,0:T(8,128)(2,1)}) custom-call(bf16[112,1408]{1,0:T(8,128)(2,1)} %get-tuple-element.201.refs_0_, bf16[112,1408]{1,0:T(8,128)(2,1)} %copy-done.20, bf16[112,1408]{1,0:T(8,128)(2,1)} %copy-done.18, ...), custom_call_target="tpu_custom_call" | custom-call | bytes 19800000 | tf_op jit(solution)/shard_map/project/pallas_call | solution.py:193
  88.3 7.4 %collective-permute-done.6.c_ref.refs_7_ = bf16[256,704]{1,0:T(8,128)(2,1)S(1)} collective-permute-done((bf16[256,704]{1,0:T(8,128)(2,1)}, bf16[256,704]{1,0:T(8,128)(2,1)S(1)}, u32[]{:S(2)}, u32[]{:S(2)}) %collective-permute-start.6) | collective-permute-done | bytes 360480 | tf_op jit(solution)/shard_map/ppermute | solution.py:94
  100.7 7.3 %self_attention.1 = (bf16[256,352]{1,0:T(8,128)(2,1)}, f32[256,4]{1,0:T(8,128)}, bf16[64,1408]{1,0:T(8,128)(2,1)}, bf16[64,1408]{1,0:T(8,128)(2,1)}, bf16[64,1408]{1,0:T(8,128)(2,1)}, /*index=5*/bf16[64,1408]{1,0:T(8,128)(2,1)}) custom-call(bf16[256,352]{1,0:T(8,128)(2,1)} %get-tuple-element.206.q_ref.refs_4_, ...), custom_call_target="tpu_custom_call" | custom-call | bytes 16500000 | tf_op jit(solution)/shard_map/self_attention/pallas_call | solution.py:193
  113.5 6.3 %collective-permute-done.8.refs_1_ = bf16[64,1408]{1,0:T(8,128)(2,1)S(1)} collective-permute-done((bf16[64,1408]{1,0:T(8,128)(2,1)}, bf16[64,1408]{1,0:T(8,128)(2,1)S(1)}, u32[]{:S(2)}, u32[]{:S(2)}) %collective-permute-start.8) | collective-permute-done | bytes 180256 | tf_op jit(solution)/shard_map/ppermute | solution.py:75
  142.0 10.1 %cross_layer.1 = (bf16[256,1408]{1,0:T(8,128)(2,1)}, f32[256,352]{1,0:T(8,128)}, bf16[256,352]{1,0:T(8,128)(2,1)}, bf16[64,1408]{1,0:T(8,128)(2,1)}, bf16[64,140...) custom-call(bf16[64,1408]{1,0:T(8,128)(2,1)} %get-tuple-element.220.refs_0_, ...), custom_call_target="tpu_custom_call" | custom-call | bytes 23100000 | tf_op jit(solution)/shard_map/cross_layer/pallas_call | solution.py:193
  156.5 6.7 %collective-permute-done.15.refs_1_ = bf16[64,1408]{1,0:T(8,128)(2,1)S(1)} collective-permute-done((bf16[64,1408]{1,0:T(8,128)(2,1)}, bf16[64,1408]{1,0:T(8,128)(2,1)S(1)}, u32[]{:S(2)}, u32[]{:S(2)}) %collective-permute-start.15) | collective-permute-done | bytes 180256 | tf_op jit(solution)/shard_map/ppermute | solution.py:75
  172.6 8.5 %collective-permute-done.18.refs_1_ = bf16[64,1408]{1,0:T(8,128)(2,1)S(1)} collective-permute-done((bf16[64,1408]{1,0:T(8,128)(2,1)}, bf16[64,1408]{1,0:T(8,128)(2,1)S(1)}, u32[]{:S(2)}, u32[]{:S(2)}) %collective-permute-start.18) | collective-permute-done | bytes 180256 | tf_op jit(solution)/shard_map/ppermute | solution.py:70
  181.9 13.6 %feed_forward.1 = (bf16[256,1408]{1,0:T(8,128)(2,1)}, bf16[2,2,256,768]{3,2,1,0:T(8,128)(2,1)}, bf16[64,1408]{1,0:T(8,128)(2,1)}, bf16[64,1408]{1,0:T(8,128)(2,1...) custom-call(bf16[64,1408]{1,0:T(8,128)(2,1)} %get-tuple-element.241., ...), custom_call_target="tpu_custom_call" | custom-call | bytes 29700000 | tf_op jit(solution)/shard_map/feed_forward/pallas_call | solution.py:193
  199.1 7.1 %feed_forward_grads.1 = bf16[8,2,192,1408]{3,2,1,0:T(8,128)(2,1)} custom-call(bf16[2,2,256,768]{3,2,1,0:T(8,128)(2,1)} %get-tuple-element.250.acts_ref, bf16[256,1408]{1,0:T(8,128)(2,1)} %get-tuple-element.251.x_ref, bf16[256,1408]{1,0:T(8,128)(2,1)} %pad_maximum_fusion.2.refs_4_.cot_ref), custom_call_target="tpu_custom_call" | custom-call | bytes 23100000 | tf_op jit(solution)/shard_map/feed_forward_grads/pallas_call | solution.py:193
  210.0 7.3 %all-gather.12.cloned.1.call-done.pack_ref = bf16[8,8,48,1408]{3,2,1,0:T(8,128)(2,1)} async-done(((bf16[1,8,48,1408]{3,2,1,0:T(8,128)(2,1)}), bf16[8,8,48,1408]{3,2,1,0:T(8,128)(2,1)}) %all-gather.12.cloned.1.call-update) | async-done | bytes 8650768 | tf_op jit(solution)/shard_map/all_gather | solution.py:164
  232.8 11.4 %cross_layer_back.1 = (bf16[256,1408]{1,0:T(8,128)(2,1)}, bf16[256,352]{1,0:T(8,128)(2,1)}, bf16[352,352]{1,0:T(8,128)(2,1)}, bf16[352,352]{1,0:T(8,128)(2,1)}, ...) custom-call(bf16[64,1408]{1,0:T(8,128)(2,1)} %get-tuple-element.257., ...), custom_call_target="tpu_custom_call" | custom-call | bytes 33000000 | tf_op jit(solution)/shard_map/cross_layer_back/pallas_call | solution.py:193
  264.9 8.8 %text_layer_back.1 = bf16[8,2,144,1408]{3,2,1,0:T(8,128)(2,1)} custom-call(bf16[8,2,48,1408]{3,2,1,0:T(8,128)(2,1)} %cross_grads.1.first_ref, bf16[352,352]{1,0:T(8,128)(2,1)} %get-tuple-element.274.a_ref, bf16[352,352]{1,0:T(8,128)(2,1)} %get-tuple-element.275.b_ref, f32[352,176]{1,0:T(8,128)} %get-tuple-element.276.ua_ref, ...), custom_call_target="tpu_custom_call" | custom-call | bytes 29700000 | tf_op jit(solution)/shard_map/text_layer_back/pallas_call | solution.py:193
  274.7 10.5 %self_attention_back.1 = (bf16[256,1408]{1,0:T(8,128)(2,1)}, f32[256,352]{1,0:T(8,128)}, f32[256,704]{1,0:T(8,128)}, bf16[256,704]{1,0:T(8,128)(2,1)}, bf16[256,...) custom-call(bf16[64,1408]{1,0:T(8,128)(2,1)} %get-tuple-element.285.refs_0_, bf16[64,1408]{1,0:T(8,128)(2,1)} %copy-done.38, ...), custom_call_target="tpu_custom_call" | custom-call | bytes 29700000 | tf_op jit(solution)/shard_map/self_attention_back/pallas_call | solution.py:193
  289.8 9.2 %collective-permute-done.35.half_ref = bf16[256,704]{1,0:T(8,128)(2,1)S(1)} collective-permute-done((bf16[256,704]{1,0:T(8,128)(2,1)}, bf16[256,704]{1,0:T(8,128)(2,1)S(1)}, u32[]{:S(2)}, u32[]{:S(2)}) %collective-permute-start.35) | collective-permute-done | bytes 360480 | tf_op jit(solution)/shard_map/ppermute | solution.py:94
  298.9 8.6 %collective-permute-done.36.far_ref = bf16[256,704]{1,0:T(8,128)(2,1)S(1)} collective-permute-done((bf16[256,704]{1,0:T(8,128)(2,1)}, bf16[256,704]{1,0:T(8,128)(2,1)S(1)}, u32[]{:S(2)}, u32[]{:S(2)}) %collective-permute-start.36) | collective-permute-done | bytes 360480 | tf_op jit(solution)/shard_map/ppermute | solution.py:145
  311.3 12.4 %project_back.1 = (bf16[256,528]{1,0:T(8,128)(2,1)}, bf16[256,528]{1,0:T(8,128)(2,1)}, f32[1,88]{1,0:T(1,128)}, f32[1,88]{1,0:T(1,128)}, bf16[64,1408]{1,0:T(8,1...) custom-call(f32[256,704]{1,0:T(8,128)} %get-tuple-element.204.unit_ref, ...), custom_call_target="tpu_custom_call" | custom-call | bytes 26400000 | tf_op jit(solution)/shard_map/project_back/pallas_call | solution.py:193
  337.4 9.9 %collective-permute-done.42 = bf16[144,1408]{1,0:T(8,128)(2,1)S(1)} collective-permute-done((bf16[144,1408]{1,0:T(8,128)(2,1)S(1)}, bf16[144,1408]{1,0:T(8,128)(2,1)S(1)}, u32[]{:S(2)}, u32[]{:S(2)}) %collective-permute-start.42) | collective-permute-done | bytes 405536 | tf_op jit(solution)/shard_map/ppermute | solution.py:94
  405.2 6.4 %collective-permute-done.53 = bf16[2,48,1408]{2,1,0:T(8,128)(2,1)S(1)} collective-permute-done((bf16[2,48,1408]{2,1,0:T(8,128)(2,1)S(1)}, bf16[2,48,1408]{2,1,0:T(8,128)(2,1)S(1)}, u32[]{:S(2)}, u32[]{:S(2)}) %collective-permute-start.53) | collective-permute-done | bytes 270368 | tf_op jit(solution)/shard_map/ppermute | solution.py:174
  415.4 8.8 %collective-permute-done.51 = bf16[2,48,1408]{2,1,0:T(8,128)(2,1)S(1)} collective-permute-done((bf16[2,48,1408]{2,1,0:T(8,128)(2,1)S(1)}, bf16[2,48,1408]{2,1,0:T(8,128)(2,1)S(1)}, u32[]{:S(2)}, u32[]{:S(2)}) %collective-permute-start.51) | collective-permute-done | bytes 270368 | tf_op jit(solution)/shard_map/ppermute | solution.py:174
  439.9 12.2 %joined_grads.1 = (f32[512,1408]{1,0:T(8,128)}, f32[512,1408]{1,0:T(8,128)}) custom-call(bf16[512,1408]{1,0:T(8,128)(2,1)} %copy-done, bf16[8,8,48,1408]{3,2,1,0:T(8,128)(2,1)} %all-gather.12.cloned.1.call-done.pack_ref), custom_call_target="tpu_custom_call" | custom-call | bytes 29700000 | tf_op jit(solution)/shard_map/joined_grads/pallas_call | solution.py:193
  467.9 6.5 %collective-permute-done.63 = bf16[256,1408]{1,0:T(8,128)(2,1)S(1)} collective-permute-done((bf16[256,1408]{1,0:T(8,128)(2,1)S(1)}, bf16[256,1408]{1,0:T(8,128)(2,1)S(1)}, u32[]{:S(2)}, u32[]{:S(2)}) %collective-permute-start.63) | collective-permute-done | bytes 720928 | tf_op jit(solution)/shard_map/ppermute | solution.py:94
  474.6 11.8 %all-gather.22.cloned.1.call-done = bf16[1152,1408]{1,0:T(8,128)(2,1)} async-done(((bf16[144,1408]{1,0:T(8,128)(2,1)}), bf16[1152,1408]{1,0:T(8,128)(2,1)}) %all-gather.22.cloned.1.call-update) | async-done | bytes 3244048 | tf_op jit(solution)/shard_map/all_gather | solution.py:164
  (440 shorter events, 274.5 us)
Async XLA Ops:
  7.2 67.2 %all-gather.14.cloned.1.call-start = ((), (), s32[]{:S(2)}) async-start(), calls=%async_computation.8 | async-start | bytes 3063808 | tf_op jit(solution)/shard_map/all_gather | solution.py:1056
  23.9 28.1 %all-to-all-start = ((bf16[8,64,1408]{2,1,0:T(8,128)(2,1)}), bf16[8,64,1408]{2,1,0:T(8,128)(2,1)S(1)}, u32[]{:S(2)}, u32[]{:S(2)}) async-start(bf16[8,64,1408]{2,1,0:T(8,128)(2,1)} %bitcast), calls=%async_computation | async-start | bytes 2883584 | tf_op jit(solution)/shard_map/all_to_all | solution.py:41
  30.4 102.6 %all-gather.16.cloned.1.call-start = ((), (), s32[]{:S(2)}) async-start(), calls=%async_computation.9 | async-start | bytes 2297856 | tf_op jit(solution)/shard_map/all_gather | solution.py:1090
  56.6 17.8 %collective-permute-start.1 = (bf16[112,1408]{1,0:T(8,128)(2,1)}, bf16[112,1408]{1,0:T(8,128)(2,1)S(1)}, u32[]{:S(2)}, u32[]{:S(2)}) collective-permute-start(bf16[112,1408]{1,0:T(8,128)(2,1)} %get-tuple-element.201.refs_0_), channel_id=1, source_target_pairs={{0,2},{1,3},{2,0},{3,1},{4,6},{5,7},{6,4},{7,5},{8,10},{9,11},{10,... | collective-permute-start | bytes 946184 | tf_op jit(solution)/shard_map/ppermute | solution.py:70
  62.2 22.3 %collective-permute-start.4 = (bf16[48,1408]{1,0:T(8,128)(2,1)S(1)}, bf16[48,1408]{1,0:T(8,128)(2,1)S(1)}, u32[]{:S(2)}, u32[]{:S(2)}) collective-permute-start(bf16[48,1408]{1,0:T(8,128)(2,1)S(1)} %pad_maximum_fusion.8), channel_id=1, source_target_pairs={{0,4},{1,5},{2,6},{3,7},{4,0},{5,1},{6,2},{7,3},{8,12},{9,13},{10,... | collective-permute-start | bytes 405512 | tf_op jit(solution)/shard_map/ppermute | solution.py:94
  85.2 95.9 %all-gather.18.cloned.1.call-start = ((), (), s32[]{:S(2)}) async-start(), calls=%async_computation.10 | async-start | bytes 4866048 | tf_op jit(solution)/shard_map/all_gather | solution.py:164
  98.6 28.5 %collective-permute-start.21 = (bf16[192,1408]{1,0:T(8,128)(2,1)S(1)}, bf16[192,1408]{1,0:T(8,128)(2,1)S(1)}, u32[]{:S(2)}, u32[]{:S(2)}) collective-permute-start(bf16[192,1408]{1,0:T(8,128)(2,1)S(1)} %copy-done.29), channel_id=1, source_target_pairs={{0,4},{1,5},{2,6},{3,7},{4,0},{5,1},{6,2},{7,3},{8,12},{9,13},{10,... | collective-permute-start | bytes 1622024 | tf_op jit(solution)/shard_map/ppermute | solution.py:94
  128.0 89.3 %all-gather.12.cloned.1.call-start = ((), (), s32[]{:S(2)}) async-start(), calls=%async_computation.4 | async-start | bytes 9732096 | tf_op jit(solution)/shard_map/all_gather | solution.py:164
  129.1 23.0 %collective-permute-start.14 = (bf16[192,1408]{1,0:T(8,128)(2,1)S(1)}, bf16[192,1408]{1,0:T(8,128)(2,1)S(1)}, u32[]{:S(2)}, u32[]{:S(2)}) collective-permute-start(bf16[192,1408]{1,0:T(8,128)(2,1)S(1)} %pad_maximum_fusion.5), channel_id=1, source_target_pairs={{0,4},{1,5},{2,6},{3,7},{4,0},{5,1},{6,2},{7,3},{8,12},{9,13},{10,... | collective-permute-start | bytes 1622024 | tf_op jit(solution)/shard_map/ppermute | solution.py:94
  167.0 106.7 %reduce-scatter.4.cloned.1.call-start = ((), (), s32[]{:S(2)}) async-start(), calls=%async_computation.5 | async-start | bytes 9732096 | tf_op jit(solution)/shard_map/reduce_scatter | solution.py:158
  217.3 116.7 %reduce-scatter.6.cloned.1.call-start = ((), (), s32[]{:S(2)}) async-start(), calls=%async_computation.6 | async-start | bytes 7299072 | tf_op jit(solution)/shard_map/reduce_scatter | solution.py:158
  274.4 107.8 %reduce-scatter.8.cloned.1.call-start = ((), (), s32[]{:S(2)}) async-start(), calls=%async_computation.7 | async-start | bytes 4866048 | tf_op jit(solution)/shard_map/reduce_scatter | solution.py:158
  289.4 18.1 %collective-permute-start.36 = (bf16[256,704]{1,0:T(8,128)(2,1)}, bf16[256,704]{1,0:T(8,128)(2,1)S(1)}, u32[]{:S(2)}, u32[]{:S(2)}) collective-permute-start(bf16[256,704]{1,0:T(8,128)(2,1)} %get-tuple-element.294), channel_id=1, source_target_pairs={{0,12},{1,13},{2,14},{3,15},{4,8},{5,9},{6,10},{7,11},{8,4},{9,5},... | collective-permute-start | bytes 1081352 | tf_op jit(solution)/shard_map/ppermute | solution.py:145
  307.6 16.3 %collective-permute-start.37 = (bf16[192,1408]{1,0:T(8,128)(2,1)S(1)}, bf16[192,1408]{1,0:T(8,128)(2,1)S(1)}, u32[]{:S(2)}, u32[]{:S(2)}) collective-permute-start(bf16[192,1408]{1,0:T(8,128)(2,1)S(1)} %slice.115), channel_id=1, source_target_pairs={{0,4},{1,5},{2,6},{3,7},{4,0},{5,1},{6,2},{7,3},{8,12},{9,13},{10,... | collective-permute-start | bytes 1622024 | tf_op jit(solution)/shard_map/ppermute | solution.py:94
  330.8 16.6 %collective-permute-start.38 = (bf16[64,1408]{1,0:T(8,128)(2,1)}, bf16[64,1408]{1,0:T(8,128)(2,1)S(1)}, u32[]{:S(2)}, u32[]{:S(2)}) collective-permute-start(bf16[64,1408]{1,0:T(8,128)(2,1)} %get-tuple-element.305), channel_id=1, source_target_pairs={{0,3},{1,0},{2,1},{3,2},{4,7},{5,4},{6,5},{7,6},{8,11},{9,8},{10,9... | collective-permute-start | bytes 540680 | tf_op jit(solution)/shard_map/ppermute | solution.py:75
  332.9 14.6 %collective-permute-start.39 = (bf16[64,1408]{1,0:T(8,128)(2,1)}, bf16[64,1408]{1,0:T(8,128)(2,1)S(1)}, u32[]{:S(2)}, u32[]{:S(2)}) collective-permute-start(bf16[64,1408]{1,0:T(8,128)(2,1)} %get-tuple-element.306), channel_id=1, source_target_pairs={{0,2},{1,3},{2,0},{3,1},{4,6},{5,7},{6,4},{7,5},{8,10},{9,11},{10,... | collective-permute-start | bytes 540680 | tf_op jit(solution)/shard_map/ppermute | solution.py:75
  333.2 14.3 %collective-permute-start.40 = (bf16[64,1408]{1,0:T(8,128)(2,1)S(1)}, bf16[64,1408]{1,0:T(8,128)(2,1)S(1)}, u32[]{:S(2)}, u32[]{:S(2)}) collective-permute-start(bf16[64,1408]{1,0:T(8,128)(2,1)S(1)} %copy-done.84), channel_id=1, source_target_pairs={{0,1},{1,2},{2,3},{3,0},{4,5},{5,6},{6,7},{7,4},{8,9},{9,10},{10,1... | collective-permute-start | bytes 540680 | tf_op jit(solution)/shard_map/ppermute | solution.py:75
  348.2 104.7 %all-gather.20.cloned.1.call-start = ((), (), s32[]{:S(2)}) async-start(), calls=%async_computation.11 | async-start | bytes 8515584 | tf_op jit(solution)/shard_map/all_gather | solution.py:164
  382.2 104.1 %all-gather.22.cloned.1.call-start = ((), (), s32[]{:S(2)}) async-start(), calls=%async_computation.12 | async-start | bytes 3649536 | tf_op jit(solution)/shard_map/all_gather | solution.py:164
  387.6 36.7 %collective-permute-start.57 = (bf16[256,1408]{1,0:T(8,128)(2,1)}, bf16[256,1408]{1,0:T(8,128)(2,1)S(1)}, u32[]{:S(2)}, u32[]{:S(2)}) collective-permute-start(bf16[256,1408]{1,0:T(8,128)(2,1)} %get-tuple-element.349), channel_id=1, source_target_pairs={{0,4},{1,5},{2,6},{3,7},{4,0},{5,1},{6,2},{7,3},{8,12},{9,13},{10,... | collective-permute-start | bytes 2162696 | tf_op jit(solution)/shard_map/ppermute | solution.py:94
  400.2 15.2 %collective-permute-start.52 = (bf16[2,48,1408]{2,1,0:T(8,128)(2,1)S(1)}, bf16[2,48,1408]{2,1,0:T(8,128)(2,1)S(1)}, u32[]{:S(2)}, u32[]{:S(2)}) collective-permute-start(bf16[2,48,1408]{2,1,0:T(8,128)(2,1)S(1)} %get-tuple-element.391), channel_id=1, source_target_pairs={{0,32},{8,40},{16,48},{24,56},{32,0},{40,8},{48,16},{56,24},{64,96... | collective-permute-start | bytes 811016 | tf_op jit(solution)/shard_map/ppermute | solution.py:174
  405.0 19.1 %collective-permute-start.51 = (bf16[2,48,1408]{2,1,0:T(8,128)(2,1)S(1)}, bf16[2,48,1408]{2,1,0:T(8,128)(2,1)S(1)}, u32[]{:S(2)}, u32[]{:S(2)}) collective-permute-start(bf16[2,48,1408]{2,1,0:T(8,128)(2,1)S(1)} %get-tuple-element.389), channel_id=1, source_target_pairs={{0,16},{8,24},{16,32},{24,40},{32,48},{40,56},{48,0},{56,8},{64,80... | collective-permute-start | bytes 811016 | tf_op jit(solution)/shard_map/ppermute | solution.py:174
  438.1 14.0 %collective-permute-start.62 = (bf16[144,1408]{1,0:T(8,128)(2,1)S(1)}, bf16[144,1408]{1,0:T(8,128)(2,1)S(1)}, u32[]{:S(2)}, u32[]{:S(2)}) collective-permute-start(bf16[144,1408]{1,0:T(8,128)(2,1)S(1)} %convert_element_type.195), channel_id=1, source_target_pairs={{0,64},{8,72},{16,80},{24,88},{32,96},{40,104},{48,112},{56,120},{... | collective-permute-start | bytes 1216520 | tf_op jit(solution)/shard_map/ppermute | solution.py:150
  459.1 15.2 %collective-permute-start.63 = (bf16[256,1408]{1,0:T(8,128)(2,1)S(1)}, bf16[256,1408]{1,0:T(8,128)(2,1)S(1)}, u32[]{:S(2)}, u32[]{:S(2)}) collective-permute-start(bf16[256,1408]{1,0:T(8,128)(2,1)S(1)} %pad_maximum_fusion.3), channel_id=1, source_target_pairs={{0,4},{1,5},{2,6},{3,7},{4,0},{5,1},{6,2},{7,3},{8,12},{9,13},{10,... | collective-permute-start | bytes 2162696 | tf_op jit(solution)/shard_map/ppermute | solution.py:94
  (138 other events, 936.8 us)
Sparse Core Ops, SparseCore 0:
  18.7 50.5 all-gather.13
  85.4 36.5 all-gather.15
  128.1 31.5 all-gather.17
  167.1 50.1 all-gather.11
  219.6 52.8 reduce-scatter.3
  275.3 43.1 reduce-scatter.5
  347.6 34.5 reduce-scatter.7
  384.6 59.6 all-gather.19
  453.1 33.2 all-gather.21

commit v5 on v4

--- a/solution.py
+++ b/solution.py
@@ -1047,13 +1047,14 @@
     joined = jnp.concatenate([latent, skip_input], 1)
     joined_part = lax.dynamic_slice_in_dim(joined, tensor_place * slab_width, slab_width, 1)
     partial = jnp.dot(joined_part, skip_w, preferred_element_type=F32).astype(BF16)
-    got = exchange(partial.reshape(tensor_count, part_count, model_width))
 
     dp_place = lax.axis_index("dp")
     qkv_flat = qkv_w.transpose(1, 2, 0).reshape(qkv_rows, model_width)
     cq_turned = cq_w.T
     shares = [dp_slice(qkv_flat, 48), dp_slice(attn_out_w, 16)]
-    pack = lax.all_gather(half_swap(jnp.concatenate(shares, 0)), "dp", axis=0, tiled=False)
+    share, partial = join(half_swap(jnp.concatenate(shares, 0)), partial)
+    got = exchange(partial.reshape(tensor_count, part_count, model_width))
+    pack = lax.all_gather(share, "dp", axis=0, tiled=False)
     ckv_flat = ckv_w.reshape(text_width, 2 * local_width)
     text_rows_in = pad_rows(text_tokens, model_width // 4)
     text_pair, text_units, text_scales = text_layer(

time: 515 us -> 521 us (1.012)
  waiting for transfers between devices: 172 us -> 185 us
    all_to_all x1, waiting for transfers between devices: 0.49 us -> 17.7 us  [exchange(): return lax.all_to_all(blocks, axis, 0, 0, tiled=True)]
    unnamed x172 -> x160, local copies, waits for them, and re-layouts: 15.5 us -> 13.5 us
  transfers between devices with their start and end apart: 74 -> 74, of which waited for: 37 -> 36; matrix products, arithmetic and copies ran while one was open for 9% -> 9% of each run, Pallas kernels for 29% -> 29%
where the time goes in v5:
time: 521 us; the launch traced here: 511 us
  waiting for transfers between devices  185 us (36%)
  Pallas kernels  146 us (28%)
  starting transfers between devices  94 us (18%)
  local copies, waits for them, and re-layouts  47.4 us (9%)
  other arithmetic  18.7 us (4%)
  between operations  15.4 us (3%)
    pallas_call x22, Pallas kernels, call(): pl.pallas_call(kernel, out_shape=outs, scratch_shapes=scratch, compiler_p...  146 us
    ppermute x24, waiting for transfers between devices, ring_gather(): got = {k: lax.ppermute(block, 'tensor', ring_route(k)) for k in (1, 3, 2)}  39.9 us
    ppermute x11, waiting for transfers between devices, half_swap(): lax.ppermute(block, 'tensor', [(i, (i + count // 2) % count) for i in ran...  39.6 us
    ppermute x18, waiting for transfers between devices, ring_scatter(): lax.ppermute(blocks[k], 'tensor', ring_route(-k))  38.5 us
    ppermute x24, starting transfers between devices, ring_gather(): got = {k: lax.ppermute(block, 'tensor', ring_route(k)) for k in (1, 3, 2)}  30.1 us
    ppermute x18, starting transfers between devices, ring_scatter(): lax.ppermute(blocks[k], 'tensor', ring_route(-k))  22.2 us
    ppermute x11, starting transfers between devices, half_swap(): lax.ppermute(block, 'tensor', [(i, (i + count // 2) % count) for i in ran...  21.5 us
    ppermute x4, waiting for transfers between devices, scatter_stage(): total = total + lax.ppermute(send, 'dp', route).astype(F32)  19.1 us
  transfers between devices with their start and end apart: 74, of which 36 were waited for; matrix products, arithmetic and copies ran while one was open for 9% of the time, Pallas kernels for 29%

profile of v5, /device:TPU:1, one launch (start us, length us, event | category | flops | bytes accessed | tf_op | source)
XLA Modules:
  0.0 511.0 jit_solution(15351900110897704838)
XLA Ops:
  42.3 17.7 %all-to-all-done.got_ref = bf16[8,64,1408]{2,1,0:T(8,128)(2,1)S(1)} async-done(((bf16[8,64,1408]{2,1,0:T(8,128)(2,1)}), bf16[8,64,1408]{2,1,0:T(8,128)(2,1)S(1)}, u32[]{:S(2)}, u32[]{:S(2)}) %all-to-all-start) | async-done | bytes 1441824 | tf_op jit(solution)/shard_map/all_to_all | solution.py:41
  72.4 9.5 %collective-permute-done.2.refs_2_ = bf16[112,1408]{1,0:T(8,128)(2,1)S(1)} collective-permute-done((bf16[112,1408]{1,0:T(8,128)(2,1)}, bf16[112,1408]{1,0:T(8,128)(2,1)S(1)}, u32[]{:S(2)}, u32[]{:S(2)}) %collective-permute-start.2) | collective-permute-done | bytes 315424 | tf_op jit(solution)/shard_map/ppermute | solution.py:70
  82.8 9.3 %project.1 = (bf16[256,1408]{1,0:T(8,128)(2,1)}, f32[256,704]{1,0:T(8,128)}, f32[256,8]{1,0:T(8,128)}, bf16[256,352]{1,0:T(8,128)(2,1)}, bf16[256,704]{1,0:T(8,128)(2,1)}) custom-call(bf16[112,1408]{1,0:T(8,128)(2,1)} %get-tuple-element.204.refs_0_, bf16[112,1408]{1,0:T(8,128)(2,1)} %copy-done.19, bf16[112,1408]{1,0:T(8,128)(2,1)} %copy-done.17, ...), custom_call_target="tpu_custom_call" | custom-call | bytes 19800000 | tf_op jit(solution)/shard_map/project/pallas_call | solution.py:193
  94.8 8.8 %collective-permute-done.6.c_ref.refs_7_ = bf16[256,704]{1,0:T(8,128)(2,1)S(1)} collective-permute-done((bf16[256,704]{1,0:T(8,128)(2,1)}, bf16[256,704]{1,0:T(8,128)(2,1)S(1)}, u32[]{:S(2)}, u32[]{:S(2)}) %collective-permute-start.6) | collective-permute-done | bytes 360480 | tf_op jit(solution)/shard_map/ppermute | solution.py:94
  109.7 7.3 %self_attention.1 = (bf16[256,352]{1,0:T(8,128)(2,1)}, f32[256,4]{1,0:T(8,128)}, bf16[64,1408]{1,0:T(8,128)(2,1)}, bf16[64,1408]{1,0:T(8,128)(2,1)}, bf16[64,1408]{1,0:T(8,128)(2,1)}, /*index=5*/bf16[64,1408]{1,0:T(8,128)(2,1)}) custom-call(bf16[256,352]{1,0:T(8,128)(2,1)} %get-tuple-element.210.q_ref.refs_4_, ...), custom_call_target="tpu_custom_call" | custom-call | bytes 16500000 | tf_op jit(solution)/shard_map/self_attention/pallas_call | solution.py:193
  121.1 6.4 %collective-permute-done.8.refs_1_ = bf16[64,1408]{1,0:T(8,128)(2,1)S(1)} collective-permute-done((bf16[64,1408]{1,0:T(8,128)(2,1)}, bf16[64,1408]{1,0:T(8,128)(2,1)S(1)}, u32[]{:S(2)}, u32[]{:S(2)}) %collective-permute-start.8) | collective-permute-done | bytes 180256 | tf_op jit(solution)/shard_map/ppermute | solution.py:75
  150.0 10.0 %cross_layer.1 = (bf16[256,1408]{1,0:T(8,128)(2,1)}, f32[256,352]{1,0:T(8,128)}, bf16[256,352]{1,0:T(8,128)(2,1)}, bf16[64,1408]{1,0:T(8,128)(2,1)}, bf16[64,140...) custom-call(bf16[64,1408]{1,0:T(8,128)(2,1)} %get-tuple-element.224.refs_0_, ...), custom_call_target="tpu_custom_call" | custom-call | bytes 23100000 | tf_op jit(solution)/shard_map/cross_layer/pallas_call | solution.py:193
  164.4 6.7 %collective-permute-done.15.refs_1_ = bf16[64,1408]{1,0:T(8,128)(2,1)S(1)} collective-permute-done((bf16[64,1408]{1,0:T(8,128)(2,1)}, bf16[64,1408]{1,0:T(8,128)(2,1)S(1)}, u32[]{:S(2)}, u32[]{:S(2)}) %collective-permute-start.15) | collective-permute-done | bytes 180256 | tf_op jit(solution)/shard_map/ppermute | solution.py:75
  180.6 8.5 %collective-permute-done.18.refs_1_ = bf16[64,1408]{1,0:T(8,128)(2,1)S(1)} collective-permute-done((bf16[64,1408]{1,0:T(8,128)(2,1)}, bf16[64,1408]{1,0:T(8,128)(2,1)S(1)}, u32[]{:S(2)}, u32[]{:S(2)}) %collective-permute-start.18) | collective-permute-done | bytes 180256 | tf_op jit(solution)/shard_map/ppermute | solution.py:70
  189.9 13.5 %feed_forward.1 = (bf16[256,1408]{1,0:T(8,128)(2,1)}, bf16[2,2,256,768]{3,2,1,0:T(8,128)(2,1)}, bf16[64,1408]{1,0:T(8,128)(2,1)}, bf16[64,1408]{1,0:T(8,128)(2,1...) custom-call(bf16[64,1408]{1,0:T(8,128)(2,1)} %get-tuple-element.245., ...), custom_call_target="tpu_custom_call" | custom-call | bytes 29700000 | tf_op jit(solution)/shard_map/feed_forward/pallas_call | solution.py:193
  207.0 7.1 %feed_forward_grads.1 = bf16[8,2,192,1408]{3,2,1,0:T(8,128)(2,1)} custom-call(bf16[2,2,256,768]{3,2,1,0:T(8,128)(2,1)} %get-tuple-element.254.acts_ref, bf16[256,1408]{1,0:T(8,128)(2,1)} %get-tuple-element.255.x_ref, bf16[256,1408]{1,0:T(8,128)(2,1)} %pad_maximum_fusion.2.refs_4_.cot_ref), custom_call_target="tpu_custom_call" | custom-call | bytes 23100000 | tf_op jit(solution)/shard_map/feed_forward_grads/pallas_call | solution.py:193
  238.5 11.4 %cross_layer_back.1 = (bf16[256,1408]{1,0:T(8,128)(2,1)}, bf16[256,352]{1,0:T(8,128)(2,1)}, bf16[352,352]{1,0:T(8,128)(2,1)}, bf16[352,352]{1,0:T(8,128)(2,1)}, ...) custom-call(bf16[64,1408]{1,0:T(8,128)(2,1)} %get-tuple-element.261., ...), custom_call_target="tpu_custom_call" | custom-call | bytes 33000000 | tf_op jit(solution)/shard_map/cross_layer_back/pallas_call | solution.py:193
  270.6 8.8 %text_layer_back.1 = bf16[8,2,144,1408]{3,2,1,0:T(8,128)(2,1)} custom-call(bf16[8,2,48,1408]{3,2,1,0:T(8,128)(2,1)} %cross_grads.1.first_ref, bf16[352,352]{1,0:T(8,128)(2,1)} %get-tuple-element.278.a_ref, bf16[352,352]{1,0:T(8,128)(2,1)} %get-tuple-element.279.b_ref, f32[352,176]{1,0:T(8,128)} %get-tuple-element.280.ua_ref, ...), custom_call_target="tpu_custom_call" | custom-call | bytes 29700000 | tf_op jit(solution)/shard_map/text_layer_back/pallas_call | solution.py:193
  280.4 10.5 %self_attention_back.1 = (bf16[256,1408]{1,0:T(8,128)(2,1)}, f32[256,352]{1,0:T(8,128)}, f32[256,704]{1,0:T(8,128)}, bf16[256,704]{1,0:T(8,128)(2,1)}, bf16[256,...) custom-call(bf16[64,1408]{1,0:T(8,128)(2,1)} %get-tuple-element.289.refs_0_, bf16[64,1408]{1,0:T(8,128)(2,1)} %copy-done.35, ...), custom_call_target="tpu_custom_call" | custom-call | bytes 29700000 | tf_op jit(solution)/shard_map/self_attention_back/pallas_call | solution.py:193
  295.5 9.2 %collective-permute-done.35.half_ref = bf16[256,704]{1,0:T(8,128)(2,1)S(1)} collective-permute-done((bf16[256,704]{1,0:T(8,128)(2,1)}, bf16[256,704]{1,0:T(8,128)(2,1)S(1)}, u32[]{:S(2)}, u32[]{:S(2)}) %collective-permute-start.35) | collective-permute-done | bytes 360480 | tf_op jit(solution)/shard_map/ppermute | solution.py:94
  304.7 8.6 %collective-permute-done.36.far_ref = bf16[256,704]{1,0:T(8,128)(2,1)S(1)} collective-permute-done((bf16[256,704]{1,0:T(8,128)(2,1)}, bf16[256,704]{1,0:T(8,128)(2,1)S(1)}, u32[]{:S(2)}, u32[]{:S(2)}) %collective-permute-start.36) | collective-permute-done | bytes 360480 | tf_op jit(solution)/shard_map/ppermute | solution.py:145
  317.1 12.4 %project_back.1 = (bf16[256,528]{1,0:T(8,128)(2,1)}, bf16[256,528]{1,0:T(8,128)(2,1)}, f32[1,88]{1,0:T(1,128)}, f32[1,88]{1,0:T(1,128)}, bf16[64,1408]{1,0:T(8,1...) custom-call(f32[256,704]{1,0:T(8,128)} %get-tuple-element.208.unit_ref, ...), custom_call_target="tpu_custom_call" | custom-call | bytes 26400000 | tf_op jit(solution)/shard_map/project_back/pallas_call | solution.py:193
  343.0 10.0 %collective-permute-done.42 = bf16[144,1408]{1,0:T(8,128)(2,1)S(1)} collective-permute-done((bf16[144,1408]{1,0:T(8,128)(2,1)S(1)}, bf16[144,1408]{1,0:T(8,128)(2,1)S(1)}, u32[]{:S(2)}, u32[]{:S(2)}) %collective-permute-start.42) | collective-permute-done | bytes 405536 | tf_op jit(solution)/shard_map/ppermute | solution.py:94
  410.9 6.4 %collective-permute-done.53 = bf16[2,48,1408]{2,1,0:T(8,128)(2,1)S(1)} collective-permute-done((bf16[2,48,1408]{2,1,0:T(8,128)(2,1)S(1)}, bf16[2,48,1408]{2,1,0:T(8,128)(2,1)S(1)}, u32[]{:S(2)}, u32[]{:S(2)}) %collective-permute-start.53) | collective-permute-done | bytes 270368 | tf_op jit(solution)/shard_map/ppermute | solution.py:174
  421.2 8.8 %collective-permute-done.51 = bf16[2,48,1408]{2,1,0:T(8,128)(2,1)S(1)} collective-permute-done((bf16[2,48,1408]{2,1,0:T(8,128)(2,1)S(1)}, bf16[2,48,1408]{2,1,0:T(8,128)(2,1)S(1)}, u32[]{:S(2)}, u32[]{:S(2)}) %collective-permute-start.51) | collective-permute-done | bytes 270368 | tf_op jit(solution)/shard_map/ppermute | solution.py:174
  445.8 12.2 %joined_grads.1 = (f32[512,1408]{1,0:T(8,128)}, f32[512,1408]{1,0:T(8,128)}) custom-call(bf16[512,1408]{1,0:T(8,128)(2,1)} %copy-done, bf16[8,8,48,1408]{3,2,1,0:T(8,128)(2,1)} %all-gather.12.cloned.1.call-done.pack_ref), custom_call_target="tpu_custom_call" | custom-call | bytes 29700000 | tf_op jit(solution)/shard_map/joined_grads/pallas_call | solution.py:193
  459.0 6.1 %feed_forward_out.1 = (f32[1408,768]{1,0:T(8,128)}, f32[768,1408]{1,0:T(8,128)}) custom-call(bf16[8,336,1408]{2,1,0:T(8,128)(2,1)} %bitcast.69), custom_call_target="tpu_custom_call" | custom-call | bytes 19800000 | tf_op jit(solution)/shard_map/feed_forward_out/pallas_call | solution.py:193
  473.6 6.8 %collective-permute-done.63 = bf16[256,1408]{1,0:T(8,128)(2,1)S(1)} collective-permute-done((bf16[256,1408]{1,0:T(8,128)(2,1)S(1)}, bf16[256,1408]{1,0:T(8,128)(2,1)S(1)}, u32[]{:S(2)}, u32[]{:S(2)}) %collective-permute-start.63) | collective-permute-done | bytes 720928 | tf_op jit(solution)/shard_map/ppermute | solution.py:94
  480.5 11.6 %all-gather.22.cloned.1.call-done = bf16[1152,1408]{1,0:T(8,128)(2,1)} async-done(((bf16[144,1408]{1,0:T(8,128)(2,1)}), bf16[1152,1408]{1,0:T(8,128)(2,1)}) %all-gather.22.cloned.1.call-update) | async-done | bytes 3244048 | tf_op jit(solution)/shard_map/all_gather | solution.py:164
  (428 shorter events, 268.1 us)
Async XLA Ops:
  7.2 74.8 %all-gather.14.cloned.1.call-start = ((), (), s32[]{:S(2)}) async-start(), calls=%async_computation.8 | async-start | bytes 3063808 | tf_op jit(solution)/shard_map/all_gather | solution.py:1057
  32.6 27.4 %all-to-all-start = ((bf16[8,64,1408]{2,1,0:T(8,128)(2,1)}), bf16[8,64,1408]{2,1,0:T(8,128)(2,1)S(1)}, u32[]{:S(2)}, u32[]{:S(2)}) async-start(bf16[8,64,1408]{2,1,0:T(8,128)(2,1)} %bitcast.2), calls=%async_computation | async-start | bytes 2883584 | tf_op jit(solution)/shard_map/all_to_all | solution.py:41
  37.2 103.8 %all-gather.16.cloned.1.call-start = ((), (), s32[]{:S(2)}) async-start(), calls=%async_computation.9 | async-start | bytes 2297856 | tf_op jit(solution)/shard_map/all_gather | solution.py:1091
  65.0 16.9 %collective-permute-start.2 = (bf16[112,1408]{1,0:T(8,128)(2,1)}, bf16[112,1408]{1,0:T(8,128)(2,1)S(1)}, u32[]{:S(2)}, u32[]{:S(2)}) collective-permute-start(bf16[112,1408]{1,0:T(8,128)(2,1)} %get-tuple-element.204.refs_0_), channel_id=1, source_target_pairs={{0,2},{1,3},{2,0},{3,1},{4,6},{5,7},{6,4},{7,5},{8,10},{9,11},{10,... | collective-permute-start | bytes 946184 | tf_op jit(solution)/shard_map/ppermute | solution.py:70
  69.4 22.7 %collective-permute-start.4 = (bf16[48,1408]{1,0:T(8,128)(2,1)S(1)}, bf16[48,1408]{1,0:T(8,128)(2,1)S(1)}, u32[]{:S(2)}, u32[]{:S(2)}) collective-permute-start(bf16[48,1408]{1,0:T(8,128)(2,1)S(1)} %pad_maximum_fusion.8), channel_id=1, source_target_pairs={{0,4},{1,5},{2,6},{3,7},{4,0},{5,1},{6,2},{7,3},{8,12},{9,13},{10,... | collective-permute-start | bytes 405512 | tf_op jit(solution)/shard_map/ppermute | solution.py:94
  92.8 96.4 %all-gather.18.cloned.1.call-start = ((), (), s32[]{:S(2)}) async-start(), calls=%async_computation.10 | async-start | bytes 4866048 | tf_op jit(solution)/shard_map/all_gather | solution.py:164
  93.0 14.9 %collective-permute-start.5 = (bf16[256,704]{1,0:T(8,128)(2,1)}, bf16[256,704]{1,0:T(8,128)(2,1)S(1)}, u32[]{:S(2)}, u32[]{:S(2)}) collective-permute-start(bf16[256,704]{1,0:T(8,128)(2,1)} %get-tuple-element.214.a_ref.refs_5_), channel_id=1, source_target_pairs={{0,8},{8,0},{16,24},{24,16},{32,40},{40,32},{48,56},{56,48},{64,72... | collective-permute-start | bytes 1081352 | tf_op jit(solution)/shard_map/ppermute | solution.py:99
  107.6 26.7 %collective-permute-start.21 = (bf16[192,1408]{1,0:T(8,128)(2,1)S(1)}, bf16[192,1408]{1,0:T(8,128)(2,1)S(1)}, u32[]{:S(2)}, u32[]{:S(2)}) collective-permute-start(bf16[192,1408]{1,0:T(8,128)(2,1)S(1)} %copy-done.27), channel_id=1, source_target_pairs={{0,4},{1,5},{2,6},{3,7},{4,0},{5,1},{6,2},{7,3},{8,12},{9,13},{10,... | collective-permute-start | bytes 1622024 | tf_op jit(solution)/shard_map/ppermute | solution.py:94
  135.1 87.9 %all-gather.12.cloned.1.call-start = ((), (), s32[]{:S(2)}) async-start(), calls=%async_computation.4 | async-start | bytes 9732096 | tf_op jit(solution)/shard_map/all_gather | solution.py:164
  136.3 23.7 %collective-permute-start.14 = (bf16[192,1408]{1,0:T(8,128)(2,1)S(1)}, bf16[192,1408]{1,0:T(8,128)(2,1)S(1)}, u32[]{:S(2)}, u32[]{:S(2)}) collective-permute-start(bf16[192,1408]{1,0:T(8,128)(2,1)S(1)} %pad_maximum_fusion.5), channel_id=1, source_target_pairs={{0,4},{1,5},{2,6},{3,7},{4,0},{5,1},{6,2},{7,3},{8,12},{9,13},{10,... | collective-permute-start | bytes 1622024 | tf_op jit(solution)/shard_map/ppermute | solution.py:94
  175.0 104.5 %reduce-scatter.4.cloned.1.call-start = ((), (), s32[]{:S(2)}) async-start(), calls=%async_computation.5 | async-start | bytes 9732096 | tf_op jit(solution)/shard_map/reduce_scatter | solution.py:158
  223.1 116.7 %reduce-scatter.6.cloned.1.call-start = ((), (), s32[]{:S(2)}) async-start(), calls=%async_computation.6 | async-start | bytes 7299072 | tf_op jit(solution)/shard_map/reduce_scatter | solution.py:158
  280.2 107.8 %reduce-scatter.8.cloned.1.call-start = ((), (), s32[]{:S(2)}) async-start(), calls=%async_computation.7 | async-start | bytes 4866048 | tf_op jit(solution)/shard_map/reduce_scatter | solution.py:158
  295.1 18.1 %collective-permute-start.36 = (bf16[256,704]{1,0:T(8,128)(2,1)}, bf16[256,704]{1,0:T(8,128)(2,1)S(1)}, u32[]{:S(2)}, u32[]{:S(2)}) collective-permute-start(bf16[256,704]{1,0:T(8,128)(2,1)} %get-tuple-element.298), channel_id=1, source_target_pairs={{0,12},{1,13},{2,14},{3,15},{4,8},{5,9},{6,10},{7,11},{8,4},{9,5},... | collective-permute-start | bytes 1081352 | tf_op jit(solution)/shard_map/ppermute | solution.py:145
  313.3 16.2 %collective-permute-start.37 = (bf16[192,1408]{1,0:T(8,128)(2,1)S(1)}, bf16[192,1408]{1,0:T(8,128)(2,1)S(1)}, u32[]{:S(2)}, u32[]{:S(2)}) collective-permute-start(bf16[192,1408]{1,0:T(8,128)(2,1)S(1)} %slice.115), channel_id=1, source_target_pairs={{0,4},{1,5},{2,6},{3,7},{4,0},{5,1},{6,2},{7,3},{8,12},{9,13},{10,... | collective-permute-start | bytes 1622024 | tf_op jit(solution)/shard_map/ppermute | solution.py:94
  336.5 16.6 %collective-permute-start.38 = (bf16[64,1408]{1,0:T(8,128)(2,1)}, bf16[64,1408]{1,0:T(8,128)(2,1)S(1)}, u32[]{:S(2)}, u32[]{:S(2)}) collective-permute-start(bf16[64,1408]{1,0:T(8,128)(2,1)} %get-tuple-element.309), channel_id=1, source_target_pairs={{0,3},{1,0},{2,1},{3,2},{4,7},{5,4},{6,5},{7,6},{8,11},{9,8},{10,9... | collective-permute-start | bytes 540680 | tf_op jit(solution)/shard_map/ppermute | solution.py:75
  338.6 14.6 %collective-permute-start.39 = (bf16[64,1408]{1,0:T(8,128)(2,1)}, bf16[64,1408]{1,0:T(8,128)(2,1)S(1)}, u32[]{:S(2)}, u32[]{:S(2)}) collective-permute-start(bf16[64,1408]{1,0:T(8,128)(2,1)} %get-tuple-element.310), channel_id=1, source_target_pairs={{0,2},{1,3},{2,0},{3,1},{4,6},{5,7},{6,4},{7,5},{8,10},{9,11},{10,... | collective-permute-start | bytes 540680 | tf_op jit(solution)/shard_map/ppermute | solution.py:75
  338.9 14.3 %collective-permute-start.40 = (bf16[64,1408]{1,0:T(8,128)(2,1)S(1)}, bf16[64,1408]{1,0:T(8,128)(2,1)S(1)}, u32[]{:S(2)}, u32[]{:S(2)}) collective-permute-start(bf16[64,1408]{1,0:T(8,128)(2,1)S(1)} %copy-done.78), channel_id=1, source_target_pairs={{0,1},{1,2},{2,3},{3,0},{4,5},{5,6},{6,7},{7,4},{8,9},{9,10},{10,1... | collective-permute-start | bytes 540680 | tf_op jit(solution)/shard_map/ppermute | solution.py:75
  353.9 104.8 %all-gather.20.cloned.1.call-start = ((), (), s32[]{:S(2)}) async-start(), calls=%async_computation.11 | async-start | bytes 8515584 | tf_op jit(solution)/shard_map/all_gather | solution.py:164
  388.0 104.1 %all-gather.22.cloned.1.call-start = ((), (), s32[]{:S(2)}) async-start(), calls=%async_computation.12 | async-start | bytes 3649536 | tf_op jit(solution)/shard_map/all_gather | solution.py:164
  393.4 36.7 %collective-permute-start.57 = (bf16[256,1408]{1,0:T(8,128)(2,1)}, bf16[256,1408]{1,0:T(8,128)(2,1)S(1)}, u32[]{:S(2)}, u32[]{:S(2)}) collective-permute-start(bf16[256,1408]{1,0:T(8,128)(2,1)} %get-tuple-element.353), channel_id=1, source_target_pairs={{0,4},{1,5},{2,6},{3,7},{4,0},{5,1},{6,2},{7,3},{8,12},{9,13},{10,... | collective-permute-start | bytes 2162696 | tf_op jit(solution)/shard_map/ppermute | solution.py:94
  406.1 15.1 %collective-permute-start.52 = (bf16[2,48,1408]{2,1,0:T(8,128)(2,1)S(1)}, bf16[2,48,1408]{2,1,0:T(8,128)(2,1)S(1)}, u32[]{:S(2)}, u32[]{:S(2)}) collective-permute-start(bf16[2,48,1408]{2,1,0:T(8,128)(2,1)S(1)} %get-tuple-element.395), channel_id=1, source_target_pairs={{0,32},{8,40},{16,48},{24,56},{32,0},{40,8},{48,16},{56,24},{64,96... | collective-permute-start | bytes 811016 | tf_op jit(solution)/shard_map/ppermute | solution.py:174
  410.8 19.2 %collective-permute-start.51 = (bf16[2,48,1408]{2,1,0:T(8,128)(2,1)S(1)}, bf16[2,48,1408]{2,1,0:T(8,128)(2,1)S(1)}, u32[]{:S(2)}, u32[]{:S(2)}) collective-permute-start(bf16[2,48,1408]{2,1,0:T(8,128)(2,1)S(1)} %get-tuple-element.393), channel_id=1, source_target_pairs={{0,16},{8,24},{16,32},{24,40},{32,48},{40,56},{48,0},{56,8},{64,80... | collective-permute-start | bytes 811016 | tf_op jit(solution)/shard_map/ppermute | solution.py:174
  465.0 15.3 %collective-permute-start.63 = (bf16[256,1408]{1,0:T(8,128)(2,1)S(1)}, bf16[256,1408]{1,0:T(8,128)(2,1)S(1)}, u32[]{:S(2)}, u32[]{:S(2)}) collective-permute-start(bf16[256,1408]{1,0:T(8,128)(2,1)S(1)} %pad_maximum_fusion.3), channel_id=1, source_target_pairs={{0,4},{1,5},{2,6},{3,7},{4,0},{5,1},{6,2},{7,3},{8,12},{9,13},{10,... | collective-permute-start | bytes 2162696 | tf_op jit(solution)/shard_map/ppermute | solution.py:94
  (132 other events, 897.9 us)
Sparse Core Ops, SparseCore 0:
  20.5 49.4 all-gather.13
  92.9 35.3 all-gather.15
  135.3 30.6 all-gather.17
  175.1 47.8 all-gather.11
  225.3 52.8 reduce-scatter.3
  281.1 43.1 reduce-scatter.5
  353.4 34.5 reduce-scatter.7
  390.4 59.6 all-gather.19
  458.9 33.1 all-gather.21
